TPU v7x, 32 devices: a whole 2x2x4 slice. The times are simulated.
32 devices in a mesh: narrow: 4 (over y, x), wide: 8 (over z, core).
Axes of the slice: x: 2, y: 2, z: 4, core: 2. Of those that a mesh axis runs over, the one named last changes fastest.
Arguments:
- tokens: bfloat16 [4096, 2, 1024], P(('wide', 'narrow')), may hold values from -6 to 6
- gain_attn: float32 [1024], replicated, may hold values from 0.5 to 1.5
- w_query: bfloat16 [1024, 1024], P(None, 'narrow'), may hold values from -0.109375 to 0.109375
- w_key: bfloat16 [1024, 512], P(None, 'narrow'), may hold values from -0.109375 to 0.109375
- w_value: bfloat16 [1024, 512], P(None, 'narrow'), may hold values from -0.1875 to 0.1875
- w_out: bfloat16 [1024, 1024], P('narrow'), may hold values from -0.375 to 0.375
- gain_moe: float32 [1024], replicated, may hold values from 0.5 to 1.5
- w_router: bfloat16 [1024, 16], replicated, may hold values from -0.08984375 to 0.08984375
- w_gate: bfloat16 [16, 1024, 512], P('wide'), may hold values from -0.1875 to 0.1875
- w_up: bfloat16 [16, 1024, 512], P('wide'), may hold values from -0.1875 to 0.1875
- w_down: bfloat16 [16, 512, 1024], P('wide'), may hold values from -0.75 to 0.75
- routes: int32 [4096, 2, 8], P(('wide', 'narrow')), may hold values from 0 to 15, all different within a row; in each aligned block of 256 rows (0 to 255, 256 to 511, ..., all dimensions but the last counted through in order) at most 192 rows name the same one
- rope_scale: float32 [1], replicated, may hold values from 1 to 4
- cotangent: bfloat16 [4096, 2, 1024], P(('wide', 'narrow')), may hold values from -6 to 6
Outputs:
- mixed: bfloat16 [4096, 2, 1024], P(('wide', 'narrow'))
- grad_tokens: float32 [4096, 2, 1024], P(('wide', 'narrow'))
- grad_gain_attn: float32 [1024], replicated
- grad_w_query: float32 [1024, 1024], P('wide', 'narrow')
- grad_w_key: float32 [1024, 512], P('wide', 'narrow')
- grad_w_value: float32 [1024, 512], P('wide', 'narrow')
- grad_w_out: float32 [1024, 1024], P('narrow', 'wide')
- grad_gain_moe: float32 [1024], replicated
- grad_router: float32 [1024, 16], replicated
- grad_gate: float32 [16, 1024, 512], P('wide', 'narrow')
- grad_up: float32 [16, 1024, 512], P('wide', 'narrow')
- grad_down: float32 [16, 512, 1024], P('wide', 'narrow')
Inputs may be any that keep to these rules, and one draw needn't show every extreme that they name: `routes`: each token names 8 different experts. Among the tokens of one device no expert is named more than 192 times, a bound that some block reaches.
All inputs are finite; a program needn't handle non-finite values.
Results may differ from a plain program's by a relative error of at most 0.028.
Values may be sent and summed in bfloat16 or wider, within the bound.
A program may use at most 192 MiB of HBM per device.

v0:
```python
import jax
import jax.numpy as jnp
from jax import lax
from jax.sharding import PartitionSpec as P

HD = 64


EPSILON = 1e-06
ROPE_BASE = 10000.0
MASKED = -1e30
PRECISE = lax.Precision.HIGHEST


def rotate(tensor, positions, factor, direction):
    half_size = tensor.shape[-1] // 2
    frequency = ROPE_BASE ** (-jnp.arange(half_size, dtype=jnp.float32) * 2.0 / tensor.shape[-1])
    angles = (positions.astype(jnp.float32) / factor)[:, None] * frequency[None, :]
    cosine = jnp.cos(angles)[:, None, None, :]
    sine_part = direction * jnp.sin(angles)[:, None, None, :]
    leading = tensor[..., :half_size]
    trailing = tensor[..., half_size:]
    return jnp.concatenate(
        [leading * cosine - trailing * sine_part, trailing * cosine + leading * sine_part], axis=-1
    )


def normalize(inputs, gain_vector):
    inverse = lax.rsqrt(jnp.mean(inputs * inputs, axis=-1, keepdims=True) + EPSILON)
    return (inputs * inverse * gain_vector, inverse)


def normalize_back(inputs, inverse, gain_vector, upstream):
    scaled = inputs * inverse
    through = upstream * gain_vector
    input_grad = inverse * (through - scaled * jnp.mean(through * scaled, axis=-1, keepdims=True))
    gain_grad = jnp.sum(upstream * scaled, axis=(0, 1))
    return (input_grad, gain_grad)


def block_scores(query_group, key_block, query_pos, key_pos, score_scale):
    products = (
        jnp.einsum("qskgd,tskd->skgqt", query_group, key_block, preferred_element_type=jnp.float32)
        * score_scale
    )
    return jnp.where(key_pos[None, :] <= query_pos[:, None], products, MASKED)


def block_backward(
    query_group,
    attended_group,
    log_total,
    row_inner,
    key_block,
    value_block,
    query_pos,
    key_pos,
    score_scale,
):
    scores = block_scores(query_group, key_block, query_pos, key_pos, score_scale)
    attention = jnp.exp(scores - log_total[..., None])
    prob_grads = jnp.einsum(
        "qskgd,tskd->skgqt", attended_group, value_block, preferred_element_type=jnp.float32
    )
    score_grads = (attention * (prob_grads - row_inner[..., None])).astype(jnp.bfloat16)
    query_grad = score_scale * jnp.einsum(
        "skgqt,tskd->qskgd", score_grads, key_block, preferred_element_type=jnp.float32
    )
    key_grad = score_scale * jnp.einsum(
        "skgqt,qskgd->tskd", score_grads, query_group, preferred_element_type=jnp.float32
    )
    value_grad = jnp.einsum(
        "skgqt,qskgd->tskd",
        attention.astype(jnp.bfloat16),
        attended_group,
        preferred_element_type=jnp.float32,
    )
    return (query_grad, key_grad, value_grad)


def on_device(
    tokens,
    gain_attn,
    w_query,
    w_key,
    w_value,
    w_out,
    gain_moe,
    w_router,
    w_gate,
    w_up,
    w_down,
    routes,
    rope_scale,
    cotangent,
):
    narrow_count = lax.axis_size("narrow")
    wide_count = lax.axis_size("wide")
    wide_place = lax.axis_index("wide")
    local_rows, sequences, model_width = tokens.shape
    block_rows = local_rows * narrow_count
    head_size = HD
    query_cols = w_query.shape[1]
    kv_cols = w_key.shape[1]
    kv_heads = kv_cols // head_size
    group_size = query_cols // kv_cols
    score_scale = head_size ** (-0.5)
    factor = rope_scale[0]
    token_float = tokens.astype(jnp.float32)
    attn_normed, attn_inverse = normalize(token_float, gain_attn)
    attn_low = attn_normed.astype(jnp.bfloat16)
    attn_block = lax.all_gather(attn_low, "narrow", axis=0, tiled=True)
    joint_weight = jnp.concatenate([w_query, w_key, w_value], axis=1)
    joint_proj = jnp.einsum(
        "tsd,dc->tsc", attn_block, joint_weight, preferred_element_type=jnp.float32
    )
    query_pos = wide_place * block_rows + lax.iota(jnp.int32, block_rows)
    query_rot = rotate(
        joint_proj[..., :query_cols].reshape(
            block_rows, sequences, kv_heads * group_size, head_size
        ),
        query_pos,
        factor,
        1.0,
    )
    query_group = query_rot.astype(jnp.bfloat16).reshape(
        block_rows, sequences, kv_heads, group_size, head_size
    )
    key_rot = rotate(
        joint_proj[..., query_cols : query_cols + kv_cols].reshape(
            block_rows, sequences, kv_heads, head_size
        ),
        query_pos,
        factor,
        1.0,
    )
    key_local = key_rot.astype(jnp.bfloat16).reshape(block_rows, sequences, kv_cols)
    value_local = joint_proj[..., query_cols + kv_cols :].astype(jnp.bfloat16)
    pair_local = jnp.concatenate([key_local, value_local], axis=-1)
    pair_all = lax.all_gather(pair_local, "wide", axis=0, tiled=True)

    def split_pair(block_index):
        pair_block = lax.dynamic_slice_in_dim(pair_all, block_index * block_rows, block_rows, 0)
        key_block = pair_block[..., :kv_cols].reshape(block_rows, sequences, kv_heads, head_size)
        value_block = pair_block[..., kv_cols:].reshape(block_rows, sequences, kv_heads, head_size)
        key_pos = block_index * block_rows + lax.iota(jnp.int32, block_rows)
        return (key_block, value_block, key_pos)

    def forward_block(block_index, carried):
        running, denominator, accumulated = carried
        key_block, value_block, key_pos = split_pair(block_index)
        scores = block_scores(query_group, key_block, query_pos, key_pos, score_scale)
        new_running = jnp.maximum(running, jnp.max(scores, axis=-1))
        rescale = jnp.exp(running - new_running)
        weights = jnp.exp(scores - new_running[..., None])
        denominator = denominator * rescale + jnp.sum(weights, axis=-1)
        accumulated = accumulated * rescale[..., None] + jnp.einsum(
            "skgqt,tskd->skgqd",
            weights.astype(jnp.bfloat16),
            value_block,
            preferred_element_type=jnp.float32,
        )
        return (new_running, denominator, accumulated)

    stat_shape = (sequences, kv_heads, group_size, block_rows)
    starting = (
        jnp.full(stat_shape, MASKED, jnp.float32),
        jnp.zeros(stat_shape, jnp.float32),
        jnp.zeros(stat_shape + (head_size,), jnp.float32),
    )
    running, denominator, accumulated = lax.fori_loop(0, wide_place + 1, forward_block, starting)
    attn_result = accumulated / denominator[..., None]
    log_total = running + jnp.log(denominator)
    out_tokens = attn_result.transpose(3, 0, 1, 2, 4).reshape(block_rows, sequences, query_cols)
    out_low = out_tokens.astype(jnp.bfloat16)
    rows_part = out_low
    attn_branch = lax.psum_scatter(
        jnp.einsum("tsc,cd->tsd", rows_part, w_out, preferred_element_type=jnp.float32).astype(
            jnp.bfloat16
        ),
        "narrow",
        scatter_dimension=0,
        tiled=True,
    ).astype(jnp.float32)
    residual = token_float + attn_branch
    moe_normed, moe_inverse = normalize(residual, gain_moe)
    moe_low = moe_normed.astype(jnp.bfloat16)
    token_count = local_rows * sequences
    moe_flat = moe_low.reshape(token_count, model_width)
    expert_count = w_router.shape[1]
    local_experts = w_gate.shape[0]
    choose = routes.shape[-1]
    capacity = 3 * token_count * choose // (2 * expert_count)
    expert_ids = routes.reshape(token_count, choose)
    onehot = (expert_ids[:, :, None] == lax.iota(jnp.int32, expert_count)[None, None, :]).astype(
        jnp.float32
    )
    logits = jnp.dot(moe_flat, w_router, preferred_element_type=jnp.float32)
    chosen = jnp.sum(onehot * logits[:, None, :], axis=-1)
    gate_weights = jax.nn.softmax(chosen, axis=-1)
    flat_hot = onehot.reshape(token_count * choose, expert_count)
    before = jnp.cumsum(flat_hot, axis=0) - flat_hot
    slot_index = jnp.sum(before * flat_hot, axis=-1).astype(jnp.int32)
    destination = expert_ids.reshape(-1) * capacity + slot_index

    def pack_rows(rows_in):
        blank_rows = jnp.zeros((expert_count * capacity, model_width), jnp.bfloat16)
        filled = blank_rows.at[destination].set(rows_in)
        return filled.reshape(wide_count, local_experts, capacity, model_width)

    def unpack_rows(arrived_back):
        return arrived_back.reshape(expert_count * capacity, model_width)[destination].reshape(
            token_count, choose, model_width
        )

    copies = jnp.broadcast_to(moe_flat[:, None, :], (token_count, choose, model_width)).reshape(
        token_count * choose, model_width
    )
    arrived = lax.all_to_all(pack_rows(copies), "wide", split_axis=0, concat_axis=0, tiled=True)
    gate_part = jnp.einsum("wecd,edf->wecf", arrived, w_gate, preferred_element_type=jnp.float32)
    up_part = jnp.einsum("wecd,edf->wecf", arrived, w_up, preferred_element_type=jnp.float32)
    sigmoid_gate = jax.nn.sigmoid(gate_part)
    activated = gate_part * sigmoid_gate
    hidden_low = (activated * up_part).astype(jnp.bfloat16)
    expert_out = jnp.einsum(
        "wecf,efd->wecd", hidden_low, w_down, preferred_element_type=jnp.float32
    ).astype(jnp.bfloat16)
    returned = lax.all_to_all(expert_out, "wide", split_axis=0, concat_axis=0, tiled=True)
    expert_rows = unpack_rows(returned).astype(jnp.float32)
    moe_part = jnp.sum(gate_weights[:, :, None] * expert_rows, axis=1)
    layer_out = (residual + moe_part.reshape(local_rows, sequences, model_width)).astype(
        jnp.bfloat16
    )
    upstream = cotangent.astype(jnp.float32)
    upstream_flat = upstream.reshape(token_count, model_width)
    pick_grads = jnp.sum(upstream_flat[:, None, :] * expert_rows, axis=-1)
    chosen_grads = gate_weights * (
        pick_grads - jnp.sum(gate_weights * pick_grads, axis=-1, keepdims=True)
    )
    logit_grads = jnp.sum(chosen_grads[:, :, None] * onehot, axis=1)
    router_grads = jnp.dot(moe_flat.astype(jnp.float32).T, logit_grads, precision=PRECISE)
    moe_grads = jnp.dot(logit_grads, w_router.astype(jnp.float32).T, precision=PRECISE)
    scaled_grads = (
        (gate_weights[:, :, None] * upstream_flat[:, None, :])
        .astype(jnp.bfloat16)
        .reshape(token_count * choose, model_width)
    )
    grad_arrived = lax.all_to_all(
        pack_rows(scaled_grads), "wide", split_axis=0, concat_axis=0, tiled=True
    )
    hidden_grads = jnp.einsum(
        "wecd,efd->wecf", grad_arrived, w_down, preferred_element_type=jnp.float32
    )
    down_update = jnp.einsum(
        "wecf,wecd->efd", hidden_low, grad_arrived, preferred_element_type=jnp.float32
    )
    slope = sigmoid_gate * (1.0 + gate_part * (1.0 - sigmoid_gate))
    gate_signal = (hidden_grads * up_part * slope).astype(jnp.bfloat16)
    up_signal = (hidden_grads * activated).astype(jnp.bfloat16)
    gate_update = jnp.einsum(
        "wecd,wecf->edf", arrived, gate_signal, preferred_element_type=jnp.float32
    )
    up_update = jnp.einsum("wecd,wecf->edf", arrived, up_signal, preferred_element_type=jnp.float32)
    input_grads = jnp.einsum(
        "wecf,edf->wecd", gate_signal, w_gate, preferred_element_type=jnp.float32
    )
    input_grads = (
        input_grads
        + jnp.einsum("wecf,edf->wecd", up_signal, w_up, preferred_element_type=jnp.float32)
    ).astype(jnp.bfloat16)
    grads_back = lax.all_to_all(input_grads, "wide", split_axis=0, concat_axis=0, tiled=True)
    moe_grads = moe_grads + jnp.sum(unpack_rows(grads_back).astype(jnp.float32), axis=1)
    expert_grads = (
        lax.psum_scatter(
            gate_update.astype(jnp.bfloat16), "narrow", scatter_dimension=1, tiled=True
        ).astype(jnp.float32),
        lax.psum_scatter(
            up_update.astype(jnp.bfloat16), "narrow", scatter_dimension=1, tiled=True
        ).astype(jnp.float32),
        lax.psum_scatter(
            down_update.astype(jnp.bfloat16), "narrow", scatter_dimension=1, tiled=True
        ).astype(jnp.float32),
    )
    norm_grads, moe_gain = normalize_back(
        residual, moe_inverse, gain_moe, moe_grads.reshape(local_rows, sequences, model_width)
    )
    residual_grads = upstream + norm_grads
    branch_low = residual_grads.astype(jnp.bfloat16)
    branch_all = lax.all_gather(branch_low, "narrow", axis=0, tiled=True)
    out_update = jnp.einsum("tsc,tsd->cd", out_low, branch_all, preferred_element_type=jnp.float32)
    attended_grads = jnp.einsum(
        "tsd,cd->tsc", branch_all, w_out, preferred_element_type=jnp.float32
    ).astype(jnp.bfloat16)
    attended_group = attended_grads.reshape(block_rows, sequences, kv_heads, group_size, head_size)
    row_inner = jnp.sum(
        attended_group.astype(jnp.float32).transpose(1, 2, 3, 0, 4) * attn_result, axis=-1
    )
    query_zero = jnp.zeros((block_rows, sequences, kv_heads, group_size, head_size), jnp.float32)

    def both_block(block_index, carried):
        query_grads, pair_grads = carried
        key_block, value_block, key_pos = split_pair(block_index)
        query_part, key_grad, value_grad = block_backward(
            query_group,
            attended_group,
            log_total,
            row_inner,
            key_block,
            value_block,
            query_pos,
            key_pos,
            score_scale,
        )
        pair_part = jnp.concatenate(
            [
                key_grad.reshape(block_rows, sequences, kv_cols),
                value_grad.reshape(block_rows, sequences, kv_cols),
            ],
            axis=-1,
        )
        pair_grads = lax.dynamic_update_slice_in_dim(
            pair_grads, pair_part, block_index * block_rows, 0
        )
        return (query_grads + query_part, pair_grads)

    pair_zero = jnp.zeros((block_rows * wide_count, sequences, 2 * kv_cols), jnp.float32)
    query_grads, pair_grads = lax.fori_loop(0, wide_place + 1, both_block, (query_zero, pair_zero))
    pair_own = lax.psum_scatter(
        pair_grads.astype(jnp.bfloat16), "wide", scatter_dimension=0, tiled=True
    ).astype(jnp.float32)
    query_low = (
        rotate(
            query_grads.reshape(block_rows, sequences, kv_heads * group_size, head_size),
            query_pos,
            factor,
            -1.0,
        )
        .astype(jnp.bfloat16)
        .reshape(block_rows, sequences, query_cols)
    )
    key_low = (
        rotate(
            pair_own[..., :kv_cols].reshape(block_rows, sequences, kv_heads, head_size),
            query_pos,
            factor,
            -1.0,
        )
        .astype(jnp.bfloat16)
        .reshape(block_rows, sequences, kv_cols)
    )
    value_low = pair_own[..., kv_cols:].astype(jnp.bfloat16)
    joint_grads = jnp.concatenate([query_low, key_low, value_low], axis=-1)
    joint_update = jnp.einsum(
        "tsd,tsc->dc", attn_block, joint_grads, preferred_element_type=jnp.float32
    )
    rows_part = joint_grads
    attn_grads = lax.psum_scatter(
        jnp.einsum(
            "tsc,dc->tsd", rows_part, joint_weight, preferred_element_type=jnp.float32
        ).astype(jnp.bfloat16),
        "narrow",
        scatter_dimension=0,
        tiled=True,
    ).astype(jnp.float32)
    token_grads, attn_gain = normalize_back(token_float, attn_inverse, gain_attn, attn_grads)
    token_grads = residual_grads + token_grads
    joint_summed, out_summed = (
        lax.psum_scatter(
            joint_update.astype(jnp.bfloat16), "wide", scatter_dimension=0, tiled=True
        ).astype(jnp.float32),
        lax.psum_scatter(
            out_update.T.astype(jnp.bfloat16), "wide", scatter_dimension=0, tiled=True
        ).astype(jnp.float32),
    )
    summed_small = lax.psum((attn_gain, moe_gain, router_grads), ("narrow", "wide"))
    return (
        layer_out,
        token_grads,
        summed_small[0],
        joint_summed[:, :query_cols],
        joint_summed[:, query_cols : query_cols + kv_cols],
        joint_summed[:, query_cols + kv_cols :],
        out_summed.T,
        summed_small[1],
        summed_small[2],
        expert_grads[0],
        expert_grads[1],
        expert_grads[2],
    )


def solution(mesh):
    return jax.shard_map(
        on_device,
        mesh=mesh,
        in_specs=(
            P(("wide", "narrow"), None, None),
            P(),
            P(None, "narrow"),
            P(None, "narrow"),
            P(None, "narrow"),
            P("narrow", None),
            P(),
            P(),
            P("wide", None, None),
            P("wide", None, None),
            P("wide", None, None),
            P(("wide", "narrow"), None, None),
            P(),
            P(("wide", "narrow"), None, None),
        ),
        out_specs=(
            P(("wide", "narrow"), None, None),
            P(("wide", "narrow"), None, None),
            P(),
            P("wide", "narrow"),
            P("wide", "narrow"),
            P("wide", "narrow"),
            P("narrow", "wide"),
            P(),
            P(),
            P("wide", "narrow", None),
            P("wide", "narrow", None),
            P("wide", "narrow", None),
        ),
        check_vma=False,
    )
```

profile of v0, /device:TPU:0, one launch (start us, length us, event | category | flops | bytes accessed | tf_op | source)
XLA Modules:
  0.0 1390.7 jit_solution(18236117494126367271)
XLA Ops:
  8.6 2.0 fusion.83
  16.1 32.8 %all-gather.4.cloned.1.call-done = bf16[512,2,1024]{2,0,1:T(8,128)(2,1)} async-done(((bf16[128,2,1024]{2,0,1:T(8,128)(2,1)}), bf16[512,2,1024]{2,0,1:T(8,128)(2,1)}) %all-gather.4.cloned.1.call-update) | async-done | bytes 2097168 | tf_op jit(solution)/shard_map/all_gather | solution.py:112
  48.9 2.9 fusion.90
  54.8 46.7 %all-gather.6.cloned.1.call-done = bf16[4096,2,256]{0,2,1:T(8,128)(2,1)} async-done(((bf16[512,2,256]{0,2,1:T(8,128)(2,1)}), bf16[4096,2,256]{0,2,1:T(8,128)(2,1)}) %all-gather.6.cloned.1.call-update) | async-done | bytes 4194320 | tf_op jit(solution)/shard_map/all_gather | solution.py:140
  102.6 7.9 while.28
  105.4 1.8 fusion.165
  107.2 2.3 fusion.166
  112.7 3.1 convolution_convert_fusion.1
  117.5 8.1 reduce-window.6
  126.2 79.2 %reduce-scatter.9.cloned.1.call-done = bf16[128,2,1024]{2,0,1:T(8,128)(2,1)} async-done(((bf16[512,2,1024]{2,0,1:T(8,128)(2,1)}), bf16[128,2,1024]{2,0,1:T(8,128)(2,1)}) %reduce-scatter.9.cloned.1.call-update) | async-done | bytes 524304 | tf_op jit(solution)/shard_map/reduce_scatter | solution.py:177
  209.2 2.0 reshape.391
  211.2 14.2 %scatter_custom_fusion = bf16[3072,1024]{1,0:T(8,128)(2,1)} fusion(s32[2048]{0:T(1024)S(1)} %bitcast.321, bf16[]{:T(256)} %constant.29.clone.1, bf16[256,1024]{1,0:T(8,128)(2,1)} %reshape.391), kind=kCustom, calls=%fused_computation.83 | custom fusion | bytes 6815746 | tf_op jit(solution)/shard_map/scatter | solution.py:208
  225.5 4.8 all-to-all-start
  231.6 1.8 copy.185
  233.3 2.9 mul.455
  237.9 14.6 %scatter_custom_fusion.1 = bf16[3072,1024]{1,0:T(8,128)(2,1)} fusion(s32[2048]{0:T(1024)S(1)} %bitcast.322, f32[2048]{0:T(1024)S(1)} %div.77, f32[256,1024]{1,0:T(8,128)} %mul.455, bf16[]{:T(256)} %constant.29.clone.1), kind=kCustom, calls=%fused_computation.79 | custom fusion | flops 4194304 | bytes 7348226 | tf_op jit(solution)/shard_map/scatter | solution.py:208
  252.5 116.8 %all-to-all-done = bf16[8,2,192,1024]{3,2,1,0:T(8,128)(2,1)} async-done(((bf16[8,2,192,1024]{3,2,1,0:T(8,128)(2,1)}), bf16[8,2,192,1024]{3,2,1,0:T(8,128)(2,1)}, u32[]{:S(2)}, u32[]{:S(2)}) %all-to-all-start) | async-done | bytes 6291488 | tf_op jit(solution)/shard_map/all_to_all | solution.py:219
  369.2 5.0 all-to-all-start.2
  374.2 9.6 fusion.45
  383.9 8.2 fusion.47
  392.1 121.1 %all-to-all-done.2 = bf16[8,2,192,1024]{3,2,1,0:T(8,128)(2,1)} async-done(((bf16[8,2,192,1024]{3,2,1,0:T(8,128)(2,1)}), bf16[8,2,192,1024]{3,2,1,0:T(8,128)(2,1)}, u32[]{:S(2)}, u32[]{:S(2)}) %all-to-all-start.2) | async-done | bytes 6291488 | tf_op jit(solution)/shard_map/all_to_all | solution.py:248
  513.2 12.7 fusion.34
  525.9 3.6 convert_bitcast_fusion
  529.5 3.4 copy.182
  533.0 4.8 all-to-all-start.1
  537.8 10.7 fusion.65
  548.5 7.4 fusion.31
  555.9 3.4 copy.190
  559.4 117.3 %all-to-all-done.1 = bf16[8,2,192,1024]{3,2,1,0:T(8,128)(2,1)} async-done(((bf16[8,2,192,1024]{3,2,1,0:T(8,128)(2,1)}), bf16[8,2,192,1024]{3,2,1,0:T(8,128)(2,1)}, u32[]{:S(2)}, u32[]{:S(2)}) %all-to-all-start.1) | async-done | bytes 6291488 | tf_op jit(solution)/shard_map/all_to_all | solution.py:228
  676.7 4.8 all-to-all-start.3
  681.9 14.6 %gather_fusion = bf16[2048,1024]{1,0:T(8,128)(2,1)} fusion(bf16[3072,1024]{1,0:T(8,128)(2,1)} %bitcast.25, s32[2048]{0:T(1024)S(1)} %broadcast_clamp_fusion), kind=kCustom, calls=%fused_computation | custom fusion | bytes 8396800 | tf_op jit(solution)/shard_map/gather | solution.py:212
  696.6 6.1 fusion.29
  702.8 117.6 %all-to-all-done.3 = bf16[8,2,192,1024]{3,2,1,0:T(8,128)(2,1)} async-done(((bf16[8,2,192,1024]{3,2,1,0:T(8,128)(2,1)}), bf16[8,2,192,1024]{3,2,1,0:T(8,128)(2,1)}, u32[]{:S(2)}, u32[]{:S(2)}) %all-to-all-start.3) | async-done | bytes 6291488 | tf_op jit(solution)/shard_map/all_to_all | solution.py:271
  820.4 14.6 %gather_fusion.1 = bf16[2048,1024]{1,0:T(8,128)(2,1)} fusion(bf16[3072,1024]{1,0:T(8,128)(2,1)} %bitcast.35, s32[2048]{0:T(1024)S(1)} %broadcast_clamp_fusion), kind=kCustom, calls=%fused_computation.1 | custom fusion | bytes 8396800 | tf_op jit(solution)/shard_map/gather | solution.py:212
  835.0 5.5 convert_reduce_fusion
  840.5 1.6 convolution_add_fusion
  842.1 1.8 reshape.399
  846.2 33.1 %all-gather.8.cloned.1.call-done = bf16[512,2,1024]{2,0,1:T(8,128)(2,1)} async-done(((bf16[128,2,1024]{2,0,1:T(8,128)(2,1)}), bf16[512,2,1024]{2,0,1:T(8,128)(2,1)}) %all-gather.8.cloned.1.call-update) | async-done | bytes 2097168 | tf_op jit(solution)/shard_map/all_gather | solution.py:289
  879.3 3.2 convolution_convert_fusion.2
  882.5 1.6 fusion.87
  884.2 2.2 broadcast_in_dim.35.clone
  886.5 13.3 while.29
  889.1 3.3 fusion.180
  892.4 4.1 fusion.178
  899.9 8.5 bitcast_convert_fusion
  908.7 8.5 bitcast_convert_fusion.1
  917.3 8.6 bitcast_convert_fusion.2
  926.1 3.1 fusion.79
  929.6 113.0 %reduce-scatter.11.cloned.1.call-done = bf16[512,2,256]{2,0,1:T(8,128)(2,1)} async-done(((bf16[4096,2,256]{2,0,1:T(8,128)(2,1)}), bf16[512,2,256]{2,0,1:T(8,128)(2,1)}) %reduce-scatter.11.cloned.1.call-update) | async-done | bytes 524304 | tf_op jit(solution)/shard_map/reduce_scatter | solution.py:328
  1044.2 4.0 bitcast_convert_fusion.3
  1048.2 2.6 convolution_convert_fusion
  1051.2 27.8 %reduce-scatter.23.cloned.1.call-done = bf16[2,128,1024]{2,1,0:T(8,128)(2,1)} async-done(((bf16[2,512,1024]{2,1,0:T(8,128)(2,1)}), bf16[2,128,1024]{2,1,0:T(8,128)(2,1)}) %reduce-scatter.23.cloned.1.call-update) | async-done | bytes 524304 | tf_op jit(solution)/shard_map/reduce_scatter | solution.py:280
  1079.0 2.1 convert_element_type.220
  1081.1 36.1 %reduce-scatter.21.cloned.1.call-done = bf16[2,256,512]{2,1,0:T(8,128)(2,1)} async-done(((bf16[2,1024,512]{2,1,0:T(8,128)(2,1)}), bf16[2,256,512]{2,1,0:T(8,128)(2,1)}) %reduce-scatter.21.cloned.1.call-update) | async-done | bytes 524304 | tf_op jit(solution)/shard_map/reduce_scatter | solution.py:277
  1117.2 2.1 convert_element_type.218
  1119.4 36.3 %reduce-scatter.19.cloned.1.call-done = bf16[2,256,512]{2,1,0:T(8,128)(2,1)} async-done(((bf16[2,1024,512]{2,1,0:T(8,128)(2,1)}), bf16[2,256,512]{2,1,0:T(8,128)(2,1)}) %reduce-scatter.19.cloned.1.call-update) | async-done | bytes 524304 | tf_op jit(solution)/shard_map/reduce_scatter | solution.py:274
  1155.6 2.1 convert_element_type.216
  1160.4 28.5 %reduce-scatter.17.cloned.1.call-done = bf16[128,256]{1,0:T(8,128)(2,1)} async-done(((bf16[1024,256]{1,0:T(8,128)(2,1)}), bf16[128,256]{1,0:T(8,128)(2,1)}) %reduce-scatter.17.cloned.1.call-update) | async-done | bytes 65552 | tf_op jit(solution)/shard_map/reduce_scatter | solution.py:371
  1190.5 31.2 %reduce-scatter.15.cloned.1.call-done = bf16[128,512]{1,0:T(8,128)(2,1)} async-done(((bf16[1024,512]{1,0:T(8,128)(2,1)}), bf16[128,512]{1,0:T(8,128)(2,1)}) %reduce-scatter.15.cloned.1.call-update) | async-done | bytes 131088 | tf_op jit(solution)/shard_map/reduce_scatter | solution.py:368
  1224.6 33.8 %reduce-scatter.13.cloned.1.call-done = bf16[128,2,1024]{2,0,1:T(8,128)(2,1)} async-done(((bf16[512,2,1024]{2,0,1:T(8,128)(2,1)}), bf16[128,2,1024]{2,0,1:T(8,128)(2,1)}) %reduce-scatter.13.cloned.1.call-update) | async-done | bytes 524304 | tf_op jit(solution)/shard_map/reduce_scatter | solution.py:357
  1260.0 3.1 fusion.82
  1263.1 1.8 copy.205
  1266.2 39.5 %all-reduce = (f32[1024]{0:T(1024)}, f32[1024]{0:T(1024)}) all-reduce(f32[1024]{0:T(1024)S(1)} %get-tuple-element.224, f32[1024]{0:T(1024)S(1)} %get-tuple-element.222), channel_id=1, replica_groups=mesh['narrow'=4,'wide'=8] {'narrow','wide'}, use_global_device_ids=true, to_apply=%region_28.29 | all-reduce | flops 2048 | bytes 16384 | tf_op jit(solution)/shard_map/psum | solution.py:375
  1305.7 76.4 %all-reduce.3.cloned.1.call-done = f32[1024,16]{0,1:T(8,128)} async-done(((f32[1024,16]{0,1:T(8,128)}), f32[1024,16]{0,1:T(8,128)}) %all-reduce.3.cloned.1.call-update) | async-done | bytes 65552 | tf_op jit(solution)/shard_map/psum | solution.py:375
  (181 shorter events, 48.0 us)
Async XLA Ops:
  7.2 506.0 %copy-start = (bf16[2,512,1024]{2,1,0:T(8,128)(2,1)S(1)}, bf16[2,512,1024]{2,1,0:T(8,128)(2,1)}, u32[]{:S(2)}) copy-start(bf16[2,512,1024]{2,1,0:T(8,128)(2,1)} %param.28) | copy-start | bytes 6291460
  7.2 41.7 %all-gather.4.cloned.1.call-start = ((), (), s32[]{:S(2)}) async-start(), calls=%async_computation.12 | async-start | bytes 2621440 | tf_op jit(solution)/shard_map/all_gather | solution.py:112
  8.6 3.9 copy-start.29
  10.7 90.7 %all-gather.6.cloned.1.call-start = ((), (), s32[]{:S(2)}) async-start(), calls=%async_computation.13 | async-start | bytes 4718592 | tf_op jit(solution)/shard_map/all_gather | solution.py:140
  12.5 39.2 %copy-start.21 = (bf16[1024,128]{0,1:T(8,128)(2,1)}, bf16[1024,128]{0,1:T(8,128)(2,1)S(1)}, u32[]{:S(2)}) copy-start(bf16[1024,128]{0,1:T(8,128)(2,1)S(1)} %copy.170) | copy-start | bytes 786436
  13.7 38.1 %copy-start.23 = (bf16[1024,128]{0,1:T(8,128)(2,1)}, bf16[1024,128]{0,1:T(8,128)(2,1)S(1)}, u32[]{:S(2)}) copy-start(bf16[1024,128]{0,1:T(8,128)(2,1)S(1)} %copy.171) | copy-start | bytes 786436
  15.1 36.8 %copy-start.19 = (bf16[1024,256]{0,1:T(8,128)(2,1)}, bf16[1024,256]{0,1:T(8,128)(2,1)S(1)}, u32[]{:S(2)}) copy-start(bf16[1024,256]{0,1:T(8,128)(2,1)S(1)} %copy.169) | copy-start | bytes 1572868
  16.1 38.3 %copy-start.16 = (f32[512,32]{0,1:T(8,128)}, f32[512,32]{0,1:T(8,128)S(1)}, u32[]{:S(2)}) copy-start(f32[512,32]{0,1:T(8,128)S(1)} %get-tuple-element.295) | copy-start | bytes 196612
  51.8 1.3 copy-start.12
  53.2 1.4 slice-start
  54.1 151.2 %reduce-scatter.9.cloned.1.call-start = ((), (), s32[]{:S(2)}) async-start(), calls=%async_computation.14 | async-start | bytes 2621440 | tf_op jit(solution)/shard_map/reduce_scatter | solution.py:177
  105.4 1.8 copy-start.7
  109.5 1.0 copy-start.8
  110.5 5.4 copy-start.28
  110.5 94.8 %copy-start.2 = (bf16[128,2,1024]{2,1,0:T(2,128)(2,1)S(1)}, bf16[128,2,1024]{2,1,0:T(2,128)(2,1)}, u32[]{:S(2)}) copy-start(bf16[128,2,1024]{2,1,0:T(2,128)(2,1)} %param.18) | copy-start | bytes 1572868
  111.9 0.8 copy-start.14
  111.9 94.7 %copy-start.26 = (f32[1024]{0:T(1024)S(1)}, f32[1024]{0:T(1024)}, u32[]{:S(2)}) copy-start(f32[1024]{0:T(1024)} %param.24) | copy-start | bytes 12292
  225.5 143.8 %all-to-all-start = ((bf16[8,2,192,1024]{3,2,1,0:T(8,128)(2,1)}), bf16[8,2,192,1024]{3,2,1,0:T(8,128)(2,1)}, u32[]{:S(2)}, u32[]{:S(2)}) async-start(bf16[8,2,192,1024]{3,2,1,0:T(8,128)(2,1)} %bitcast.304), calls=%async_computation.1 | async-start | bytes 12582912 | tf_op jit(solution)/shard_map/all_to_all | solution.py:219
  230.3 6.0 copy-start.25
  369.2 143.9 %all-to-all-start.2 = ((bf16[8,2,192,1024]{3,2,1,0:T(8,128)(2,1)}), bf16[8,2,192,1024]{3,2,1,0:T(8,128)(2,1)}, u32[]{:S(2)}, u32[]{:S(2)}) async-start(bf16[8,2,192,1024]{3,2,1,0:T(8,128)(2,1)} %bitcast.305), calls=%async_computation.3 | async-start | bytes 12582912 | tf_op jit(solution)/shard_map/all_to_all | solution.py:248
  374.2 9.7 copy-start.31
  525.9 3.6 copy-start.32
  533.0 143.7 %all-to-all-start.1 = ((bf16[8,2,192,1024]{3,2,1,0:T(8,128)(2,1)}), bf16[8,2,192,1024]{3,2,1,0:T(8,128)(2,1)}, u32[]{:S(2)}, u32[]{:S(2)}) async-start(bf16[8,2,192,1024]{3,2,1,0:T(8,128)(2,1)} %copy.182), calls=%async_computation.2 | async-start | bytes 12582912 | tf_op jit(solution)/shard_map/all_to_all | solution.py:228
  537.8 10.7 copy-start.13
  676.7 143.7 %all-to-all-start.3 = ((bf16[8,2,192,1024]{3,2,1,0:T(8,128)(2,1)}), bf16[8,2,192,1024]{3,2,1,0:T(8,128)(2,1)}, u32[]{:S(2)}, u32[]{:S(2)}) async-start(bf16[8,2,192,1024]{3,2,1,0:T(8,128)(2,1)} %copy.190), calls=%async_computation.4 | async-start | bytes 12582912 | tf_op jit(solution)/shard_map/all_to_all | solution.py:271
  681.5 197.9 %all-gather.8.cloned.1.call-start = ((), (), s32[]{:S(2)}) async-start(), calls=%async_computation.15 | async-start | bytes 2621440 | tf_op jit(solution)/shard_map/all_gather | solution.py:289
  681.9 14.6 %copy-start.6 = (f32[256,1024]{1,0:T(8,128)S(1)}, f32[256,1024]{1,0:T(8,128)}, u32[]{:S(2)}) copy-start(f32[256,1024]{1,0:T(8,128)} %mul.455) | copy-start | bytes 3145732
  835.0 9.0 copy-start.4
  840.5 4.0 copy-start.10
  844.0 38.5 %copy-start.3 = (f32[128,2,1024]{2,1,0:T(2,128)}, f32[128,2,1024]{2,1,0:T(2,128)S(1)}, u32[]{:S(2)}) copy-start(f32[128,2,1024]{2,1,0:T(2,128)S(1)} %reshape.399) | copy-start | bytes 3145732
  845.9 196.6 %reduce-scatter.11.cloned.1.call-start = ((), (), s32[]{:S(2)}) async-start(), calls=%async_computation.16 | async-start | bytes 4718592 | tf_op jit(solution)/shard_map/reduce_scatter | solution.py:328
  899.8 179.2 %reduce-scatter.23.cloned.1.call-start = ((), (), s32[]{:S(2)}) async-start(), calls=%async_computation.23 | async-start | bytes 2621440 | tf_op jit(solution)/shard_map/reduce_scatter | solution.py:280
  908.4 208.8 %reduce-scatter.21.cloned.1.call-start = ((), (), s32[]{:S(2)}) async-start(), calls=%async_computation.22 | async-start | bytes 2621440 | tf_op jit(solution)/shard_map/reduce_scatter | solution.py:277
  917.2 8.7 copy-start.17
  917.2 8.7 copy-start.18
  917.2 8.9 copy-start.15
  917.2 238.4 %reduce-scatter.19.cloned.1.call-start = ((), (), s32[]{:S(2)}) async-start(), calls=%async_computation.21 | async-start | bytes 2621440 | tf_op jit(solution)/shard_map/reduce_scatter | solution.py:274
  925.9 263.0 %reduce-scatter.17.cloned.1.call-start = ((), (), s32[]{:S(2)}) async-start(), calls=%async_computation.19 | async-start | bytes 589824 | tf_op jit(solution)/shard_map/reduce_scatter | solution.py:371
  929.3 292.4 %reduce-scatter.15.cloned.1.call-start = ((), (), s32[]{:S(2)}) async-start(), calls=%async_computation.18 | async-start | bytes 1179648 | tf_op jit(solution)/shard_map/reduce_scatter | solution.py:368
  1044.1 4.1 copy-start.20
  1044.2 4.1 copy-start.22
  1044.2 4.1 copy-start.24
  1048.2 210.3 %reduce-scatter.13.cloned.1.call-start = ((), (), s32[]{:S(2)}) async-start(), calls=%async_computation.17 | async-start | bytes 2621440 | tf_op jit(solution)/shard_map/reduce_scatter | solution.py:357
  1050.8 107.0 %copy-start.11 = (f32[256,1024]{1,0:T(8,128)S(1)}, f32[256,1024]{1,0:T(8,128)}, u32[]{:S(2)}) copy-start(f32[256,1024]{1,0:T(8,128)} %get-tuple-element.221) | copy-start | bytes 3145732
  1050.8 108.6 %copy-start.9 = (bf16[256,1024]{1,0:T(8,128)(2,1)S(1)}, bf16[256,1024]{1,0:T(8,128)(2,1)}, u32[]{:S(2)}) copy-start(bf16[256,1024]{1,0:T(8,128)(2,1)} %reshape.391) | copy-start | bytes 1572868
  1050.9 207.6 %copy-start.27 = (f32[1024]{0:T(1024)S(1)}, f32[1024]{0:T(1024)}, u32[]{:S(2)}) copy-start(f32[1024]{0:T(1024)} %param.19) | copy-start | bytes 12292
  1050.9 207.6 %copy-start.30 = (f32[128,2]{0,1:T(2,128)S(1)}, f32[128,2]{0,1:T(2,128)}, u32[]{:S(2)}) copy-start(f32[128,2]{0,1:T(2,128)} %copy-done.29) | copy-start | bytes 3076
  1050.9 331.2 %all-reduce.3.cloned.1.call-start = ((), (), s32[]{:S(2)}) async-start(), calls=%async_computation.20 | async-start | bytes 131072 | tf_op jit(solution)/shard_map/psum | solution.py:375
  1081.1 178.9 %copy-start.5 = (bf16[128,2,1024]{2,0,1:T(8,128)(2,1)S(1)}, bf16[128,2,1024]{2,0,1:T(8,128)(2,1)}, u32[]{:S(2)}) copy-start(bf16[128,2,1024]{2,0,1:T(8,128)(2,1)} %reduce-scatter.9.cloned.1.call-done) | copy-start | bytes 1572868
  1260.0 123.6 %copy-start.1 = (bf16[2,512,1024]{2,1,0:T(8,128)(2,1)S(1)}, bf16[2,512,1024]{2,1,0:T(8,128)(2,1)}, u32[]{:S(2)}) copy-start(bf16[2,512,1024]{2,1,0:T(8,128)(2,1)} %param.28) | copy-start | bytes 6291460
Sparse Core Ops, SparseCore 0:
  10.8 38.0 all-gather.3
  54.3 47.1 all-gather.5
  116.0 89.2 reduce-scatter.8
  846.1 33.2 all-gather.7
  899.9 142.5 reduce-scatter.10
  1045.7 33.3 reduce-scatter.22
  1082.0 35.1 reduce-scatter.20
  1120.4 35.1 reduce-scatter.18
  1157.9 30.9 reduce-scatter.16
  1191.1 30.5 reduce-scatter.14
  1224.9 33.4 reduce-scatter.12
  1264.5 117.5 all-reduce.2
where the time goes:
time: 1400 us; the launch traced here: 1390 us
  waiting for transfers between devices  1050 us (75%)
  matrix products  115 us (8%)
  local copies, waits for them, and re-layouts  85.8 us (6%)
  other arithmetic  65.1 us (5%)
  blocking collectives  39.5 us (3%)
  starting transfers between devices  21 us (2%)
  between operations  15.9 us (1%)
    all_to_all x1, waiting for transfers between devices, on_device(): lax.all_to_all(pack_rows(scaled_grads), 'wide', split_axis=0, concat_axis...  121 us
    all_to_all x1, waiting for transfers between devices, on_device(): lax.all_to_all(input_grads, 'wide', split_axis=0, concat_axis=0, tiled=True)  118 us
    all_to_all x1, waiting for transfers between devices, on_device(): lax.all_to_all(expert_out, 'wide', split_axis=0, concat_axis=0, tiled=True)  117 us
    all_to_all x1, waiting for transfers between devices, on_device(): lax.all_to_all(pack_rows(copies), 'wide', split_axis=0, concat_axis=0, ti...  117 us
    reduce_scatter x1, waiting for transfers between devices, on_device(): lax.psum_scatter(pair_grads.astype(jnp.bfloat16), 'wide', scatter_dimensi...  113 us
    reduce_scatter x1, waiting for transfers between devices, on_device(): lax.psum_scatter(jnp.einsum('tsc,cd->tsd', rows_part, w_out, preferred_el...  79.2 us
    psum x1, waiting for transfers between devices, on_device(): lax.psum((attn_gain, moe_gain, router_grads), ('narrow', 'wide'))  76.4 us
    all_gather x1, waiting for transfers between devices, on_device(): pair_all = lax.all_gather(pair_local, 'wide', axis=0, tiled=True)  46.7 us
  transfers between devices with their start and end apart: 16, of which 16 were waited for; matrix products, arithmetic and copies ran while one was open for 11% of the time, Pallas kernels for 0%

commit v1 on v0

--- a/solution.py
+++ b/solution.py
@@ -190,86 +190,69 @@
     expert_count = w_router.shape[1]
     local_experts = w_gate.shape[0]
     choose = routes.shape[-1]
-    capacity = 3 * token_count * choose // (2 * expert_count)
     expert_ids = routes.reshape(token_count, choose)
     onehot = (expert_ids[:, :, None] == lax.iota(jnp.int32, expert_count)[None, None, :]).astype(
         jnp.float32
     )
+    named = jnp.sum(onehot, axis=1)
     logits = jnp.dot(moe_flat, w_router, preferred_element_type=jnp.float32)
-    chosen = jnp.sum(onehot * logits[:, None, :], axis=-1)
-    gate_weights = jax.nn.softmax(chosen, axis=-1)
-    flat_hot = onehot.reshape(token_count * choose, expert_count)
-    before = jnp.cumsum(flat_hot, axis=0) - flat_hot
-    slot_index = jnp.sum(before * flat_hot, axis=-1).astype(jnp.int32)
-    destination = expert_ids.reshape(-1) * capacity + slot_index
-
-    def pack_rows(rows_in):
-        blank_rows = jnp.zeros((expert_count * capacity, model_width), jnp.bfloat16)
-        filled = blank_rows.at[destination].set(rows_in)
-        return filled.reshape(wide_count, local_experts, capacity, model_width)
-
-    def unpack_rows(arrived_back):
-        return arrived_back.reshape(expert_count * capacity, model_width)[destination].reshape(
-            token_count, choose, model_width
-        )
-
-    copies = jnp.broadcast_to(moe_flat[:, None, :], (token_count, choose, model_width)).reshape(
-        token_count * choose, model_width
-    )
-    arrived = lax.all_to_all(pack_rows(copies), "wide", split_axis=0, concat_axis=0, tiled=True)
-    gate_part = jnp.einsum("wecd,edf->wecf", arrived, w_gate, preferred_element_type=jnp.float32)
-    up_part = jnp.einsum("wecd,edf->wecf", arrived, w_up, preferred_element_type=jnp.float32)
+    masked = jnp.where(named > 0, logits, MASKED)
+    powers = jnp.exp(masked - jnp.max(masked, axis=-1, keepdims=True)) * named
+    shares = powers / jnp.sum(powers, axis=-1, keepdims=True)
+    upstream = cotangent.astype(jnp.float32)
+    upstream_flat = upstream.reshape(token_count, model_width)
+    upstream_all = lax.all_gather(
+        cotangent.reshape(token_count, model_width), "wide", axis=0, tiled=True
+    )
+    moe_all = lax.all_gather(moe_flat, "wide", axis=0, tiled=True)
+    shares_all = lax.all_gather(shares, "wide", axis=0, tiled=True)
+    first_expert = wide_place * local_experts
+    own_shares = lax.dynamic_slice_in_dim(shares_all, first_expert, local_experts, 1).T
+    gate_part = jnp.einsum("td,edf->etf", moe_all, w_gate, preferred_element_type=jnp.float32)
+    up_part = jnp.einsum("td,edf->etf", moe_all, w_up, preferred_element_type=jnp.float32)
+    down_back = jnp.einsum("td,efd->etf", upstream_all, w_down, preferred_element_type=jnp.float32)
     sigmoid_gate = jax.nn.sigmoid(gate_part)
     activated = gate_part * sigmoid_gate
-    hidden_low = (activated * up_part).astype(jnp.bfloat16)
-    expert_out = jnp.einsum(
-        "wecf,efd->wecd", hidden_low, w_down, preferred_element_type=jnp.float32
-    ).astype(jnp.bfloat16)
-    returned = lax.all_to_all(expert_out, "wide", split_axis=0, concat_axis=0, tiled=True)
-    expert_rows = unpack_rows(returned).astype(jnp.float32)
-    moe_part = jnp.sum(gate_weights[:, :, None] * expert_rows, axis=1)
-    layer_out = (residual + moe_part.reshape(local_rows, sequences, model_width)).astype(
-        jnp.bfloat16
-    )
-    upstream = cotangent.astype(jnp.float32)
-    upstream_flat = upstream.reshape(token_count, model_width)
-    pick_grads = jnp.sum(upstream_flat[:, None, :] * expert_rows, axis=-1)
-    chosen_grads = gate_weights * (
-        pick_grads - jnp.sum(gate_weights * pick_grads, axis=-1, keepdims=True)
-    )
-    logit_grads = jnp.sum(chosen_grads[:, :, None] * onehot, axis=1)
-    router_grads = jnp.dot(moe_flat.astype(jnp.float32).T, logit_grads, precision=PRECISE)
-    moe_grads = jnp.dot(logit_grads, w_router.astype(jnp.float32).T, precision=PRECISE)
-    scaled_grads = (
-        (gate_weights[:, :, None] * upstream_flat[:, None, :])
-        .astype(jnp.bfloat16)
-        .reshape(token_count * choose, model_width)
-    )
-    grad_arrived = lax.all_to_all(
-        pack_rows(scaled_grads), "wide", split_axis=0, concat_axis=0, tiled=True
-    )
-    hidden_grads = jnp.einsum(
-        "wecd,efd->wecf", grad_arrived, w_down, preferred_element_type=jnp.float32
-    )
-    down_update = jnp.einsum(
-        "wecf,wecd->efd", hidden_low, grad_arrived, preferred_element_type=jnp.float32
-    )
+    hidden = activated * up_part
+    hidden_low = hidden.astype(jnp.bfloat16)
+    own_picks = jnp.sum(hidden * down_back, axis=-1)
+    hidden_shared = (hidden * own_shares[:, :, None]).astype(jnp.bfloat16)
+    part_out = jnp.einsum("etf,efd->td", hidden_shared, w_down, preferred_element_type=jnp.float32)
+    hidden_grads = down_back * own_shares[:, :, None]
     slope = sigmoid_gate * (1.0 + gate_part * (1.0 - sigmoid_gate))
     gate_signal = (hidden_grads * up_part * slope).astype(jnp.bfloat16)
     up_signal = (hidden_grads * activated).astype(jnp.bfloat16)
-    gate_update = jnp.einsum(
-        "wecd,wecf->edf", arrived, gate_signal, preferred_element_type=jnp.float32
-    )
-    up_update = jnp.einsum("wecd,wecf->edf", arrived, up_signal, preferred_element_type=jnp.float32)
     input_grads = jnp.einsum(
-        "wecf,edf->wecd", gate_signal, w_gate, preferred_element_type=jnp.float32
-    )
-    input_grads = (
-        input_grads
-        + jnp.einsum("wecf,edf->wecd", up_signal, w_up, preferred_element_type=jnp.float32)
-    ).astype(jnp.bfloat16)
-    grads_back = lax.all_to_all(input_grads, "wide", split_axis=0, concat_axis=0, tiled=True)
-    moe_grads = moe_grads + jnp.sum(unpack_rows(grads_back).astype(jnp.float32), axis=1)
+        "etf,edf->td", gate_signal, w_gate, preferred_element_type=jnp.float32
+    ) + jnp.einsum("etf,edf->td", up_signal, w_up, preferred_element_type=jnp.float32)
+    pick_high = own_picks.T.astype(jnp.bfloat16)
+    pick_low = (own_picks.T - pick_high.astype(jnp.float32)).astype(jnp.bfloat16)
+    pick_pair = jnp.zeros((moe_all.shape[0], 2, expert_count), jnp.bfloat16)
+    pick_pair = lax.dynamic_update_slice(
+        pick_pair, jnp.stack([pick_high, pick_low], axis=1), (0, 0, first_expert)
+    ).reshape(moe_all.shape[0], 2 * expert_count)
+    pick_pair = lax.psum_scatter(pick_pair, "wide", scatter_dimension=0, tiled=True).astype(
+        jnp.float32
+    )
+    moe_part = lax.psum_scatter(
+        part_out.astype(jnp.bfloat16), "wide", scatter_dimension=0, tiled=True
+    ).astype(jnp.float32)
+    copy_sum = lax.psum_scatter(
+        input_grads.astype(jnp.bfloat16), "wide", scatter_dimension=0, tiled=True
+    ).astype(jnp.float32)
+    layer_out = (residual + moe_part.reshape(local_rows, sequences, model_width)).astype(
+        jnp.bfloat16
+    )
+    picks = pick_pair[:, :expert_count] + pick_pair[:, expert_count:]
+    logit_grads = shares * (picks - jnp.sum(shares * picks, axis=-1, keepdims=True))
+    router_grads = jnp.dot(moe_flat.astype(jnp.float32).T, logit_grads, precision=PRECISE)
+    moe_grads = jnp.dot(logit_grads, w_router.astype(jnp.float32).T, precision=PRECISE)
+    moe_grads = moe_grads + copy_sum
+    down_update = jnp.einsum(
+        "etf,td->efd", hidden_shared, upstream_all, preferred_element_type=jnp.float32
+    )
+    gate_update = jnp.einsum("td,etf->edf", moe_all, gate_signal, preferred_element_type=jnp.float32)
+    up_update = jnp.einsum("td,etf->edf", moe_all, up_signal, preferred_element_type=jnp.float32)
     expert_grads = (
         lax.psum_scatter(
             gate_update.astype(jnp.bfloat16), "narrow", scatter_dimension=1, tiled=True
@@ -372,7 +355,14 @@
             out_update.T.astype(jnp.bfloat16), "wide", scatter_dimension=0, tiled=True
         ).astype(jnp.float32),
     )
-    summed_small = lax.psum((attn_gain, moe_gain, router_grads), ("narrow", "wide"))
+    moe_small = lax.psum(
+        jnp.concatenate([moe_gain[:, None], router_grads], axis=1), ("narrow", "wide")
+    )
+    summed_small = (
+        lax.psum(attn_gain, ("narrow", "wide")),
+        moe_small[:, 0],
+        moe_small[:, 1:],
+    )
     return (
         layer_out,
         token_grads,

time: 1400 us -> 1160 us (0.83)
  waiting for transfers between devices: 1050 us -> 867 us
  local copies, waits for them, and re-layouts: 85.8 us -> 47.9 us
  other arithmetic: 65.1 us -> 43.3 us
  starting transfers between devices: 21 us -> 1.56 us
  blocking collectives: 39.5 us -> 53.7 us
    all_to_all x4 -> x0, waiting for transfers between devices: 473 us -> none  [the longest x1 121 us: on_device(): lax.all_to_all(pack_rows(scaled_grads), 'wide', split_axis=0, concat_axis...]
    reduce_scatter x0 -> x3, waiting for transfers between devices: none -> 126 us  [the longest x1 50.3 us: on_device(): lax.psum_scatter(part_out.astype(jnp.bfloat16), 'wide', scatter_dimension...]
    all_gather x0 -> x2, waiting for transfers between devices: none -> 75 us  [the longest x1 44.7 us: on_device(): moe_all = lax.all_gather(moe_flat, 'wide', axis=0, tiled=True)]
    psum x1, waiting for transfers between devices: 76.4 us -> 123 us  [on_device(): lax.psum(jnp.concatenate([moe_gain[:, None], router_grads], axis=1), ('na...]
    reduce_scatter x1, waiting for transfers between devices: 113 us -> 148 us  [on_device(): lax.psum_scatter(pair_grads.astype(jnp.bfloat16), 'wide', scatter_dimensi...]
    gather x2 -> x0, local copies, waits for them, and re-layouts: 29.2 us -> none  [unpack_rows(): arrived_back.reshape(expert_count * capacity, model_width)[destination]]
    all_to_all x4 -> x0, starting transfers between devices: 19.3 us -> none  [the longest x1 4.95 us: on_device(): lax.all_to_all(pack_rows(scaled_grads), 'wide', split_axis=0, concat_axis...]
    scatter x1 -> x0, other arithmetic: 14.6 us -> none  [pack_rows(): filled = blank_rows.at[destination].set(rows_in)]
  transfers between devices with their start and end apart: 16 -> 17, of which waited for: 16 -> 17; matrix products, arithmetic and copies ran while one was open for 11% -> 8% of each run, Pallas kernels for 0% -> 0%
where the time goes in v1:
time: 1160 us; the launch traced here: 1150 us
  waiting for transfers between devices  867 us (75%)
  matrix products  125 us (11%)
  blocking collectives  53.7 us (5%)
  local copies, waits for them, and re-layouts  47.9 us (4%)
  other arithmetic  43.3 us (4%)
  between operations  15.6 us (1%)
    reduce_scatter x1, waiting for transfers between devices, on_device(): lax.psum_scatter(pair_grads.astype(jnp.bfloat16), 'wide', scatter_dimensi...  148 us
    psum x1, waiting for transfers between devices, on_device(): lax.psum(jnp.concatenate([moe_gain[:, None], router_grads], axis=1), ('na...  123 us
    reduce_scatter x1, waiting for transfers between devices, on_device(): lax.psum_scatter(jnp.einsum('tsc,cd->tsd', rows_part, w_out, preferred_el...  89.1 us
    reduce_scatter x1, waiting for transfers between devices, on_device(): lax.psum_scatter(part_out.astype(jnp.bfloat16), 'wide', scatter_dimension...  50.3 us
    reduce_scatter x1, waiting for transfers between devices, on_device(): lax.psum_scatter(input_grads.astype(jnp.bfloat16), 'wide', scatter_dimens...  48.2 us
    all_gather x1, waiting for transfers between devices, on_device(): pair_all = lax.all_gather(pair_local, 'wide', axis=0, tiled=True)  46.6 us
    all_gather x1, waiting for transfers between devices, on_device(): moe_all = lax.all_gather(moe_flat, 'wide', axis=0, tiled=True)  44.7 us
    psum x1, blocking collectives, on_device(): lax.psum(attn_gain, ('narrow', 'wide'))  39.3 us
  transfers between devices with their start and end apart: 17, of which 17 were waited for; matrix products, arithmetic and copies ran while one was open for 8% of the time, Pallas kernels for 0%

profile of v1, /device:TPU:0, one launch (start us, length us, event | category | flops | bytes accessed | tf_op | source)
XLA Modules:
  0.0 1154.0 jit_solution(15104490900131088374)
XLA Ops:
  9.2 2.0 fusion.64
  16.7 32.7 %all-gather.6.cloned.1.call-done = bf16[512,2,1024]{2,0,1:T(8,128)(2,1)} async-done(((bf16[128,2,1024]{2,0,1:T(8,128)(2,1)}), bf16[512,2,1024]{2,0,1:T(8,128)(2,1)}) %all-gather.6.cloned.1.call-update) | async-done | bytes 2097168 | tf_op jit(solution)/shard_map/all_gather | solution.py:112
  49.4 2.9 fusion.71
  55.3 46.6 %all-gather.8.cloned.1.call-done = bf16[4096,2,256]{0,2,1:T(8,128)(2,1)} async-done(((bf16[512,2,256]{0,2,1:T(8,128)(2,1)}), bf16[4096,2,256]{0,2,1:T(8,128)(2,1)}) %all-gather.8.cloned.1.call-update) | async-done | bytes 4194320 | tf_op jit(solution)/shard_map/all_gather | solution.py:140
  103.1 7.9 while.28
  104.4 1.5 fusion.148
  105.9 1.7 fusion.149
  107.7 2.3 fusion.150
  113.2 3.1 convolution_convert_fusion.1
  116.4 89.1 %reduce-scatter.12.cloned.1.call-done = bf16[128,2,1024]{2,0,1:T(8,128)(2,1)} async-done(((bf16[512,2,1024]{2,0,1:T(8,128)(2,1)}), bf16[128,2,1024]{2,0,1:T(8,128)(2,1)}) %reduce-scatter.12.cloned.1.call-update) | async-done | bytes 524304 | tf_op jit(solution)/shard_map/reduce_scatter | solution.py:177
  209.4 2.0 reshape.225
  211.6 2.0 reshape.228
  214.1 44.7 %all-gather.10.cloned.1.call-done = bf16[2048,1024]{1,0:T(8,128)(2,1)} async-done(((bf16[256,1024]{1,0:T(8,128)(2,1)}), bf16[2048,1024]{1,0:T(8,128)(2,1)}) %all-gather.10.cloned.1.call-update) | async-done | bytes 4194320 | tf_op jit(solution)/shard_map/all_gather | solution.py:207
  258.8 10.8 fusion.45
  269.7 6.8 fusion.47
  276.5 30.3 %all-gather.12.cloned.1.call-done = bf16[2048,1024]{1,0:T(8,128)(2,1)} async-done(((bf16[256,1024]{1,0:T(8,128)(2,1)}), bf16[2048,1024]{1,0:T(8,128)(2,1)}) %all-gather.12.cloned.1.call-update) | async-done | bytes 4194320 | tf_op jit(solution)/shard_map/all_gather | solution.py:204
  306.8 12.2 %fusion.29 = (f32[2,2048]{1,0:T(2,128)S(1)}, f32[2,512,2048]{2,1,0:T(8,128)}) fusion(f32[2048,2,512]{0,2,1:T(8,128)} %fusion.45, f32[2048,2,512]{0,2,1:T(8,128)} %fusion.47, bf16[2,512,1024]{2,1,0:T(8,128)(2,1)S(1)} %copy-done, bf16[2048,1024]{1,0:T(8,128)(2,1)} %all-gather.12.cloned.1.call-done), kind=kOutput, calls=%fused_computation.46 | convolution fusion | flops 4309643264 | bytes 31473664 | tf_op jit(solution)/shard_map/td,efd->etf/dot_general | solution.py:213
  321.2 27.6 %reduce-scatter.16.cloned.1.call-done = bf16[256,32]{0,1:T(8,128)(2,1)} async-done(((bf16[2048,32]{0,1:T(8,128)(2,1)}), bf16[256,32]{0,1:T(8,128)(2,1)}) %reduce-scatter.16.cloned.1.call-update) | async-done | bytes 16400 | tf_op jit(solution)/shard_map/reduce_scatter | solution.py:234
  349.6 14.4 %all_gather.21 = f32[2048,16]{0,1:T(8,128)S(1)} all-gather(f32[256,16]{0,1:T(8,128)S(1)} %get-tuple-element.239), channel_id=1, replica_groups=mesh['narrow'=4,'wide'=8] {'wide'}, dimensions={0}, use_global_device_ids=true | all-gather | bytes 147456 | tf_op jit(solution)/shard_map/all_gather | solution.py:208
  364.0 12.8 %multiply_convert_fusion = (bf16[2,2048,512]{1,2,0:T(8,128)(2,1)S(1)}, bf16[2,2048,512]{1,2,0:T(8,128)(2,1)S(1)}, bf16[2,2048,512]{1,2,0:T(8,128)(2,1)}) fusion(f32[2,512,2048]{2,1,0:T(8,128)} %get-tuple-element.271, f32[2,2048]{1,0:T(2,128)S(1)} %dynamic-slice_bitcast_fusion, f32[2048,2,512]{0,2,1:T(8,128)} %fusion.47, f32[2048,2,512]{0,2,1:T(8,128)} %fusion.45), kind=kLoop, calls=%fused_computation.60 | loop fusion | flops 35651584 | bytes 37765120 | tf_op jit(solution)/shard_map/convert_element_type | solution.py:224
  376.9 6.9 fusion.87
  383.8 8.4 fusion.28
  392.3 48.2 %reduce-scatter.18.cloned.1.call-done = bf16[256,1024]{1,0:T(8,128)(2,1)} async-done(((bf16[2048,1024]{1,0:T(8,128)(2,1)}), bf16[256,1024]{1,0:T(8,128)(2,1)}) %reduce-scatter.18.cloned.1.call-update) | async-done | bytes 524304 | tf_op jit(solution)/shard_map/reduce_scatter | solution.py:240
  440.5 2.6 convolution_add_fusion
  443.2 2.8 reshape.230
  446.0 1.9 multiply_reduce_fusion
  447.9 2.9 fusion.83
  451.0 33.4 %all-gather.14.cloned.1.call-done = bf16[512,2,1024]{2,0,1:T(8,128)(2,1)} async-done(((bf16[128,2,1024]{2,0,1:T(8,128)(2,1)}), bf16[512,2,1024]{2,0,1:T(8,128)(2,1)}) %all-gather.14.cloned.1.call-update) | async-done | bytes 2097168 | tf_op jit(solution)/shard_map/all_gather | solution.py:272
  484.4 3.3 convolution_convert_fusion.2
  489.0 2.3 broadcast_in_dim.42.clone
  492.4 20.5 %while.29 = (s32[]{:T(128)}, f32[512,2,2,2,64]{0,4,3,2,1:T(8,128)}, bf16[4096,2,256]{2,0,1:T(8,128)(2,1)}, s32[]{:T(128)}, bf16[4096,2,256]{0,2,1:T(8,128)(2,1)}...) while((s32[]{:T(128)}, f32[512,2,2,2,64]{0,4,3,2,1:T(8,128)}, ...), condition=%wide.region_18.19_spmd.clone, body=%wide.region_17.18_spmd.clone.sunk | while | flops 1365246976 | bytes 65069300 | solution.py:310
  495.0 4.1 fusion.162
  499.1 1.9 copy-done.1
  502.4 3.3 fusion.164
  506.8 1.9 constant_dynamic-update-slice_fusion.2
  508.6 4.3 fusion.163
  513.0 9.3 convert_bitcast_fusion.1
  522.5 9.3 convert_bitcast_fusion
  531.9 9.3 fusion.53
  541.2 8.4 bitcast_convert_fusion
  552.4 3.2 fusion.60
  558.6 147.7 %reduce-scatter.20.cloned.1.call-done = bf16[512,2,256]{2,0,1:T(8,128)(2,1)} async-done(((bf16[4096,2,256]{2,0,1:T(8,128)(2,1)}), bf16[512,2,256]{2,0,1:T(8,128)(2,1)}) %reduce-scatter.20.cloned.1.call-update) | async-done | bytes 524304 | tf_op jit(solution)/shard_map/reduce_scatter | solution.py:311
  706.3 1.8 slice_convert_fusion.1
  709.3 4.2 bitcast_convert_fusion.1
  713.8 3.7 convolution_convert_fusion
  717.6 24.9 %reduce-scatter.28.cloned.1.call-done = bf16[2,256,512]{1,2,0:T(8,128)(2,1)} async-done(((bf16[2,1024,512]{1,2,0:T(8,128)(2,1)}), bf16[2,256,512]{1,2,0:T(8,128)(2,1)}) %reduce-scatter.28.cloned.1.call-update) | async-done | bytes 524304 | tf_op jit(solution)/shard_map/reduce_scatter | solution.py:257
  742.5 2.2 copy.120
  744.7 36.2 %reduce-scatter.30.cloned.1.call-done = bf16[2,256,512]{1,2,0:T(8,128)(2,1)} async-done(((bf16[2,1024,512]{1,2,0:T(8,128)(2,1)}), bf16[2,256,512]{1,2,0:T(8,128)(2,1)}) %reduce-scatter.30.cloned.1.call-update) | async-done | bytes 524304 | tf_op jit(solution)/shard_map/reduce_scatter | solution.py:260
  781.0 2.2 copy.121
  783.2 35.8 %reduce-scatter.32.cloned.1.call-done = bf16[2,128,1024]{2,1,0:T(8,128)(2,1)} async-done(((bf16[2,512,1024]{2,1,0:T(8,128)(2,1)}), bf16[2,128,1024]{2,1,0:T(8,128)(2,1)}) %reduce-scatter.32.cloned.1.call-update) | async-done | bytes 524304 | tf_op jit(solution)/shard_map/reduce_scatter | solution.py:263
  819.0 2.1 convert_element_type.195
  821.1 50.3 %reduce-scatter.14.cloned.1.call-done = bf16[256,1024]{1,0:T(8,128)(2,1)} async-done(((bf16[2048,1024]{1,0:T(8,128)(2,1)}), bf16[256,1024]{1,0:T(8,128)(2,1)}) %reduce-scatter.14.cloned.1.call-update) | async-done | bytes 524304 | tf_op jit(solution)/shard_map/reduce_scatter | solution.py:237
  871.4 2.7 reshape.236
  874.1 123.0 %all-reduce.2.cloned.1.call-done = f32[1024,17]{0,1:T(8,128)} async-done(((f32[1024,17]{0,1:T(8,128)}), f32[1024,17]{0,1:T(8,128)}) %all-reduce.2.cloned.1.call-update) | async-done | bytes 69648 | tf_op jit(solution)/shard_map/psum | solution.py:358
  997.1 1.5 slice.118
  1000.0 31.1 %reduce-scatter.26.cloned.1.call-done = bf16[128,256]{1,0:T(8,128)(2,1)} async-done(((bf16[1024,256]{1,0:T(8,128)(2,1)}), bf16[128,256]{1,0:T(8,128)(2,1)}) %reduce-scatter.26.cloned.1.call-update) | async-done | bytes 65552 | tf_op jit(solution)/shard_map/reduce_scatter | solution.py:354
  1032.7 31.2 %reduce-scatter.24.cloned.1.call-done = bf16[128,512]{1,0:T(8,128)(2,1)} async-done(((bf16[1024,512]{1,0:T(8,128)(2,1)}), bf16[128,512]{1,0:T(8,128)(2,1)}) %reduce-scatter.24.cloned.1.call-update) | async-done | bytes 131088 | tf_op jit(solution)/shard_map/reduce_scatter | solution.py:351
  1063.9 1.5 slice.114
  1065.4 1.4 fusion.84
  1066.8 33.3 %reduce-scatter.22.cloned.1.call-done = bf16[128,2,1024]{2,0,1:T(8,128)(2,1)} async-done(((bf16[512,2,1024]{2,0,1:T(8,128)(2,1)}), bf16[128,2,1024]{2,0,1:T(8,128)(2,1)}) %reduce-scatter.22.cloned.1.call-update) | async-done | bytes 524304 | tf_op jit(solution)/shard_map/reduce_scatter | solution.py:340
  1100.1 1.5 fusion.66
  1101.6 3.0 fusion.63
  1104.6 1.8 copy.118
  1107.7 39.3 %psum.14 = f32[1024]{0:T(1024)} all-reduce(f32[1024]{0:T(1024)S(1)} %get-tuple-element.198), channel_id=1, replica_groups=mesh['narrow'=4,'wide'=8] {'narrow','wide'}, use_global_device_ids=true, to_apply=%region_23.24 | all-reduce | flops 1024 | bytes 8192 | tf_op jit(solution)/shard_map/psum | solution.py:362
  (171 shorter events, 42.2 us)
Async XLA Ops:
  7.2 299.6 %copy-start = (bf16[2,512,1024]{2,1,0:T(8,128)(2,1)S(1)}, bf16[2,512,1024]{2,1,0:T(8,128)(2,1)}, u32[]{:S(2)}) copy-start(bf16[2,512,1024]{2,1,0:T(8,128)(2,1)} %param.28) | copy-start | bytes 6291460
  7.2 42.2 %all-gather.6.cloned.1.call-start = ((), (), s32[]{:S(2)}) async-start(), calls=%async_computation.11 | async-start | bytes 2621440 | tf_op jit(solution)/shard_map/all_gather | solution.py:112
  8.6 0.6 copy-start.26
  11.3 90.7 %all-gather.8.cloned.1.call-start = ((), (), s32[]{:S(2)}) async-start(), calls=%async_computation.12 | async-start | bytes 4718592 | tf_op jit(solution)/shard_map/all_gather | solution.py:140
  13.2 39.1 %copy-start.16 = (bf16[1024,256]{0,1:T(8,128)(2,1)}, bf16[1024,256]{0,1:T(8,128)(2,1)S(1)}, u32[]{:S(2)}) copy-start(bf16[1024,256]{0,1:T(8,128)(2,1)S(1)} %copy.93) | copy-start | bytes 1572868
  14.5 37.9 %copy-start.21 = (bf16[1024,128]{0,1:T(8,128)(2,1)}, bf16[1024,128]{0,1:T(8,128)(2,1)S(1)}, u32[]{:S(2)}) copy-start(bf16[1024,128]{0,1:T(8,128)(2,1)S(1)} %copy.94) | copy-start | bytes 786436
  15.7 36.7 %copy-start.22 = (bf16[1024,128]{0,1:T(8,128)(2,1)}, bf16[1024,128]{0,1:T(8,128)(2,1)S(1)}, u32[]{:S(2)}) copy-start(bf16[1024,128]{0,1:T(8,128)(2,1)S(1)} %copy.95) | copy-start | bytes 786436
  16.7 38.0 %copy-start.13 = (f32[512,32]{0,1:T(8,128)}, f32[512,32]{0,1:T(8,128)S(1)}, u32[]{:S(2)}) copy-start(f32[512,32]{0,1:T(8,128)S(1)} %get-tuple-element.269) | copy-start | bytes 196612
  52.3 1.3 copy-start.11
  53.7 1.4 slice-start
  54.7 150.9 %reduce-scatter.12.cloned.1.call-start = ((), (), s32[]{:S(2)}) async-start(), calls=%async_computation.13 | async-start | bytes 2621440 | tf_op jit(solution)/shard_map/reduce_scatter | solution.py:177
  105.9 1.8 copy-start.6
  110.0 1.0 copy-start.7
  111.0 94.6 %copy-start.3 = (bf16[128,2,1024]{2,1,0:T(2,128)(2,1)S(1)}, bf16[128,2,1024]{2,1,0:T(2,128)(2,1)}, u32[]{:S(2)}) copy-start(bf16[128,2,1024]{2,1,0:T(2,128)(2,1)} %param.18) | copy-start | bytes 1572868
  111.0 95.8 %copy-start.24 = (f32[1024]{0:T(1024)S(1)}, f32[1024]{0:T(1024)}, u32[]{:S(2)}) copy-start(f32[1024]{0:T(1024)} %param.24) | copy-start | bytes 12292
  112.4 0.8 copy-start.12
  116.4 97.5 %copy-start.30 = (s32[128,2,8]{0,2,1:T(8,128)S(1)}, s32[128,2,8]{0,2,1:T(8,128)}, u32[]{:S(2)}) copy-start(s32[128,2,8]{0,2,1:T(8,128)} %param.29) | copy-start | bytes 24580
  116.4 142.4 %all-gather.10.cloned.1.call-start = ((), (), s32[]{:S(2)}) async-start(), calls=%async_computation.14 | async-start | bytes 4718592 | tf_op jit(solution)/shard_map/all_gather | solution.py:207
  211.5 95.3 %all-gather.12.cloned.1.call-start = ((), (), s32[]{:S(2)}) async-start(), calls=%async_computation.16 | async-start | bytes 4718592 | tf_op jit(solution)/shard_map/all_gather | solution.py:204
  213.6 135.3 %reduce-scatter.16.cloned.1.call-start = ((), (), s32[]{:S(2)}) async-start(), calls=%async_computation.17 | async-start | bytes 147456 | tf_op jit(solution)/shard_map/reduce_scatter | solution.py:234
  258.8 10.8 copy-start.31
  258.8 10.8 copy-start.32
  276.5 43.4 %copy-start.23 = (bf16[1024,16]{0,1:T(8,128)(2,1)S(1)}, bf16[1024,16]{0,1:T(8,128)(2,1)}, u32[]{:S(2)}) copy-start(bf16[1024,16]{0,1:T(8,128)(2,1)} %param.25) | copy-start | bytes 98308
  319.1 0.7 copy-start.19
  319.8 120.7 %reduce-scatter.18.cloned.1.call-start = ((), (), s32[]{:S(2)}) async-start(), calls=%async_computation.18 | async-start | bytes 4718592 | tf_op jit(solution)/shard_map/reduce_scatter | solution.py:240
  349.6 90.9 %copy-start.28 = (f32[256]{0:T(256)}, f32[256]{0:T(256)S(1)}, u32[]{:S(2)}) copy-start(f32[256]{0:T(256)S(1)} %get-tuple-element.238) | copy-start | bytes 3076
  364.0 12.8 %copy-start.33 = (bf16[2,1024,512]{2,1,0:T(8,128)(2,1)S(1)}, bf16[2,1024,512]{2,1,0:T(8,128)(2,1)}, u32[]{:S(2)}) copy-start(bf16[2,1024,512]{2,1,0:T(8,128)(2,1)} %param.26) | copy-start | bytes 6291460
  376.8 6.9 copy-start.10
  376.8 6.9 copy-start.9
  376.9 6.9 copy-start.34
  392.3 92.2 %all-gather.14.cloned.1.call-start = ((), (), s32[]{:S(2)}) async-start(), calls=%async_computation.19 | async-start | bytes 2621440 | tf_op jit(solution)/shard_map/all_gather | solution.py:272
  450.8 255.5 %reduce-scatter.20.cloned.1.call-start = ((), (), s32[]{:S(2)}) async-start(), calls=%async_computation.20 | async-start | bytes 4718592 | tf_op jit(solution)/shard_map/reduce_scatter | solution.py:311
  484.4 3.3 copy-start.8
  499.1 2.0 copy-start.1
  512.9 229.6 %reduce-scatter.28.cloned.1.call-start = ((), (), s32[]{:S(2)}) async-start(), calls=%async_computation.25 | async-start | bytes 2621440 | tf_op jit(solution)/shard_map/reduce_scatter | solution.py:257
  522.2 258.7 %reduce-scatter.30.cloned.1.call-start = ((), (), s32[]{:S(2)}) async-start(), calls=%async_computation.26 | async-start | bytes 2621440 | tf_op jit(solution)/shard_map/reduce_scatter | solution.py:260
  531.9 287.1 %reduce-scatter.32.cloned.1.call-start = ((), (), s32[]{:S(2)}) async-start(), calls=%async_computation.27 | async-start | bytes 2621440 | tf_op jit(solution)/shard_map/reduce_scatter | solution.py:263
  541.2 330.2 %reduce-scatter.14.cloned.1.call-start = ((), (), s32[]{:S(2)}) async-start(), calls=%async_computation.15 | async-start | bytes 4718592 | tf_op jit(solution)/shard_map/reduce_scatter | solution.py:237
  549.7 0.7 copy-start.29
  549.7 6.0 copy-start.2
  549.7 6.0 copy-start.14
  549.7 6.0 copy-start.15
  549.7 447.4 %all-reduce.2.cloned.1.call-start = ((), (), s32[]{:S(2)}) async-start(), calls=%async_computation.24 | async-start | bytes 196608 | tf_op jit(solution)/shard_map/psum | solution.py:358
  552.4 478.7 %reduce-scatter.26.cloned.1.call-start = ((), (), s32[]{:S(2)}) async-start(), calls=%async_computation.23 | async-start | bytes 589824 | tf_op jit(solution)/shard_map/reduce_scatter | solution.py:354
  556.6 507.3 %reduce-scatter.24.cloned.1.call-start = ((), (), s32[]{:S(2)}) async-start(), calls=%async_computation.22 | async-start | bytes 1179648 | tf_op jit(solution)/shard_map/reduce_scatter | solution.py:351
  709.3 4.5 copy-start.17
  709.3 4.6 copy-start.18
  709.3 4.6 copy-start.20
  713.5 386.6 %reduce-scatter.22.cloned.1.call-start = ((), (), s32[]{:S(2)}) async-start(), calls=%async_computation.21 | async-start | bytes 2621440 | tf_op jit(solution)/shard_map/reduce_scatter | solution.py:340
  717.5 382.5 %copy-start.4 = (bf16[128,2,1024]{2,1,0:T(2,128)(2,1)S(1)}, bf16[128,2,1024]{2,1,0:T(2,128)(2,1)}, u32[]{:S(2)}) copy-start(bf16[128,2,1024]{2,1,0:T(2,128)(2,1)} %param.18) | copy-start | bytes 1572868
  717.6 382.5 %copy-start.25 = (f32[1024]{0:T(1024)S(1)}, f32[1024]{0:T(1024)}, u32[]{:S(2)}) copy-start(f32[1024]{0:T(1024)} %param.19) | copy-start | bytes 12292
  717.6 382.5 %copy-start.27 = (f32[128,2]{0,1:T(2,128)S(1)}, f32[128,2]{0,1:T(2,128)}, u32[]{:S(2)}) copy-start(f32[128,2]{0,1:T(2,128)} %copy-done.26) | copy-start | bytes 3076
  717.6 384.0 %copy-start.5 = (bf16[128,2,1024]{2,0,1:T(8,128)(2,1)S(1)}, bf16[128,2,1024]{2,0,1:T(8,128)(2,1)}, u32[]{:S(2)}) copy-start(bf16[128,2,1024]{2,0,1:T(8,128)(2,1)} %reduce-scatter.12.cloned.1.call-done) | copy-start | bytes 1572868
Sparse Core Ops, SparseCore 0:
  11.4 38.0 all-gather.5
  54.8 47.1 all-gather.7
  116.5 89.0 reduce-scatter.11
  211.6 47.1 all-gather.9
  260.9 45.8 all-gather.11
  319.9 28.8 reduce-scatter.15
  392.4 48.0 reduce-scatter.17
  450.9 33.4 all-gather.13
  513.0 193.2 reduce-scatter.19
  709.1 33.3 reduce-scatter.27
  745.8 35.1 reduce-scatter.29
  783.8 35.1 reduce-scatter.31
  821.4 49.9 reduce-scatter.13
  878.4 118.6 all-reduce.1
  999.3 31.7 reduce-scatter.25
  1033.2 30.5 reduce-scatter.23
  1066.7 33.3 reduce-scatter.21

commit v2 on v1

v2 whole, which is shorter than its diff:
```python
import functools

import jax
import jax.numpy as jnp
from jax import lax
from jax.experimental import pallas as pl
from jax.experimental.pallas import tpu as pltpu
from jax.sharding import PartitionSpec as P

HD = 64


EPSILON = 1e-06
ROPE_BASE = 10000.0
MASKED = -1e30
PRECISE = lax.Precision.HIGHEST
VMEM_BYTES = 56 << 20


def dot_t(left, right):
    return lax.dot_general(left, right, (((1,), (1,)), ((), ())), preferred_element_type=jnp.float32)


def dot_n(left, right):
    return lax.dot_general(left, right, (((1,), (0,)), ((), ())), preferred_element_type=jnp.float32)


def dot_c(left, right):
    return lax.dot_general(left, right, (((0,), (0,)), ((), ())), preferred_element_type=jnp.float32)


def head_mask(shape, head):
    lane = lax.broadcasted_iota(jnp.int32, shape, len(shape) - 1)
    return jnp.logical_and(lane >= head * HD, lane < (head + 1) * HD)


def only_head(block, head):
    if block.shape[-1] == HD:
        return block
    return jnp.where(head_mask(block.shape, head), block, jnp.zeros_like(block))


def attn_fwd_kernel(place_ref, q_ref, k_ref, v_ref, o_ref, low_ref, log_ref, top_ref, sum_ref, acc_ref):
    step = pl.program_id(1)
    place = place_ref[0]
    groups, rows, cols = q_ref.shape[1:]
    pairs = [(group, head) for group in range(groups) for head in range(cols // HD)]

    @pl.when(step == 0)
    def _():
        top_ref[...] = jnp.full(top_ref.shape, MASKED, jnp.float32)
        sum_ref[...] = jnp.zeros(sum_ref.shape, jnp.float32)
        acc_ref[...] = jnp.zeros(acc_ref.shape, jnp.float32)

    def one(masked):
        key_block = k_ref[0]

        def scores_of(number):
            group, head = pairs[number]
            return dot_t(key_block, only_head(q_ref[0, group], head))

        ahead = scores_of(0)
        for number, (group, head) in enumerate(pairs):
            part = pl.ds(number * rows, rows)
            lanes = pl.ds(head * HD, HD)
            scores = ahead
            if number + 1 < len(pairs):
                ahead = scores_of(number + 1)
            if masked:
                row = lax.broadcasted_iota(jnp.int32, scores.shape, 0)
                col = lax.broadcasted_iota(jnp.int32, scores.shape, 1)
                scores = jnp.where(row <= col, scores, MASKED)
            old = top_ref[:1, part]
            new = jnp.maximum(old, jnp.max(scores, axis=0, keepdims=True))
            fade = jnp.exp(old - new)
            weights = jnp.exp(scores - new)
            sum_ref[:1, part] = sum_ref[:1, part] * fade + jnp.sum(weights, axis=0, keepdims=True)
            acc_ref[group, lanes, :] = acc_ref[group, lanes, :] * fade + dot_n(
                v_ref[0, lanes, :], weights.astype(jnp.bfloat16)
            )
            top_ref[:1, part] = new

    @pl.when(step < place)
    def _():
        one(False)

    @pl.when(step == place)
    def _():
        one(True)
        for number, (group, head) in enumerate(pairs):
            part = pl.ds(number * rows, rows)
            lanes = pl.ds(head * HD, HD)
            total = sum_ref[:1, part]
            acc_ref[group, lanes, :] = acc_ref[group, lanes, :] / total
            log_ref[0, :, part] = jnp.broadcast_to(top_ref[:1, part] + jnp.log(total), (8, rows))
        for group in range(groups):
            result = jnp.transpose(acc_ref[group])
            o_ref[0, group] = result
            low_ref[0, group] = result.astype(jnp.bfloat16)


def attn_fwd(place, q, k, v_turned):
    seqs, groups, rows, cols = q.shape
    count = k.shape[1] // rows
    heads = groups * cols // HD
    whole = pl.BlockSpec((1, groups, rows, cols), lambda s, j, p: (s, 0, 0, 0))
    return pl.pallas_call(
        attn_fwd_kernel,
        grid_spec=pltpu.PrefetchScalarGridSpec(
            num_scalar_prefetch=1,
            grid=(seqs, count),
            in_specs=[
                whole,
                pl.BlockSpec((1, rows, cols), lambda s, j, p: (s, jnp.minimum(j, p[0]), 0)),
                pl.BlockSpec((1, cols, rows), lambda s, j, p: (s, 0, jnp.minimum(j, p[0]))),
            ],
            out_specs=[whole, whole, pl.BlockSpec((1, 8, heads * rows), lambda s, j, p: (s, 0, 0))],
            scratch_shapes=[
                pltpu.VMEM((8, heads * rows), jnp.float32),
                pltpu.VMEM((8, heads * rows), jnp.float32),
                pltpu.VMEM((groups, cols, rows), jnp.float32),
            ],
        ),
        out_shape=[
            jax.ShapeDtypeStruct(q.shape, jnp.float32),
            jax.ShapeDtypeStruct(q.shape, jnp.bfloat16),
            jax.ShapeDtypeStruct((seqs, 8, heads * rows), jnp.float32),
        ],
        compiler_params=pltpu.CompilerParams(vmem_limit_bytes=VMEM_BYTES),
        name="attention_forward",
    )(place, q, k, v_turned)


def attn_bwd_kernel(scale, place_ref, q_ref, g_ref, o_ref, log_ref, k_ref, v_ref, dq_ref, dk_ref, dv_ref, inner_ref, acc_ref):
    step = pl.program_id(1)
    place = place_ref[0]
    groups, rows, cols = q_ref.shape[1:]
    pairs = [(group, head) for group in range(groups) for head in range(cols // HD)]

    @pl.when(step == 0)
    def _():
        acc_ref[...] = jnp.zeros(acc_ref.shape, jnp.float32)
        ones = jnp.ones((8, cols), jnp.float32)
        for number, (group, head) in enumerate(pairs):
            prod = only_head(g_ref[0, group].astype(jnp.float32) * o_ref[0, group], head)
            inner_ref[:, pl.ds(number * rows, rows)] = lax.dot_general(
                ones, prod, (((1,), (1,)), ((), ())), precision=PRECISE, preferred_element_type=jnp.float32
            )

    def one(masked):
        key_block = k_ref[0]
        value_block = v_ref[0]
        dk = jnp.zeros(dk_ref.shape[1:], jnp.float32)
        dv = jnp.zeros(dv_ref.shape[1:], jnp.float32)

        def ahead_of(number):
            group, head = pairs[number]
            q = only_head(q_ref[0, group], head)
            g = only_head(g_ref[0, group], head)
            return q, g, dot_t(key_block, q), dot_t(value_block, g)

        ahead = ahead_of(0)
        for number, (group, head) in enumerate(pairs):
            part = pl.ds(number * rows, rows)
            q, g, scores, back = ahead
            if number + 1 < len(pairs):
                ahead = ahead_of(number + 1)
            probs = jnp.exp(scores - log_ref[0, :1, part])
            if masked:
                row = lax.broadcasted_iota(jnp.int32, scores.shape, 0)
                col = lax.broadcasted_iota(jnp.int32, scores.shape, 1)
                probs = jnp.where(row <= col, probs, 0.0)
            grads = (probs * (back - inner_ref[:1, part])).astype(jnp.bfloat16)
            dv = dv + dot_n(probs.astype(jnp.bfloat16), g)
            dk = dk + dot_n(grads, q)
            acc_ref[group] = acc_ref[group] + dot_c(grads, only_head(key_block, head))
        dk_ref[0] = dk.astype(dk_ref.dtype)
        dv_ref[0] = dv.astype(dv_ref.dtype)

    @pl.when(step < place)
    def _():
        one(False)

    @pl.when(step == place)
    def _():
        one(True)
        dq_ref[0] = acc_ref[...] * scale

    @pl.when(step > place)
    def _():
        dk_ref[...] = jnp.zeros(dk_ref.shape, dk_ref.dtype)
        dv_ref[...] = jnp.zeros(dv_ref.shape, dv_ref.dtype)


def attn_bwd(scale, place, q, g, o, logs, k, v):
    seqs, groups, rows, cols = q.shape
    count = k.shape[1] // rows
    heads = groups * cols // HD
    whole = pl.BlockSpec((1, groups, rows, cols), lambda s, j, p: (s, 0, 0, 0))
    kv_spec = pl.BlockSpec((1, rows, cols), lambda s, j, p: (s, jnp.minimum(j, p[0]), 0))
    out_spec = pl.BlockSpec((1, rows, cols), lambda s, j, p: (s, j, 0))
    return pl.pallas_call(
        functools.partial(attn_bwd_kernel, scale),
        grid_spec=pltpu.PrefetchScalarGridSpec(
            num_scalar_prefetch=1,
            grid=(seqs, count),
            in_specs=[
                whole,
                whole,
                whole,
                pl.BlockSpec((1, 8, heads * rows), lambda s, j, p: (s, 0, 0)),
                kv_spec,
                kv_spec,
            ],
            out_specs=[whole, out_spec, out_spec],
            scratch_shapes=[
                pltpu.VMEM((8, heads * rows), jnp.float32),
                pltpu.VMEM((groups, rows, cols), jnp.float32),
            ],
        ),
        out_shape=[
            jax.ShapeDtypeStruct(q.shape, jnp.float32),
            jax.ShapeDtypeStruct(k.shape, jnp.bfloat16),
            jax.ShapeDtypeStruct(k.shape, jnp.bfloat16),
        ],
        compiler_params=pltpu.CompilerParams(vmem_limit_bytes=VMEM_BYTES),
        name="attention_backward",
    )(place, q, g, o, logs, k, v)


def expert_kernel(x_ref, u_ref, share_ref, gate_ref, up_ref, down_ref, out_ref, copy_ref, pick_ref, hid_ref, sig_ref):
    x = x_ref[...]
    u = u_ref[...]
    experts, width = gate_ref.shape[0], gate_ref.shape[2]
    out = jnp.zeros(out_ref.shape, jnp.float32)
    copy = jnp.zeros(copy_ref.shape, jnp.float32)
    share_columns = jnp.transpose(share_ref[0])
    lane = lax.broadcasted_iota(jnp.int32, (x.shape[0], 128), 1)
    picks = jnp.zeros((x.shape[0], 128), jnp.float32)
    for e in range(experts):
        gate = dot_n(x, gate_ref[e])
        up = dot_n(x, up_ref[e])
        back = dot_t(u, down_ref[e])
        share = share_columns[:, e : e + 1]
        sig = 1.0 / (1.0 + jnp.exp(-gate))
        act = gate * sig
        hidden = act * up
        picks = jnp.where(lane == e, jnp.sum(hidden * back, axis=1, keepdims=True), picks)
        hidden_low = (hidden * share).astype(jnp.bfloat16)
        back = back * share
        gate_signal = (back * up * (sig * (1.0 + gate * (1.0 - sig)))).astype(jnp.bfloat16)
        up_signal = (back * act).astype(jnp.bfloat16)
        hid_ref[:, e * width : (e + 1) * width] = hidden_low
        sig_ref[:, (2 * e) * width : (2 * e + 1) * width] = gate_signal
        sig_ref[:, (2 * e + 1) * width : (2 * e + 2) * width] = up_signal
        out = out + dot_n(hidden_low, down_ref[e])
        copy = copy + dot_t(gate_signal, gate_ref[e]) + dot_t(up_signal, up_ref[e])
    out_ref[...] = out.astype(out_ref.dtype)
    copy_ref[...] = copy.astype(copy_ref.dtype)
    pick_ref[0] = jnp.transpose(picks)[: pick_ref.shape[1]]


def experts_both(x, u, shares, gate, up, down):
    tokens, model = x.shape
    tile = shares.shape[2]
    experts, _, width = gate.shape
    def rows(cols): return pl.BlockSpec((tile, cols), lambda t: (t, 0))
    def fixed(a): return pl.BlockSpec(a.shape, lambda t: (0,) * a.ndim, pipeline_mode=pl.Buffered(1))
    small = pl.BlockSpec((1,) + shares.shape[1:], lambda t: (t, 0, 0))
    return pl.pallas_call(
        expert_kernel,
        grid=(tokens // tile,),
        in_specs=[rows(model), rows(model), small, fixed(gate), fixed(up), fixed(down)],
        out_specs=[rows(model), rows(model), small, rows(experts * width), rows(2 * experts * width)],
        out_shape=[
            jax.ShapeDtypeStruct((tokens, model), jnp.bfloat16),
            jax.ShapeDtypeStruct((tokens, model), jnp.bfloat16),
            jax.ShapeDtypeStruct(shares.shape, jnp.float32),
            jax.ShapeDtypeStruct((tokens, experts * width), jnp.bfloat16),
            jax.ShapeDtypeStruct((tokens, 2 * experts * width), jnp.bfloat16),
        ],
        compiler_params=pltpu.CompilerParams(vmem_limit_bytes=VMEM_BYTES),
        name="experts_both",
    )(x, u, shares, gate, up, down)


def turned_kernel(left_ref, right_ref, out_ref):
    out_ref[...] = dot_c(left_ref[...], right_ref[...]).astype(out_ref.dtype)


def turned_product(left, right, rows):
    return pl.pallas_call(
        turned_kernel,
        grid=(left.shape[1] // rows,),
        in_specs=[
            pl.BlockSpec((left.shape[0], rows), lambda i: (0, i)),
            pl.BlockSpec(right.shape, lambda i: (0, 0), pipeline_mode=pl.Buffered(1)),
        ],
        out_specs=pl.BlockSpec((rows, right.shape[1]), lambda i: (i, 0)),
        out_shape=jax.ShapeDtypeStruct((left.shape[1], right.shape[1]), jnp.bfloat16),
        compiler_params=pltpu.CompilerParams(vmem_limit_bytes=VMEM_BYTES),
        name="turned_product",
    )(left, right)


MESH = pl.DeviceIdType.MESH


def greet(targets):
    barrier = pltpu.get_barrier_semaphore()
    awaited = 0
    for target, there in targets:
        if there is None:
            pl.semaphore_signal(barrier, inc=1, device_id=target, device_id_type=MESH)
            awaited = awaited + 1
        else:

            @pl.when(there)
            def _():
                pl.semaphore_signal(barrier, inc=1, device_id=target, device_id_type=MESH)

            awaited = awaited + jnp.where(there, 1, 0)
    pl.semaphore_wait(barrier, awaited)


def copier(source, target, sends, receives, number, device):
    return pltpu.make_async_remote_copy(
        src_ref=source,
        dst_ref=target,
        send_sem=sends.at[number],
        recv_sem=receives.at[number],
        device_id=device,
        device_id_type=MESH,
    )


def square_gather_kernel(x_ref, o_ref, local_sem, sends, receives):
    narrow, wide = lax.axis_index("narrow"), lax.axis_index("wide")
    rows = x_ref.shape[1]
    beside, across = jnp.bitwise_xor(narrow, 1), jnp.bitwise_xor(narrow, 2)
    corner = jnp.bitwise_xor(narrow, 3)
    to_beside, to_across = (beside, wide), (across, wide)
    greet([(to_beside, None), (to_across, None)])

    def place(half, owner):
        return o_ref.at[half, pl.ds(owner * rows, rows)]

    own = pltpu.make_async_copy(x_ref, o_ref.at[:, pl.ds(narrow * rows, rows)], local_sem)
    first = copier(x_ref.at[0], place(0, narrow), sends, receives, 0, to_beside)
    second = copier(x_ref.at[1], place(1, narrow), sends, receives, 1, to_across)
    third = copier(x_ref.at[1], place(1, narrow), sends, receives, 2, to_beside)
    fourth = copier(x_ref.at[0], place(0, narrow), sends, receives, 3, to_across)
    for copy in (first, second, third, fourth):
        copy.start()
    own.start()
    copier(x_ref.at[0], place(0, beside), sends, receives, 0, to_beside).wait_recv()
    fifth = copier(place(0, beside), place(0, beside), sends, receives, 4, to_across)
    fifth.start()
    copier(x_ref.at[1], place(1, across), sends, receives, 1, to_across).wait_recv()
    sixth = copier(place(1, across), place(1, across), sends, receives, 5, to_beside)
    sixth.start()
    copier(x_ref.at[1], place(1, beside), sends, receives, 2, to_beside).wait_recv()
    copier(x_ref.at[0], place(0, across), sends, receives, 3, to_across).wait_recv()
    copier(x_ref.at[0], place(0, corner), sends, receives, 4, to_across).wait_recv()
    copier(x_ref.at[1], place(1, corner), sends, receives, 5, to_beside).wait_recv()
    for copy in (first, second, third, fourth, fifth, sixth):
        copy.wait_send()
    own.wait()


def gather_narrow(block, number):
    count = lax.axis_size("narrow")
    if count != 4 or block.shape[0] != 2:
        return lax.all_gather(block, "narrow", axis=1, tiled=True)
    return pl.pallas_call(
        square_gather_kernel,
        out_shape=jax.ShapeDtypeStruct(
            (block.shape[0], count * block.shape[1], block.shape[2]), block.dtype
        ),
        in_specs=[pl.BlockSpec(memory_space=pl.ANY)],
        out_specs=pl.BlockSpec(memory_space=pl.ANY),
        scratch_shapes=[
            pltpu.SemaphoreType.DMA,
            pltpu.SemaphoreType.DMA((6,)),
            pltpu.SemaphoreType.DMA((6,)),
        ],
        compiler_params=pltpu.CompilerParams(collective_id=number, has_side_effects=True),
        name="square_gather",
    )(block)


def square_scatter_kernel(p_ref, o_ref, part_ref, sum_ref, in_ref, sends, receives):
    narrow, wide = lax.axis_index("narrow"), lax.axis_index("wide")
    rows = o_ref.shape[1]
    beside, across = jnp.bitwise_xor(narrow, 1), jnp.bitwise_xor(narrow, 2)
    corner = jnp.bitwise_xor(narrow, 3)
    to_beside, to_across = (beside, wide), (across, wide)
    greet([(to_beside, None), (to_across, None)])

    def mine(half, owner):
        return p_ref.at[half, pl.ds(owner * rows, rows)]

    first = copier(mine(0, corner), part_ref.at[0], sends, receives, 0, to_beside)
    second = copier(mine(1, corner), part_ref.at[1], sends, receives, 1, to_across)
    third = copier(mine(0, beside), in_ref.at[0, 0], sends, receives, 2, to_beside)
    fourth = copier(mine(1, across), in_ref.at[1, 1], sends, receives, 3, to_across)
    for copy in (first, second, third, fourth):
        copy.start()
    first.wait_recv()
    sum_ref[0] = (
        part_ref[0].astype(jnp.float32) + mine(0, across)[...].astype(jnp.float32)
    ).astype(sum_ref.dtype)
    fifth = copier(sum_ref.at[0], in_ref.at[1, 0], sends, receives, 4, to_across)
    fifth.start()
    second.wait_recv()
    sum_ref[1] = (
        part_ref[1].astype(jnp.float32) + mine(1, beside)[...].astype(jnp.float32)
    ).astype(sum_ref.dtype)
    sixth = copier(sum_ref.at[1], in_ref.at[0, 1], sends, receives, 5, to_beside)
    sixth.start()
    third.wait_recv()
    fifth.wait_recv()
    o_ref[0] = (
        mine(0, narrow)[...].astype(jnp.float32)
        + in_ref[0, 0].astype(jnp.float32)
        + in_ref[1, 0].astype(jnp.float32)
    )
    fourth.wait_recv()
    sixth.wait_recv()
    o_ref[1] = (
        mine(1, narrow)[...].astype(jnp.float32)
        + in_ref[0, 1].astype(jnp.float32)
        + in_ref[1, 1].astype(jnp.float32)
    )
    for copy in (first, second, third, fourth, fifth, sixth):
        copy.wait_send()


def scatter_narrow(partial, number):
    count = lax.axis_size("narrow")
    seqs, rows, cols = partial.shape
    if count != 4 or seqs != 2:
        return lax.psum_scatter(partial, "narrow", scatter_dimension=1, tiled=True).astype(
            jnp.float32
        )
    return pl.pallas_call(
        square_scatter_kernel,
        out_shape=jax.ShapeDtypeStruct((seqs, rows // count, cols), jnp.float32),
        in_specs=[pl.BlockSpec(memory_space=pltpu.VMEM)],
        out_specs=pl.BlockSpec(memory_space=pltpu.VMEM),
        scratch_shapes=[
            pltpu.VMEM((2, rows // count, cols), partial.dtype),
            pltpu.VMEM((2, rows // count, cols), partial.dtype),
            pltpu.VMEM((2, 2, rows // count, cols), partial.dtype),
            pltpu.SemaphoreType.DMA((6,)),
            pltpu.SemaphoreType.DMA((6,)),
        ],
        compiler_params=pltpu.CompilerParams(
            collective_id=number, has_side_effects=True, vmem_limit_bytes=VMEM_BYTES
        ),
        name="square_scatter",
    )(partial)


def line_places():
    narrow, wide = lax.axis_index("narrow"), lax.axis_index("wide")
    chips = lax.axis_size("wide") // 2
    chip, core = wide // 2, lax.rem(wide, 2)
    sibling = (narrow, wide + 1 - 2 * core)
    above = (narrow, jnp.minimum(wide + 2, 2 * chips - 2 + core))
    below = (narrow, jnp.maximum(wide - 2, core))
    return chips, chip, core, sibling, above, below


def line_gather_kernel(axes, falling, *refs):
    count = len(axes)
    x_refs, o_refs = refs[:count], refs[count : 2 * count]
    local_sem, core_s, core_r, up_s, up_r, down_s, down_r = refs[2 * count :]
    chips, chip, core, sibling, above, below = line_places()
    has_above, has_below = chip < chips - 1, chip > 0
    greet([(sibling, None), (above, has_above), (below, has_below)])

    def place(item, owner_chip, owner_core):
        axis = axes[item]
        size = x_refs[item].shape[axis]
        at = (owner_chip * 2 + owner_core) * size
        return o_refs[item].at[(slice(None),) * axis + (pl.ds(at, size),)]

    def send(item, source, owner_chip, sems, number, device):
        return copier(source, place(item, owner_chip, core), sems[0].at[item], sems[1].at[item], number, device)

    def arrival(item, owner_chip, owner_core, sems, number):
        spot = place(item, owner_chip, owner_core)
        return copier(spot, spot, sems[0].at[item], sems[1].at[item], number, sibling)

    ups, downs, cores = (up_s, up_r), (down_s, down_r), (core_s, core_r)
    for item in range(count):
        x_ref = x_refs[item]

        @pl.when(has_above)
        def _():
            send(item, x_ref, chip, ups, 1, above).start()

        if falling:

            @pl.when(has_below)
            def _():
                send(item, x_ref, chip, downs, 1, below).start()

        send(item, x_ref, chip, cores, 0, sibling).start()
        pltpu.make_async_copy(x_ref, place(item, chip, core), local_sem.at[item]).start()
    for step in range(1, chips):
        for item in range(count):

            @pl.when(chip >= step)
            def _():
                came = chip - step
                arrival(item, came, core, ups, step).wait_recv()
                spot = place(item, came, core)

                @pl.when(has_above)
                def _():
                    send(item, spot, came, ups, step + 1, above).start()

                send(item, spot, came, cores, step, sibling).start()

            if falling:

                @pl.when(chip + step < chips)
                def _():
                    came = chip + step
                    arrival(item, came, core, downs, step).wait_recv()
                    spot = place(item, came, core)

                    @pl.when(has_below)
                    def _():
                        send(item, spot, came, downs, step + 1, below).start()

                    send(item, spot, came, cores, chips - 1 + step, sibling).start()

    for item in range(count):
        for step in range(chips):

            @pl.when(chip >= step)
            def _():
                came = chip - step
                arrival(item, came, 1 - core, cores, step).wait_recv()
                arrival(item, came, core, cores, step).wait_send()

                @pl.when(has_above)
                def _():
                    arrival(item, came, core, ups, step + 1).wait_send()

            if falling:

                @pl.when(chip + step < chips)
                def _():
                    came = chip + step
                    if step:
                        arrival(item, came, 1 - core, cores, chips - 1 + step).wait_recv()
                        arrival(item, came, core, cores, chips - 1 + step).wait_send()

                    @pl.when(has_below)
                    def _():
                        arrival(item, came, core, downs, step + 1).wait_send()

        pltpu.make_async_copy(x_refs[item], place(item, chip, core), local_sem.at[item]).wait()


def gather_wide(blocks, axes, falling, number):
    wide_count = lax.axis_size("wide")
    chips = wide_count // 2
    count = len(blocks)

    def grown(block, axis):
        shape = list(block.shape)
        shape[axis] *= wide_count
        return jax.ShapeDtypeStruct(tuple(shape), block.dtype)

    sems = [pltpu.SemaphoreType.DMA((count, 2 * chips))] * 2
    sems += [pltpu.SemaphoreType.DMA((count, chips + 1))] * 4
    return pl.pallas_call(
        functools.partial(line_gather_kernel, axes, falling),
        out_shape=[grown(block, axis) for block, axis in zip(blocks, axes)],
        in_specs=[pl.BlockSpec(memory_space=pl.ANY)] * count,
        out_specs=[pl.BlockSpec(memory_space=pl.ANY)] * count,
        scratch_shapes=[pltpu.SemaphoreType.DMA((count,))] + sems,
        compiler_params=pltpu.CompilerParams(collective_id=number, has_side_effects=True),
        name="line_gather",
    )(*blocks)


def line_scatter_kernel(rising, count, *refs):
    p_refs, o_refs = refs[:count], refs[count : 2 * count]
    core_in = refs[2 * count : 3 * count]
    up_in, down_in = refs[3 * count : 4 * count], refs[4 * count : 5 * count]
    up_out, down_out = refs[5 * count : 6 * count], refs[6 * count : 7 * count]
    core_s, core_r, up_s, up_r, down_s, down_r = refs[7 * count :]
    chips, chip, core, sibling, above, below = line_places()
    has_above, has_below = chip < chips - 1, chip > 0
    greet([(sibling, None), (above, has_above), (below, has_below)])
    order = [step for step in range(chips - 1, -1, -1)]

    def core_copy(item, distance, target):
        return copier(
            p_refs[item].at[target * 2 + 1 - core],
            core_in[item].at[chips - 1 + distance],
            core_s.at[item],
            core_r.at[item],
            chips - 1 + distance,
            sibling,
        )

    def both_ways(action):
        for step in order:

            @pl.when(chip >= step)
            def _():
                action(-step, chip - step)

            if rising and step:

                @pl.when(chip + step < chips)
                def _():
                    action(step, chip + step)

    def start_core(distance, target):
        for item in range(count):
            core_copy(item, distance, target).start()

    both_ways(start_core)

    def own_sum(item, distance, target):
        core_copy(item, distance, target).wait_recv()
        return p_refs[item][target * 2 + core].astype(jnp.float32) + core_in[item][
            chips - 1 + distance
        ].astype(jnp.float32)

    def up_copy(item, distance):
        return copier(
            up_out[item].at[distance],
            up_in[item].at[distance - 1],
            up_s.at[item],
            up_r.at[item],
            distance - 1,
            above,
        )

    def down_copy(item, distance):
        return copier(
            down_out[item].at[distance],
            down_in[item].at[distance - 1],
            down_s.at[item],
            down_r.at[item],
            distance - 1,
            below,
        )

    def pass_on(distance, target):
        for item in range(count):
            total = own_sum(item, distance, target)
            if distance > 0:
                out, copy_of, arrived, more = up_out[item], up_copy, up_in[item], has_below
            else:
                out, copy_of, arrived, more = down_out[item], down_copy, down_in[item], has_above
            size = abs(distance)
            if size + 1 < chips:

                @pl.when(more)
                def _():
                    copy_of(item, size + 1).wait_recv()
                    out[size] = (total + arrived[size].astype(jnp.float32)).astype(out.dtype)

                @pl.when(jnp.logical_not(more))
                def _():
                    out[size] = total.astype(out.dtype)

            else:
                out[size] = total.astype(out.dtype)
            copy_of(item, size).start()

    for step in order[:-1]:

        @pl.when(chip >= step)
        def _():
            pass_on(-step, chip - step)

        if rising:

            @pl.when(chip + step < chips)
            def _():
                pass_on(step, chip + step)

    for item in range(count):
        o_refs[item][...] = own_sum(item, 0, chip)

        @pl.when(has_above)
        def _():
            down_copy(item, 1).wait_recv()
            o_refs[item][...] += down_in[item][0].astype(jnp.float32)

        if rising:

            @pl.when(has_below)
            def _():
                up_copy(item, 1).wait_recv()
                o_refs[item][...] += up_in[item][0].astype(jnp.float32)

    def finish(distance, target):
        for item in range(count):
            core_copy(item, distance, target).wait_send()
            if distance > 0:
                up_copy(item, distance).wait_send()
            if distance < 0:
                down_copy(item, -distance).wait_send()

    both_ways(finish)


def scatter_wide(partials, rising, number):
    chips = lax.axis_size("wide") // 2
    count = len(partials)

    def several(size):
        return [pltpu.VMEM((size,) + partial.shape[1:], partial.dtype) for partial in partials]

    sems = [pltpu.SemaphoreType.DMA((count, 2 * chips))] * 2
    sems += [pltpu.SemaphoreType.DMA((count, chips + 1))] * 4
    buffers = several(2 * chips - 1) + several(chips) * 2 + several(chips) * 2
    return pl.pallas_call(
        functools.partial(line_scatter_kernel, rising, count),
        out_shape=[jax.ShapeDtypeStruct(partial.shape[1:], jnp.float32) for partial in partials],
        in_specs=[pl.BlockSpec(memory_space=pltpu.VMEM)] * count,
        out_specs=[pl.BlockSpec(memory_space=pltpu.VMEM)] * count,
        scratch_shapes=buffers + sems,
        compiler_params=pltpu.CompilerParams(
            collective_id=number, has_side_effects=True, vmem_limit_bytes=VMEM_BYTES
        ),
        name="line_scatter",
    )(*partials)


def small_sum_kernel(steps, x_ref, o_ref, in_ref, out_ref, sends, receives):
    narrow, wide = lax.axis_index("narrow"), lax.axis_index("wide")
    partners = [
        (jnp.bitwise_xor(narrow, bit), wide) if axis else (narrow, jnp.bitwise_xor(wide, bit))
        for axis, bit in steps
    ]
    greet([(partner, None) for partner in partners])
    o_ref[...] = x_ref[...]
    for step, partner in enumerate(partners):
        out_ref[step] = o_ref[...]
        copy = copier(out_ref.at[step], in_ref.at[step], sends, receives, step, partner)
        copy.start()
        copy.wait_recv()
        o_ref[...] += in_ref[step]
    for step, partner in enumerate(partners):
        copier(out_ref.at[step], in_ref.at[step], sends, receives, step, partner).wait_send()


def small_sum(values, number):
    counts = (lax.axis_size("wide"), lax.axis_size("narrow"))
    steps = [
        (axis, 1 << bit) for axis in (1, 0) for bit in range(counts[axis].bit_length() - 1)
    ]
    return pl.pallas_call(
        functools.partial(small_sum_kernel, steps),
        out_shape=jax.ShapeDtypeStruct(values.shape, values.dtype),
        in_specs=[pl.BlockSpec(memory_space=pltpu.VMEM)],
        out_specs=pl.BlockSpec(memory_space=pltpu.VMEM),
        scratch_shapes=[
            pltpu.VMEM((len(steps),) + values.shape, values.dtype),
            pltpu.VMEM((len(steps),) + values.shape, values.dtype),
            pltpu.SemaphoreType.DMA((len(steps),)),
            pltpu.SemaphoreType.DMA((len(steps),)),
        ],
        compiler_params=pltpu.CompilerParams(
            collective_id=number, has_side_effects=True, vmem_limit_bytes=VMEM_BYTES
        ),
        name="small_sum",
    )(values)


def angles_of(positions, factor):
    half_size = HD // 2
    frequency = ROPE_BASE ** (-jnp.arange(half_size, dtype=jnp.float32) * 2.0 / HD)
    angles = (positions.astype(jnp.float32) / factor)[:, None] * frequency[None, :]
    return jnp.cos(angles), jnp.sin(angles)


def rotate(tensor, cosine, sine):
    half_size = tensor.shape[-1] // 2
    leading = tensor[..., :half_size]
    trailing = tensor[..., half_size:]
    return jnp.concatenate(
        [leading * cosine - trailing * sine, trailing * cosine + leading * sine], axis=-1
    )


def inverse_of(inputs):
    return lax.rsqrt(jnp.mean(inputs * inputs, axis=-1, keepdims=True) + EPSILON)


def normalize_back(inputs, inverse, gain_vector, upstream):
    scaled = inputs * inverse
    through = upstream * gain_vector
    input_grad = inverse * (through - scaled * jnp.mean(through * scaled, axis=-1, keepdims=True))
    gain_grad = jnp.sum(upstream * scaled, axis=(0, 1))
    return (input_grad, gain_grad)


def on_device(
    tokens,
    gain_attn,
    w_query,
    w_key,
    w_value,
    w_out,
    gain_moe,
    w_router,
    w_gate,
    w_up,
    w_down,
    routes,
    rope_scale,
    cotangent,
):
    narrow_count = lax.axis_size("narrow")
    wide_count = lax.axis_size("wide")
    wide_place = lax.axis_index("wide")
    local_rows, sequences, model_width = tokens.shape
    block_rows = local_rows * narrow_count
    query_cols = w_query.shape[1]
    kv_cols = w_key.shape[1]
    kv_heads = kv_cols // HD
    heads = query_cols // HD
    group_size = heads // kv_heads
    score_scale = HD ** (-0.5)
    factor = rope_scale[0]
    place = wide_place.astype(jnp.int32).reshape(1)
    token_count = local_rows * sequences

    token_float = tokens.swapaxes(0, 1).astype(jnp.float32)
    upstream_low = cotangent.swapaxes(0, 1)
    upstream = upstream_low.astype(jnp.float32)
    upstream_all = lax.all_gather(
        upstream_low.reshape(token_count, model_width), "wide", axis=0, tiled=True
    )

    attn_inverse = inverse_of(token_float)
    attn_low = (token_float * attn_inverse * gain_attn).astype(jnp.bfloat16)
    attn_block = gather_narrow(attn_low, 0)
    query_weight = w_query.reshape(model_width, kv_heads, group_size, HD).swapaxes(1, 2)
    joint_weight = jnp.concatenate(
        [query_weight.reshape(model_width, query_cols), w_key, w_value], axis=1
    )
    out_weight = w_out.reshape(kv_heads, group_size, HD, model_width).swapaxes(0, 1)
    out_weight = out_weight.reshape(query_cols, model_width)
    joint_proj = jnp.einsum(
        "std,dc->stc", attn_block, joint_weight, preferred_element_type=jnp.float32
    )
    cosine, sine = angles_of(wide_place * block_rows + lax.iota(jnp.int32, block_rows), factor)
    head_cosine, head_sine = cosine[None, :, None, :], sine[None, :, None, :]

    def by_group(flat):
        return flat.reshape(sequences, block_rows, group_size, kv_cols).swapaxes(1, 2)

    def flat_of(groups):
        return groups.swapaxes(1, 2).reshape(sequences, block_rows, query_cols)

    query_rot = rotate(
        joint_proj[..., :query_cols].reshape(sequences, block_rows, heads, HD),
        head_cosine,
        head_sine,
    ).astype(jnp.bfloat16)
    query_group = by_group(
        (query_rot * jnp.bfloat16(score_scale)).reshape(sequences, block_rows, query_cols)
    )
    key_rot = rotate(
        joint_proj[..., query_cols : query_cols + kv_cols].reshape(
            sequences, block_rows, kv_heads, HD
        ),
        head_cosine,
        head_sine,
    )
    key_local = key_rot.astype(jnp.bfloat16).reshape(sequences, block_rows, kv_cols)
    value_local = joint_proj[..., query_cols + kv_cols :].astype(jnp.bfloat16)
    (pair_all,) = gather_wide([jnp.stack([key_local, value_local])], (2,), False, 1)
    key_all, value_all = pair_all[0], pair_all[1]

    attn_result, attended, log_total = attn_fwd(
        place, query_group, key_all, value_all.swapaxes(1, 2)
    )
    out_low = flat_of(attended)
    attn_branch = scatter_narrow(
        jnp.einsum("stc,cd->std", out_low, out_weight, preferred_element_type=jnp.float32).astype(
            jnp.bfloat16
        ),
        2,
    )
    residual = token_float + attn_branch
    moe_inverse = inverse_of(residual)
    moe_low = (residual * moe_inverse * gain_moe).astype(jnp.bfloat16)
    moe_flat = moe_low.reshape(token_count, model_width)

    expert_count = w_router.shape[1]
    local_experts = w_gate.shape[0]
    first_expert = wide_place * local_experts
    expert_ids = routes.swapaxes(0, 1).reshape(token_count, -1)
    onehot = expert_ids[:, :, None] == lax.iota(jnp.int32, expert_count)[None, None, :]
    named = jnp.sum(onehot.astype(jnp.float32), axis=1)
    logits = jnp.dot(moe_flat, w_router, preferred_element_type=jnp.float32)
    masked = jnp.where(named > 0, logits, MASKED)
    powers = jnp.exp(masked - jnp.max(masked, axis=-1, keepdims=True)) * named
    shares = powers / jnp.sum(powers, axis=-1, keepdims=True)

    moe_all, shares_all = gather_wide([moe_flat, shares.T[None]], (0, 0), True, 3)
    own_shares = lax.dynamic_slice_in_dim(shares_all, first_expert, local_experts, 1)
    own_shares = jnp.pad(own_shares, ((0, 0), (0, 8 - local_experts), (0, 0)))
    part_out, part_copy, own_picks, hidden_shared, signals = experts_both(
        moe_all, upstream_all, own_shares, w_gate, w_up, w_down
    )
    part_picks = lax.dynamic_update_slice_in_dim(
        jnp.zeros_like(shares_all), own_picks[:, :local_experts], first_expert, 1
    )

    def by_block(rows):
        return rows.reshape((wide_count, rows.shape[0] // wide_count) + rows.shape[1:])

    copy_sum, picks = scatter_wide([by_block(part_copy), part_picks], True, 4)
    (moe_part,) = scatter_wide([by_block(part_out)], True, 5)
    layer_out = (residual + moe_part.reshape(residual.shape)).astype(jnp.bfloat16)

    joint_signal = turned_product(moe_all, signals, block_rows // 2)
    down_update = turned_product(hidden_shared, upstream_all, block_rows // 2)
    width = w_gate.shape[2]
    split = joint_signal.reshape(model_width, local_experts, 2, width)
    expert_grads = tuple(
        lax.psum_scatter(update, "narrow", scatter_dimension=1, tiled=True).astype(jnp.float32)
        for update in (
            split[:, :, 0].swapaxes(0, 1),
            split[:, :, 1].swapaxes(0, 1),
            down_update.reshape(local_experts, width, model_width),
        )
    )

    picks = picks.T
    logit_grads = shares * (picks - jnp.sum(shares * picks, axis=-1, keepdims=True))
    router_grads = jnp.dot(logit_grads.T, moe_flat.astype(jnp.float32), precision=PRECISE)
    moe_grads = jnp.dot(logit_grads, w_router.astype(jnp.float32).T, precision=PRECISE)
    moe_grads = moe_grads + copy_sum
    norm_grads, moe_gain = normalize_back(
        residual, moe_inverse, gain_moe, moe_grads.reshape(residual.shape)
    )
    residual_grads = upstream + norm_grads
    branch_all = gather_narrow(residual_grads.astype(jnp.bfloat16), 6)
    attended_grads = jnp.einsum(
        "std,cd->stc", branch_all, out_weight, preferred_element_type=jnp.float32
    ).astype(jnp.bfloat16)
    query_grads, key_part, value_part = attn_bwd(
        score_scale,
        place,
        query_group,
        by_group(attended_grads),
        attn_result,
        log_total,
        key_all,
        value_all,
    )
    out_update = jnp.einsum("stc,std->cd", out_low, branch_all, preferred_element_type=jnp.float32)
    pair_parts = jnp.stack([key_part, value_part]).reshape(
        2, sequences, wide_count, block_rows, kv_cols
    )
    (pair_own,) = scatter_wide([pair_parts.transpose(2, 0, 1, 3, 4)], False, 7)
    query_low = rotate(
        flat_of(query_grads).reshape(sequences, block_rows, heads, HD), head_cosine, -head_sine
    ).astype(jnp.bfloat16)
    key_low = rotate(
        pair_own[0].reshape(sequences, block_rows, kv_heads, HD),
        head_cosine,
        -head_sine,
    ).astype(jnp.bfloat16)
    joint_grads = jnp.concatenate(
        [
            query_low.reshape(sequences, block_rows, query_cols),
            key_low.reshape(sequences, block_rows, kv_cols),
            pair_own[1].astype(jnp.bfloat16),
        ],
        axis=-1,
    )
    joint_update = jnp.einsum(
        "std,stc->dc", attn_block, joint_grads, preferred_element_type=jnp.float32
    )
    attn_grads = scatter_narrow(
        jnp.einsum(
            "stc,dc->std", joint_grads, joint_weight, preferred_element_type=jnp.float32
        ).astype(jnp.bfloat16),
        8,
    )
    token_grads, attn_gain = normalize_back(token_float, attn_inverse, gain_attn, attn_grads)
    token_grads = residual_grads + token_grads
    weight_updates = jnp.concatenate([joint_update, out_update.T], axis=1).astype(jnp.bfloat16)
    (joint_summed,) = scatter_wide([by_block(weight_updates)], True, 9)
    out_summed = joint_summed[:, query_cols + 2 * kv_cols :]
    small_parts = jnp.concatenate([router_grads, moe_gain[None, :], attn_gain[None, :]], axis=0)
    small_parts = jnp.pad(small_parts, ((0, -small_parts.shape[0] % 8), (0, 0)))
    small_summed = small_sum(small_parts, 10)
    return (
        layer_out.swapaxes(0, 1),
        token_grads.swapaxes(0, 1),
        small_summed[expert_count + 1],
        joint_summed[:, :query_cols]
        .reshape(-1, group_size, kv_heads, HD)
        .swapaxes(1, 2)
        .reshape(-1, query_cols),
        joint_summed[:, query_cols : query_cols + kv_cols],
        joint_summed[:, query_cols + kv_cols : query_cols + 2 * kv_cols],
        out_summed.T.reshape(group_size, kv_heads, HD, -1).swapaxes(0, 1).reshape(query_cols, -1),
        small_summed[expert_count],
        small_summed[:expert_count].T,
        expert_grads[0],
        expert_grads[1],
        expert_grads[2],
    )


def solution(mesh):
    return jax.shard_map(
        on_device,
        mesh=mesh,
        in_specs=(
            P(("wide", "narrow"), None, None),
            P(),
            P(None, "narrow"),
            P(None, "narrow"),
            P(None, "narrow"),
            P("narrow", None),
            P(),
            P(),
            P("wide", None, None),
            P("wide", None, None),
            P("wide", None, None),
            P(("wide", "narrow"), None, None),
            P(),
            P(("wide", "narrow"), None, None),
        ),
        out_specs=(
            P(("wide", "narrow"), None, None),
            P(("wide", "narrow"), None, None),
            P(),
            P("wide", "narrow"),
            P("wide", "narrow"),
            P("wide", "narrow"),
            P("narrow", "wide"),
            P(),
            P(),
            P("wide", "narrow", None),
            P("wide", "narrow", None),
            P("wide", "narrow", None),
        ),
        check_vma=False,
    )
```

time: 1160 us -> 628 us (0.54)
  waiting for transfers between devices: 867 us -> 0.07 us
  Pallas kernels: 0 us -> 496 us
  matrix products: 125 us -> 16.7 us
  blocking collectives: 53.7 us -> 0 us
  other arithmetic: 43.3 us -> 24.9 us
  local copies, waits for them, and re-layouts: 47.9 us -> 65.9 us
    reduce_scatter x11 -> x3, waiting for transfers between devices: 555 us -> 0.01 us  [on_device(): lax.psum_scatter(update, 'narrow', scatter_dimension=1, tiled=True)]
    pallas_call x0 -> x16, Pallas kernels: none -> 496 us  [the longest x4 190 us: scatter_wide(): pl.pallas_call(functools.partial(line_scatter_kernel, rising, count), out...]
    all_gather x5 -> x1, waiting for transfers between devices: 188 us -> 0.01 us  [on_device(): lax.all_gather(upstream_low.reshape(token_count, model_width), 'wide', ax...]
    psum x1 -> x0, waiting for transfers between devices: 123 us -> none  [on_device(): lax.psum(jnp.concatenate([moe_gain[:, None], router_grads], axis=1), ('na...]
    dot_general x23 -> x7, matrix products: 121 us -> 14.6 us  [the longest x1 4.03 us: on_device(): jnp.einsum('stc,dc->std', joint_grads, joint_weight, preferred_element_ty...]
    psum x1 -> x0, blocking collectives: 39.3 us -> none  [on_device(): lax.psum(attn_gain, ('narrow', 'wide'))]
    convert_element_type x7 -> x6, other arithmetic: 23.2 us -> 8.64 us  [the longest x3 6.41 us: on_device(): lax.psum_scatter(update, 'narrow', scatter_dimension=1, tiled=True)]
    all_gather x1 -> x0, blocking collectives: 14.4 us -> none  [on_device(): shares_all = lax.all_gather(shares, 'wide', axis=0, tiled=True)]
  transfers between devices with their start and end apart: 17 -> 4, of which waited for: 17 -> 0; matrix products, arithmetic and copies ran while one was open for 8% -> 16% of each run, Pallas kernels for 0% -> 73%
where the time goes in v2:
time: 628 us; the launch traced here: 619 us
  Pallas kernels  496 us (79%)
  local copies, waits for them, and re-layouts  65.9 us (10%)
  other arithmetic  24.9 us (4%)
  matrix products  16.7 us (3%)
  between operations  15.5 us (2%)
    pallas_call x4, Pallas kernels, scatter_wide(): pl.pallas_call(functools.partial(line_scatter_kernel, rising, count), out...  190 us
    pallas_call x2, Pallas kernels, gather_wide(): pl.pallas_call(functools.partial(line_gather_kernel, axes, falling), out_...  116 us
    pallas_call x2, Pallas kernels, scatter_narrow(): pl.pallas_call(square_scatter_kernel, out_shape=jax.ShapeDtypeStruct((seq...  46 us
    pallas_call x2, Pallas kernels, gather_narrow(): pl.pallas_call(square_gather_kernel, out_shape=jax.ShapeDtypeStruct((bloc...  41.6 us
    pallas_call x1, Pallas kernels, experts_both(): pl.pallas_call(expert_kernel, grid=(tokens // tile,), in_specs=[rows(mode...  34.3 us
    pallas_call x2, Pallas kernels, turned_product(): pl.pallas_call(turned_kernel, grid=(left.shape[1] // rows,), in_specs=[pl...  22.9 us
    pallas_call x1, Pallas kernels, small_sum(): pl.pallas_call(functools.partial(small_sum_kernel, steps), out_shape=jax....  21.4 us
    unnamed x72, local copies, waits for them, and re-layouts  17.5 us
  transfers between devices with their start and end apart: 4, of which 0 were waited for; matrix products, arithmetic and copies ran while one was open for 16% of the time, Pallas kernels for 73%

profile of v2, /device:TPU:0, one launch (start us, length us, event | category | flops | bytes accessed | tf_op | source)
XLA Modules:
  0.0 619.2 jit_solution(3547858505066456335)
XLA Ops:
  7.3 2.0 copy.128
  9.4 1.1 copy.119
  11.2 1.0 fusion.13.x_ref
  12.2 22.2 %square_gather.2 = bf16[2,512,1024]{2,1,0:T(8,128)(2,1)} custom-call(bf16[2,128,1024]{2,1,0:T(8,128)(2,1)} %fusion.13.x_ref), custom_call_target="tpu_custom_call" | custom-call | tf_op jit(solution)/shard_map/square_gather/pallas_call | solution.py:375
  34.4 2.9 fusion.21
  38.1 1.1 copy.126
  39.4 0.9 fusion.25
  41.1 1.0 copy.121
  42.4 0.8 pad_maximum_fusion.3.refs_0_
  43.2 23.7 %line_gather.2 = bf16[2,2,4096,128]{3,2,1,0:T(8,128)(2,1)} custom-call(bf16[2,2,512,128]{3,2,1,0:T(8,128)(2,1)} %pad_maximum_fusion.3.refs_0_), custom_call_target="tpu_custom_call" | custom-call | tf_op jit(solution)/shard_map/line_gather/pallas_call | solution.py:582
  66.9 5.5 slice_bitcast_fusion.2
  72.4 4.1 copy.124.v_ref
  76.5 7.7 %attention_forward.1 = (f32[2,2,512,128]{3,2,1,0:T(8,128)}, bf16[2,2,512,128]{3,2,1,0:T(8,128)(2,1)}, f32[2,8,2048]{2,1,0:T(8,128)}) custom-call(s32[1]{0:T(128)} %bitcast.1.place_ref, bf16[2,2,512,128]{3,2,1,0:T(8,128)(2,1)} %bitcast.195, bf16[2,4096,128]{2,1,0:T(8,128)(2,1)} %get-tuple-element.102.k_ref, bf16[2,128,4096]{2,1,0:T(8,128)(2,1)} %copy.124.v_ref), custom_call_target="tpu_custom_call" | custom-call | tf_op jit(solution)/shard_map/attention_forward/pallas_call | solution.py:107
  84.2 1.2 copy.125
  85.4 2.1 convolution_convert_fusion.1.p_ref
  87.5 22.5 %square_scatter.2 = f32[2,128,1024]{2,1,0:T(8,128)} custom-call(bf16[2,512,1024]{2,1,0:T(8,128)(2,1)} %convolution_convert_fusion.1.p_ref), custom_call_target="tpu_custom_call" | custom-call | tf_op jit(solution)/shard_map/square_scatter/pallas_call | solution.py:446
  110.1 1.4 multiply_reduce_fusion.2
  112.7 92.1 %line_gather.3 = (bf16[2048,1024]{1,0:T(8,128)(2,1)}, f32[8,16,256]{2,1,0:T(8,128)}) custom-call(bf16[256,1024]{1,0:T(8,128)(2,1)} %bitcast.193, f32[1,16,256]{2,1,0:T(8,128)} %fusion.32.refs_1_), custom_call_target="tpu_custom_call" | custom-call | tf_op jit(solution)/shard_map/line_gather/pallas_call | solution.py:582
  204.8 0.9 constant_dynamic-slice_fusion
  206.3 34.3 %experts_both.1 = (bf16[2048,1024]{1,0:T(8,128)(2,1)}, bf16[2048,1024]{1,0:T(8,128)(2,1)}, f32[8,8,256]{2,1,0:T(8,128)}, bf16[2048,1024]{1,0:T(8,128)(2,1)}, bf16[2048,2048]{1,0:T(8,128)(2,1)}) custom-call(bf16[2048,1024]{1,0:T(8,128)(2,1)} %get-tuple-element.28.x_ref.left_ref, bf16[2048,1024]{1,0:T(8,128)(2,1)} %all-gather.2.cloned.1.call-done.u_ref.right_ref, ...), custom_call_target="tpu_custom_call" | custom-call | tf_op jit(solution)/shard_map/experts_both/pallas_call | solution.py:270
  240.6 8.7 %turned_product.3 = bf16[1024,1024]{1,0:T(8,128)(2,1)} custom-call(bf16[2048,1024]{1,0:T(8,128)(2,1)} %get-tuple-element.41.left_ref, bf16[2048,1024]{1,0:T(8,128)(2,1)} %all-gather.2.cloned.1.call-done.u_ref.right_ref), custom_call_target="tpu_custom_call" | custom-call | tf_op jit(solution)/shard_map/turned_product/pallas_call | solution.py:292
  249.3 14.2 %turned_product.2 = bf16[1024,2048]{1,0:T(8,128)(2,1)} custom-call(bf16[2048,1024]{1,0:T(8,128)(2,1)} %get-tuple-element.28.x_ref.left_ref, bf16[2048,2048]{1,0:T(8,128)(2,1)} %get-tuple-element.40.right_ref), custom_call_target="tpu_custom_call" | custom-call | tf_op jit(solution)/shard_map/turned_product/pallas_call | solution.py:292
  263.6 7.8 %reshape.260 = bf16[1024,2,2,512]{3,2,1,0:T(2,128)(2,1)} reshape(bf16[1024,2048]{1,0:T(8,128)(2,1)} %turned_product.2) | data formatting | bytes 8388608 | tf_op jit(solution)/shard_map/reshape | solution.py:937
  271.4 9.8 %fusion.41 = (bf16[1024,2,1,512]{3,2,1,0:T(2,128)(2,1)S(1)}, bf16[1024,2,1,512]{3,2,1,0:T(2,128)(2,1)}) fusion(bf16[1024,2,2,512]{3,2,1,0:T(2,128)(2,1)} %reshape.260), kind=kLoop, calls=%fused_computation.98 | loop fusion | bytes 8388608 | tf_op jit(solution)/shard_map/slice | solution.py:942
  281.1 2.0 copy.181
  283.3 0.9 slice_dynamic-update-slice_fusion.refs_1_
  284.8 41.7 %line_scatter.5 = (f32[256,1024]{1,0:T(8,128)}, f32[16,256]{1,0:T(8,128)}) custom-call(bf16[8,256,1024]{2,1,0:T(8,128)(2,1)} %bitcast.198, f32[8,16,256]{2,1,0:T(8,128)} %copy-done.18), custom_call_target="tpu_custom_call" | custom-call | tf_op jit(solution)/shard_map/line_scatter/pallas_call | solution.py:730
  326.4 0.7 fusion.26
  327.2 1.9 convolution_add_fusion
  329.4 0.7 copy-done.6
  330.1 1.1 fusion.24.x_ref
  331.2 19.4 %square_gather.3 = bf16[2,512,1024]{2,1,0:T(8,128)(2,1)} custom-call(bf16[2,128,1024]{2,1,0:T(8,128)(2,1)} %fusion.24.x_ref), custom_call_target="tpu_custom_call" | custom-call | tf_op jit(solution)/shard_map/square_gather/pallas_call | solution.py:375
  350.6 3.2 convolution_convert_fusion.2
  353.8 2.0 copy.129
  355.9 16.8 %attention_backward.1 = (f32[2,2,512,128]{3,2,1,0:T(8,128)}, bf16[2,4096,128]{2,1,0:T(8,128)(2,1)}, bf16[2,4096,128]{2,1,0:T(8,128)(2,1)}) custom-call(s32[1]{0:T(128)} %bitcast.1.place_ref, bf16[2,2,512,128]{3,2,1,0:T(8,128)(2,1)} %bitcast.196, bf16[2,2,512,128]{3,2,1,0:T(8,128)(2,1)} %bitcast.202, f32[2,2,512,128]{3,2,1,0:T(8,128)} %get-tuple-element.35.o_ref, ...), custom_call_target="tpu_custom_call" | custom-call | tf_op jit(solution)/shard_map/attention_backward/pallas_call | solution.py:202
  372.7 2.5 copy.130
  375.2 4.2 copy.182
  379.5 0.8 copy-done.15
  380.3 1.4 subtract_convert_fusion
  381.7 85.1 %line_scatter.4 = f32[256,1024]{1,0:T(8,128)} custom-call(bf16[8,256,1024]{2,1,0:T(8,128)(2,1)} %bitcast.197), custom_call_target="tpu_custom_call" | custom-call | tf_op jit(solution)/shard_map/line_scatter/pallas_call | solution.py:730
  466.8 0.8 pad_maximum_fusion.4
  467.6 2.0 copy.134
  469.6 3.7 copy_bitcast_fusion.refs_0_
  473.3 42.2 %line_scatter.6 = f32[2,2,512,128]{3,2,1,0:T(8,128)} custom-call(bf16[8,2,2,512,128]{4,3,2,1,0:T(8,128)(2,1)} %copy_bitcast_fusion.refs_0_), custom_call_target="tpu_custom_call" | custom-call | tf_op jit(solution)/shard_map/line_scatter/pallas_call | solution.py:730
  515.5 1.9 slice.89
  517.4 2.0 copy.133
  519.4 1.1 subtract_convert_fusion.2
  520.5 0.8 copy.135
  521.4 1.1 fusion.23
  522.5 4.0 convolution_convert_fusion.p_ref
  526.5 23.4 %square_scatter.3 = f32[2,128,1024]{2,1,0:T(8,128)} custom-call(bf16[2,512,1024]{2,1,0:T(8,128)(2,1)} %convolution_convert_fusion.p_ref), custom_call_target="tpu_custom_call" | custom-call | tf_op jit(solution)/shard_map/square_scatter/pallas_call | solution.py:446
  550.0 0.8 fusion.6
  550.7 0.8 copy-done.8
  551.7 1.3 bitcast_convert_fusion
  553.0 1.3 pad_maximum_fusion.1.refs_0_
  554.3 20.7 %line_scatter.7 = f32[128,768]{1,0:T(8,128)} custom-call(bf16[8,128,768]{2,1,0:T(8,128)(2,1)} %pad_maximum_fusion.1.refs_0_), custom_call_target="tpu_custom_call" | custom-call | tf_op jit(solution)/shard_map/line_scatter/pallas_call | solution.py:730
  575.4 1.3 fusion.18
  576.8 1.8 copy.147
  579.5 21.4 %small_sum.1 = f32[24,1024]{1,0:T(8,128)} custom-call(f32[24,1024]{1,0:T(8,128)} %select_maximum_fusion.x_ref), custom_call_target="tpu_custom_call" | custom-call | tf_op jit(solution)/shard_map/small_sum/pallas_call | solution.py:766
  601.9 0.8 copy.148
  602.6 1.3 copy.146
  605.8 2.1 convert_element_type.104
  608.0 2.1 convert_element_type.103
  610.1 2.1 convert_element_type.102
  (110 shorter events, 9.3 us)
Async XLA Ops:
  7.2 104.6 %copy-start = (bf16[1024,16]{0,1:T(8,128)(2,1)S(1)}, bf16[1024,16]{0,1:T(8,128)(2,1)}, u32[]{:S(2)}) copy-start(bf16[1024,16]{0,1:T(8,128)(2,1)} %param.21) | copy-start | bytes 98308
  7.2 3.3 copy-start.23
  7.2 3.5 copy-start.19
  7.2 199.1 %all-gather.2.cloned.1.call-start = ((), (), s32[]{:S(2)}) async-start(), calls=%async_computation.3 | async-start | bytes 4718592 | tf_op jit(solution)/shard_map/all_gather | solution.py:846
  9.3 1.7 copy-start.2
  9.3 1.9 copy-start.29
  9.3 596.5 %reduce-scatter.8.cloned.1.call-start = ((), (), s32[]{:S(2)}) async-start(), calls=%async_computation.6 | async-start | bytes 2621440 | tf_op jit(solution)/shard_map/reduce_scatter | solution.py:939
  10.5 23.8 %copy-start.24 = (bf16[1024,128]{0,1:T(8,128)(2,1)}, bf16[1024,128]{0,1:T(8,128)(2,1)S(1)}, u32[]{:S(2)}) copy-start(bf16[1024,128]{0,1:T(8,128)(2,1)S(1)} %copy.119) | copy-start | bytes 786436
  10.7 23.7 %copy-start.25 = (bf16[1024,128]{0,1:T(8,128)(2,1)}, bf16[1024,128]{0,1:T(8,128)(2,1)S(1)}, u32[]{:S(2)}) copy-start(bf16[1024,128]{0,1:T(8,128)(2,1)S(1)} %copy.120) | copy-start | bytes 786436
  11.0 23.4 %copy-start.20 = (bf16[1024,2,2,64]{0,3,2,1:T(8,128)(2,1)}, bf16[1024,2,2,64]{0,3,2,1:T(8,128)(2,1)S(1)}, u32[]{:S(2)}) copy-start(bf16[1024,2,2,64]{0,3,2,1:T(8,128)(2,1)S(1)} %copy.118) | copy-start | bytes 1572868
  39.2 46.2 %copy-start.13 = (bf16[2,2,64,1024]{3,2,1,0:T(8,128)(2,1)}, bf16[2,2,64,1024]{3,2,1,0:T(8,128)(2,1)S(1)}, u32[]{:S(2)}) copy-start(bf16[2,2,64,1024]{3,2,1,0:T(8,128)(2,1)S(1)} %copy.126) | copy-start | bytes 1572868
  40.4 0.6 copy-start.16
  41.0 1.1 copy-start.17
  85.4 24.6 %copy-start.11 = (bf16[2,512,2,128]{1,3,2,0:T(8,128)(2,1)}, bf16[2,512,2,128]{1,3,2,0:T(8,128)(2,1)S(1)}, u32[]{:S(2)}) copy-start(bf16[2,512,2,128]{1,3,2,0:T(8,128)(2,1)S(1)} %copy.125) | copy-start | bytes 1572868
  87.5 22.6 %copy-start.30 = (s32[128,2,8]{0,2,1:T(8,128)S(1)}, s32[128,2,8]{0,2,1:T(8,128)}, u32[]{:S(2)}) copy-start(s32[128,2,8]{0,2,1:T(8,128)} %param.25) | copy-start | bytes 24580
  110.1 1.5 copy-start.28
  111.7 0.9 copy-start.4
  249.3 358.7 %reduce-scatter.6.cloned.1.call-start = ((), (), s32[]{:S(2)}) async-start(), calls=%async_computation.5 | async-start | bytes 2621440 | tf_op jit(solution)/shard_map/reduce_scatter | solution.py:939
  283.2 326.9 %reduce-scatter.4.cloned.1.call-start = ((), (), s32[]{:S(2)}) async-start(), calls=%async_computation.4 | async-start | bytes 2621440 | tf_op jit(solution)/shard_map/reduce_scatter | solution.py:939
  284.1 0.7 copy-start.18
  329.1 1.0 copy-start.6
  379.5 0.8 copy-start.15
  526.5 23.4 %copy-start.9 = (bf16[2,512,1024]{2,1,0:T(8,128)(2,1)S(1)}, bf16[2,512,1024]{2,1,0:T(8,128)(2,1)}, u32[]{:S(2)}) copy-start(bf16[2,512,1024]{2,1,0:T(8,128)(2,1)} %square_gather.3) | copy-start | bytes 6291460
  526.5 23.4 %copy-start.12 = (bf16[2,512,2,128]{1,3,2,0:T(8,128)(2,1)S(1)}, bf16[2,512,2,128]{1,3,2,0:T(8,128)(2,1)}, u32[]{:S(2)}) copy-start(bf16[2,512,2,128]{1,3,2,0:T(8,128)(2,1)} %copy-done.11) | copy-start | bytes 1572868
  549.9 1.6 copy-start.8
  550.0 1.7 copy-start.21
  550.0 1.7 copy-start.26
  553.0 22.0 %copy-start.3 = (f32[2,128,1024]{2,1,0:T(8,128)S(1)}, f32[2,128,1024]{2,1,0:T(8,128)}, u32[]{:S(2)}) copy-start(f32[2,128,1024]{2,1,0:T(8,128)} %square_scatter.3) | copy-start | bytes 3145732
  554.3 21.2 %copy-start.7 = (f32[256,1024]{1,0:T(8,128)S(1)}, f32[256,1024]{1,0:T(8,128)}, u32[]{:S(2)}) copy-start(f32[256,1024]{1,0:T(8,128)} %line_scatter.4) | copy-start | bytes 3145732
  576.8 1.8 copy-start.5
  576.8 1.8 copy-start.27
  576.8 24.2 %copy-start.14 = (f32[128,768]{1,0:T(8,128)S(1)}, f32[128,768]{1,0:T(8,128)}, u32[]{:S(2)}) copy-start(f32[128,768]{1,0:T(8,128)} %line_scatter.7) | copy-start | bytes 1179652
  576.8 25.8 %copy-start.10 = (bf16[128,2,1024]{2,0,1:T(8,128)(2,1)S(1)}, bf16[128,2,1024]{2,0,1:T(8,128)(2,1)}, u32[]{:S(2)}) copy-start(bf16[128,2,1024]{2,0,1:T(8,128)(2,1)} %get-tuple-element.108) | copy-start | bytes 1572868
  600.9 3.0 copy-start.22
  605.2 7.1 %copy-start.1 = (bf16[1024,16]{0,1:T(8,128)(2,1)S(1)}, bf16[1024,16]{0,1:T(8,128)(2,1)}, u32[]{:S(2)}) copy-start(bf16[1024,16]{0,1:T(8,128)(2,1)} %param.21) | copy-start | bytes 98308
Sparse Core Ops, SparseCore 0:
  10.2 55.4 all-gather.1
  249.4 32.4 reduce-scatter.7
  285.1 35.1 reduce-scatter.5
  379.6 73.8 reduce-scatter.3

commit v3 on v2

--- a/solution.py
+++ b/solution.py
@@ -15,292 +15,6 @@
 MASKED = -1e30
 PRECISE = lax.Precision.HIGHEST
 VMEM_BYTES = 56 << 20
-
-
-def dot_t(left, right):
-    return lax.dot_general(left, right, (((1,), (1,)), ((), ())), preferred_element_type=jnp.float32)
-
-
-def dot_n(left, right):
-    return lax.dot_general(left, right, (((1,), (0,)), ((), ())), preferred_element_type=jnp.float32)
-
-
-def dot_c(left, right):
-    return lax.dot_general(left, right, (((0,), (0,)), ((), ())), preferred_element_type=jnp.float32)
-
-
-def head_mask(shape, head):
-    lane = lax.broadcasted_iota(jnp.int32, shape, len(shape) - 1)
-    return jnp.logical_and(lane >= head * HD, lane < (head + 1) * HD)
-
-
-def only_head(block, head):
-    if block.shape[-1] == HD:
-        return block
-    return jnp.where(head_mask(block.shape, head), block, jnp.zeros_like(block))
-
-
-def attn_fwd_kernel(place_ref, q_ref, k_ref, v_ref, o_ref, low_ref, log_ref, top_ref, sum_ref, acc_ref):
-    step = pl.program_id(1)
-    place = place_ref[0]
-    groups, rows, cols = q_ref.shape[1:]
-    pairs = [(group, head) for group in range(groups) for head in range(cols // HD)]
-
-    @pl.when(step == 0)
-    def _():
-        top_ref[...] = jnp.full(top_ref.shape, MASKED, jnp.float32)
-        sum_ref[...] = jnp.zeros(sum_ref.shape, jnp.float32)
-        acc_ref[...] = jnp.zeros(acc_ref.shape, jnp.float32)
-
-    def one(masked):
-        key_block = k_ref[0]
-
-        def scores_of(number):
-            group, head = pairs[number]
-            return dot_t(key_block, only_head(q_ref[0, group], head))
-
-        ahead = scores_of(0)
-        for number, (group, head) in enumerate(pairs):
-            part = pl.ds(number * rows, rows)
-            lanes = pl.ds(head * HD, HD)
-            scores = ahead
-            if number + 1 < len(pairs):
-                ahead = scores_of(number + 1)
-            if masked:
-                row = lax.broadcasted_iota(jnp.int32, scores.shape, 0)
-                col = lax.broadcasted_iota(jnp.int32, scores.shape, 1)
-                scores = jnp.where(row <= col, scores, MASKED)
-            old = top_ref[:1, part]
-            new = jnp.maximum(old, jnp.max(scores, axis=0, keepdims=True))
-            fade = jnp.exp(old - new)
-            weights = jnp.exp(scores - new)
-            sum_ref[:1, part] = sum_ref[:1, part] * fade + jnp.sum(weights, axis=0, keepdims=True)
-            acc_ref[group, lanes, :] = acc_ref[group, lanes, :] * fade + dot_n(
-                v_ref[0, lanes, :], weights.astype(jnp.bfloat16)
-            )
-            top_ref[:1, part] = new
-
-    @pl.when(step < place)
-    def _():
-        one(False)
-
-    @pl.when(step == place)
-    def _():
-        one(True)
-        for number, (group, head) in enumerate(pairs):
-            part = pl.ds(number * rows, rows)
-            lanes = pl.ds(head * HD, HD)
-            total = sum_ref[:1, part]
-            acc_ref[group, lanes, :] = acc_ref[group, lanes, :] / total
-            log_ref[0, :, part] = jnp.broadcast_to(top_ref[:1, part] + jnp.log(total), (8, rows))
-        for group in range(groups):
-            result = jnp.transpose(acc_ref[group])
-            o_ref[0, group] = result
-            low_ref[0, group] = result.astype(jnp.bfloat16)
-
-
-def attn_fwd(place, q, k, v_turned):
-    seqs, groups, rows, cols = q.shape
-    count = k.shape[1] // rows
-    heads = groups * cols // HD
-    whole = pl.BlockSpec((1, groups, rows, cols), lambda s, j, p: (s, 0, 0, 0))
-    return pl.pallas_call(
-        attn_fwd_kernel,
-        grid_spec=pltpu.PrefetchScalarGridSpec(
-            num_scalar_prefetch=1,
-            grid=(seqs, count),
-            in_specs=[
-                whole,
-                pl.BlockSpec((1, rows, cols), lambda s, j, p: (s, jnp.minimum(j, p[0]), 0)),
-                pl.BlockSpec((1, cols, rows), lambda s, j, p: (s, 0, jnp.minimum(j, p[0]))),
-            ],
-            out_specs=[whole, whole, pl.BlockSpec((1, 8, heads * rows), lambda s, j, p: (s, 0, 0))],
-            scratch_shapes=[
-                pltpu.VMEM((8, heads * rows), jnp.float32),
-                pltpu.VMEM((8, heads * rows), jnp.float32),
-                pltpu.VMEM((groups, cols, rows), jnp.float32),
-            ],
-        ),
-        out_shape=[
-            jax.ShapeDtypeStruct(q.shape, jnp.float32),
-            jax.ShapeDtypeStruct(q.shape, jnp.bfloat16),
-            jax.ShapeDtypeStruct((seqs, 8, heads * rows), jnp.float32),
-        ],
-        compiler_params=pltpu.CompilerParams(vmem_limit_bytes=VMEM_BYTES),
-        name="attention_forward",
-    )(place, q, k, v_turned)
-
-
-def attn_bwd_kernel(scale, place_ref, q_ref, g_ref, o_ref, log_ref, k_ref, v_ref, dq_ref, dk_ref, dv_ref, inner_ref, acc_ref):
-    step = pl.program_id(1)
-    place = place_ref[0]
-    groups, rows, cols = q_ref.shape[1:]
-    pairs = [(group, head) for group in range(groups) for head in range(cols // HD)]
-
-    @pl.when(step == 0)
-    def _():
-        acc_ref[...] = jnp.zeros(acc_ref.shape, jnp.float32)
-        ones = jnp.ones((8, cols), jnp.float32)
-        for number, (group, head) in enumerate(pairs):
-            prod = only_head(g_ref[0, group].astype(jnp.float32) * o_ref[0, group], head)
-            inner_ref[:, pl.ds(number * rows, rows)] = lax.dot_general(
-                ones, prod, (((1,), (1,)), ((), ())), precision=PRECISE, preferred_element_type=jnp.float32
-            )
-
-    def one(masked):
-        key_block = k_ref[0]
-        value_block = v_ref[0]
-        dk = jnp.zeros(dk_ref.shape[1:], jnp.float32)
-        dv = jnp.zeros(dv_ref.shape[1:], jnp.float32)
-
-        def ahead_of(number):
-            group, head = pairs[number]
-            q = only_head(q_ref[0, group], head)
-            g = only_head(g_ref[0, group], head)
-            return q, g, dot_t(key_block, q), dot_t(value_block, g)
-
-        ahead = ahead_of(0)
-        for number, (group, head) in enumerate(pairs):
-            part = pl.ds(number * rows, rows)
-            q, g, scores, back = ahead
-            if number + 1 < len(pairs):
-                ahead = ahead_of(number + 1)
-            probs = jnp.exp(scores - log_ref[0, :1, part])
-            if masked:
-                row = lax.broadcasted_iota(jnp.int32, scores.shape, 0)
-                col = lax.broadcasted_iota(jnp.int32, scores.shape, 1)
-                probs = jnp.where(row <= col, probs, 0.0)
-            grads = (probs * (back - inner_ref[:1, part])).astype(jnp.bfloat16)
-            dv = dv + dot_n(probs.astype(jnp.bfloat16), g)
-            dk = dk + dot_n(grads, q)
-            acc_ref[group] = acc_ref[group] + dot_c(grads, only_head(key_block, head))
-        dk_ref[0] = dk.astype(dk_ref.dtype)
-        dv_ref[0] = dv.astype(dv_ref.dtype)
-
-    @pl.when(step < place)
-    def _():
-        one(False)
-
-    @pl.when(step == place)
-    def _():
-        one(True)
-        dq_ref[0] = acc_ref[...] * scale
-
-    @pl.when(step > place)
-    def _():
-        dk_ref[...] = jnp.zeros(dk_ref.shape, dk_ref.dtype)
-        dv_ref[...] = jnp.zeros(dv_ref.shape, dv_ref.dtype)
-
-
-def attn_bwd(scale, place, q, g, o, logs, k, v):
-    seqs, groups, rows, cols = q.shape
-    count = k.shape[1] // rows
-    heads = groups * cols // HD
-    whole = pl.BlockSpec((1, groups, rows, cols), lambda s, j, p: (s, 0, 0, 0))
-    kv_spec = pl.BlockSpec((1, rows, cols), lambda s, j, p: (s, jnp.minimum(j, p[0]), 0))
-    out_spec = pl.BlockSpec((1, rows, cols), lambda s, j, p: (s, j, 0))
-    return pl.pallas_call(
-        functools.partial(attn_bwd_kernel, scale),
-        grid_spec=pltpu.PrefetchScalarGridSpec(
-            num_scalar_prefetch=1,
-            grid=(seqs, count),
-            in_specs=[
-                whole,
-                whole,
-                whole,
-                pl.BlockSpec((1, 8, heads * rows), lambda s, j, p: (s, 0, 0)),
-                kv_spec,
-                kv_spec,
-            ],
-            out_specs=[whole, out_spec, out_spec],
-            scratch_shapes=[
-                pltpu.VMEM((8, heads * rows), jnp.float32),
-                pltpu.VMEM((groups, rows, cols), jnp.float32),
-            ],
-        ),
-        out_shape=[
-            jax.ShapeDtypeStruct(q.shape, jnp.float32),
-            jax.ShapeDtypeStruct(k.shape, jnp.bfloat16),
-            jax.ShapeDtypeStruct(k.shape, jnp.bfloat16),
-        ],
-        compiler_params=pltpu.CompilerParams(vmem_limit_bytes=VMEM_BYTES),
-        name="attention_backward",
-    )(place, q, g, o, logs, k, v)
-
-
-def expert_kernel(x_ref, u_ref, share_ref, gate_ref, up_ref, down_ref, out_ref, copy_ref, pick_ref, hid_ref, sig_ref):
-    x = x_ref[...]
-    u = u_ref[...]
-    experts, width = gate_ref.shape[0], gate_ref.shape[2]
-    out = jnp.zeros(out_ref.shape, jnp.float32)
-    copy = jnp.zeros(copy_ref.shape, jnp.float32)
-    share_columns = jnp.transpose(share_ref[0])
-    lane = lax.broadcasted_iota(jnp.int32, (x.shape[0], 128), 1)
-    picks = jnp.zeros((x.shape[0], 128), jnp.float32)
-    for e in range(experts):
-        gate = dot_n(x, gate_ref[e])
-        up = dot_n(x, up_ref[e])
-        back = dot_t(u, down_ref[e])
-        share = share_columns[:, e : e + 1]
-        sig = 1.0 / (1.0 + jnp.exp(-gate))
-        act = gate * sig
-        hidden = act * up
-        picks = jnp.where(lane == e, jnp.sum(hidden * back, axis=1, keepdims=True), picks)
-        hidden_low = (hidden * share).astype(jnp.bfloat16)
-        back = back * share
-        gate_signal = (back * up * (sig * (1.0 + gate * (1.0 - sig)))).astype(jnp.bfloat16)
-        up_signal = (back * act).astype(jnp.bfloat16)
-        hid_ref[:, e * width : (e + 1) * width] = hidden_low
-        sig_ref[:, (2 * e) * width : (2 * e + 1) * width] = gate_signal
-        sig_ref[:, (2 * e + 1) * width : (2 * e + 2) * width] = up_signal
-        out = out + dot_n(hidden_low, down_ref[e])
-        copy = copy + dot_t(gate_signal, gate_ref[e]) + dot_t(up_signal, up_ref[e])
-    out_ref[...] = out.astype(out_ref.dtype)
-    copy_ref[...] = copy.astype(copy_ref.dtype)
-    pick_ref[0] = jnp.transpose(picks)[: pick_ref.shape[1]]
-
-
-def experts_both(x, u, shares, gate, up, down):
-    tokens, model = x.shape
-    tile = shares.shape[2]
-    experts, _, width = gate.shape
-    def rows(cols): return pl.BlockSpec((tile, cols), lambda t: (t, 0))
-    def fixed(a): return pl.BlockSpec(a.shape, lambda t: (0,) * a.ndim, pipeline_mode=pl.Buffered(1))
-    small = pl.BlockSpec((1,) + shares.shape[1:], lambda t: (t, 0, 0))
-    return pl.pallas_call(
-        expert_kernel,
-        grid=(tokens // tile,),
-        in_specs=[rows(model), rows(model), small, fixed(gate), fixed(up), fixed(down)],
-        out_specs=[rows(model), rows(model), small, rows(experts * width), rows(2 * experts * width)],
-        out_shape=[
-            jax.ShapeDtypeStruct((tokens, model), jnp.bfloat16),
-            jax.ShapeDtypeStruct((tokens, model), jnp.bfloat16),
-            jax.ShapeDtypeStruct(shares.shape, jnp.float32),
-            jax.ShapeDtypeStruct((tokens, experts * width), jnp.bfloat16),
-            jax.ShapeDtypeStruct((tokens, 2 * experts * width), jnp.bfloat16),
-        ],
-        compiler_params=pltpu.CompilerParams(vmem_limit_bytes=VMEM_BYTES),
-        name="experts_both",
-    )(x, u, shares, gate, up, down)
-
-
-def turned_kernel(left_ref, right_ref, out_ref):
-    out_ref[...] = dot_c(left_ref[...], right_ref[...]).astype(out_ref.dtype)
-
-
-def turned_product(left, right, rows):
-    return pl.pallas_call(
-        turned_kernel,
-        grid=(left.shape[1] // rows,),
-        in_specs=[
-            pl.BlockSpec((left.shape[0], rows), lambda i: (0, i)),
-            pl.BlockSpec(right.shape, lambda i: (0, 0), pipeline_mode=pl.Buffered(1)),
-        ],
-        out_specs=pl.BlockSpec((rows, right.shape[1]), lambda i: (i, 0)),
-        out_shape=jax.ShapeDtypeStruct((left.shape[1], right.shape[1]), jnp.bfloat16),
-        compiler_params=pltpu.CompilerParams(vmem_limit_bytes=VMEM_BYTES),
-        name="turned_product",
-    )(left, right)
 
 
 MESH = pl.DeviceIdType.MESH
@@ -779,6 +493,469 @@
         ),
         name="small_sum",
     )(values)
+
+
+def dot_t(left, right):
+    return lax.dot_general(left, right, (((1,), (1,)), ((), ())), preferred_element_type=jnp.float32)
+
+
+def dot_n(left, right):
+    return lax.dot_general(left, right, (((1,), (0,)), ((), ())), preferred_element_type=jnp.float32)
+
+
+def dot_c(left, right):
+    return lax.dot_general(left, right, (((0,), (0,)), ((), ())), preferred_element_type=jnp.float32)
+
+
+def head_mask(shape, head):
+    lane = lax.broadcasted_iota(jnp.int32, shape, len(shape) - 1)
+    return jnp.logical_and(lane >= head * HD, lane < (head + 1) * HD)
+
+
+def only_head(block, head):
+    if block.shape[-1] == HD:
+        return block
+    return jnp.where(head_mask(block.shape, head), block, jnp.zeros_like(block))
+
+
+def pairs_of(q_ref, cols):
+    return [
+        (group, head) for group in range(q_ref.shape[2] // cols) for head in range(cols // HD)
+    ]
+
+
+def causal(shape):
+    row = lax.broadcasted_iota(jnp.int32, shape, 0)
+    col = lax.broadcasted_iota(jnp.int32, shape, 1)
+    return row <= col
+
+
+def attn_fwd_kernel(
+    q_ref, pair_ref, held_ref, o_ref, low_ref, log_ref, top_ref, sum_ref, acc_ref, *sems
+):
+    local_sem, core_s, core_r, up_s, up_r = sems
+    chips, chip, core, sibling, above, below = line_places()
+    has_above, has_below = chip < chips - 1, chip > 0
+    greet([(sibling, None), (above, has_above), (below, has_below)])
+    seqs, rows, _ = q_ref.shape
+    cols = pair_ref.shape[2] // 2
+    pairs = pairs_of(q_ref, cols)
+    own = chip * 2 + core
+
+    def up_copy(source, block, number):
+        return copier(source, held_ref.at[block], up_s, up_r, number, above)
+
+    def core_copy(source, block, number):
+        return copier(source, held_ref.at[block], core_s, core_r, number, sibling)
+
+    @pl.when(has_above)
+    def _():
+        up_copy(pair_ref, own, 1).start()
+
+    core_copy(pair_ref, own, 0).start()
+    keep = pltpu.make_async_copy(pair_ref, held_ref.at[own], local_sem)
+    keep.start()
+    top_ref[...] = jnp.full(top_ref.shape, MASKED, jnp.float32)
+    sum_ref[...] = jnp.zeros(sum_ref.shape, jnp.float32)
+    acc_ref[...] = jnp.zeros(acc_ref.shape, jnp.float32)
+
+    def one(pair_block, seq, masked):
+        key_block = pair_block[:, :cols]
+        value_turned = jnp.transpose(pair_block[:, cols:])
+
+        def scores_of(number):
+            group, head = pairs[number]
+            return dot_t(key_block, only_head(q_ref[seq, :, pl.ds(group * cols, cols)], head))
+
+        ahead = scores_of(0)
+        for number, (group, head) in enumerate(pairs):
+            part = pl.ds(number * rows, rows)
+            lanes = pl.ds(head * HD, HD)
+            scores = ahead
+            if number + 1 < len(pairs):
+                ahead = scores_of(number + 1)
+            if masked:
+                scores = jnp.where(causal(scores.shape), scores, MASKED)
+            old = top_ref[seq, :1, part]
+            new = jnp.maximum(old, jnp.max(scores, axis=0, keepdims=True))
+            fade = jnp.exp(old - new)
+            weights = jnp.exp(scores - new)
+            sum_ref[seq, :1, part] = sum_ref[seq, :1, part] * fade + jnp.sum(
+                weights, axis=0, keepdims=True
+            )
+            acc_ref[seq, group, lanes, :] = acc_ref[seq, group, lanes, :] * fade + dot_n(
+                value_turned[head * HD : (head + 1) * HD, :], weights.astype(jnp.bfloat16)
+            )
+            top_ref[seq, :1, part] = new
+
+    def block_of(block):
+        def body(seq, carried):
+            one(held_ref[block, seq], seq, False)
+            return carried
+
+        lax.fori_loop(0, seqs, body, 0)
+
+    def own_body(seq, carried):
+        one(pair_ref[seq], seq, True)
+        return carried
+
+    lax.fori_loop(0, seqs, own_body, 0)
+    core_copy(pair_ref, chip * 2 + 1 - core, 0).wait_recv()
+
+    @pl.when(core == 1)
+    def _():
+        block_of(own - 1)
+
+    def step_body(step, carried):
+        @pl.when(chip >= step)
+        def _():
+            came = (chip - step) * 2 + core
+            other = (chip - step) * 2 + 1 - core
+            up_copy(held_ref.at[came], came, step).wait_recv()
+
+            @pl.when(has_above)
+            def _():
+                up_copy(held_ref.at[came], came, step + 1).start()
+
+            core_copy(held_ref.at[came], came, step).start()
+            block_of(came)
+            core_copy(held_ref.at[other], other, step).wait_recv()
+            block_of(other)
+
+        return carried
+
+    lax.fori_loop(1, chips, step_body, 0)
+
+    def finish_body(seq, carried):
+        for number, (group, head) in enumerate(pairs):
+            part = pl.ds(number * rows, rows)
+            lanes = pl.ds(head * HD, HD)
+            total = sum_ref[seq, :1, part]
+            acc_ref[seq, group, lanes, :] = acc_ref[seq, group, lanes, :] / total
+            log_ref[seq, :, part] = jnp.broadcast_to(
+                top_ref[seq, :1, part] + jnp.log(total), (8, rows)
+            )
+        for group in range(len(pairs) * HD // cols):
+            result = jnp.transpose(acc_ref[seq, group])
+            o_ref[seq, :, pl.ds(group * cols, cols)] = result
+            low_ref[seq, :, pl.ds(group * cols, cols)] = result.astype(jnp.bfloat16)
+        return carried
+
+    lax.fori_loop(0, seqs, finish_body, 0)
+
+    def sent_body(step, carried):
+        @pl.when(chip >= step)
+        def _():
+            came = (chip - step) * 2 + core
+            core_copy(held_ref.at[came], came, step).wait_send()
+
+            @pl.when(has_above)
+            def _():
+                up_copy(held_ref.at[came], came, step + 1).wait_send()
+
+        return carried
+
+    lax.fori_loop(0, chips, sent_body, 0)
+    keep.wait()
+
+
+def attn_fwd(q, pair, number):
+    seqs, rows, query_cols = q.shape
+    cols = pair.shape[2] // 2
+    wide_count = lax.axis_size("wide")
+    chips = wide_count // 2
+    heads = query_cols // HD
+    whole = pl.BlockSpec(memory_space=pltpu.VMEM)
+    return pl.pallas_call(
+        attn_fwd_kernel,
+        in_specs=[whole, whole],
+        out_specs=[whole] * 4,
+        out_shape=[
+            jax.ShapeDtypeStruct((wide_count,) + pair.shape, pair.dtype),
+            jax.ShapeDtypeStruct(q.shape, jnp.float32),
+            jax.ShapeDtypeStruct(q.shape, jnp.bfloat16),
+            jax.ShapeDtypeStruct((seqs, 8, heads * rows), jnp.float32),
+        ],
+        scratch_shapes=[
+            pltpu.VMEM((seqs, 8, heads * rows), jnp.float32),
+            pltpu.VMEM((seqs, 8, heads * rows), jnp.float32),
+            pltpu.VMEM((seqs, query_cols // cols, cols, rows), jnp.float32),
+            pltpu.SemaphoreType.DMA,
+        ]
+        + [pltpu.SemaphoreType.DMA((chips + 1,))] * 4,
+        compiler_params=pltpu.CompilerParams(
+            collective_id=number, has_side_effects=True, vmem_limit_bytes=VMEM_BYTES
+        ),
+        name="attention_forward",
+    )(q, pair)
+
+
+def attn_bwd_kernel(
+    scale,
+    q_ref,
+    g_ref,
+    o_ref,
+    log_ref,
+    held_ref,
+    dq_ref,
+    own_ref,
+    inner_ref,
+    mine_ref,
+    core_out,
+    core_in,
+    down_out,
+    down_in,
+    core_s,
+    core_r,
+    down_s,
+    down_r,
+):
+    chips, chip, core, sibling, above, below = line_places()
+    has_above, has_below = chip < chips - 1, chip > 0
+    greet([(sibling, None), (above, has_above), (below, has_below)])
+    seqs, rows, _ = q_ref.shape
+    cols = held_ref.shape[3] // 2
+    pairs = pairs_of(q_ref, cols)
+
+    def core_copy(step):
+        return copier(core_out.at[step], core_in.at[step], core_s, core_r, step, sibling)
+
+    def down_copy(step):
+        return copier(down_out.at[step], down_in.at[step - 1], down_s, down_r, step - 1, below)
+
+    def start_body(seq, carried):
+        ones = jnp.ones((8, cols), jnp.float32)
+        for number, (group, head) in enumerate(pairs):
+            at = pl.ds(group * cols, cols)
+            prod = only_head(g_ref[seq, :, at].astype(jnp.float32) * o_ref[seq, :, at], head)
+            inner_ref[seq, :, pl.ds(number * rows, rows)] = lax.dot_general(
+                ones,
+                prod,
+                (((1,), (1,)), ((), ())),
+                precision=PRECISE,
+                preferred_element_type=jnp.float32,
+            )
+        return carried
+
+    lax.fori_loop(0, seqs, start_body, 0)
+    dq_ref[...] = jnp.zeros(dq_ref.shape, jnp.float32)
+
+    def one(block, seq, masked):
+        key_block = held_ref[block, seq, :, :cols]
+        value_block = held_ref[block, seq, :, cols:]
+        dk = jnp.zeros(key_block.shape, jnp.float32)
+        dv = jnp.zeros(key_block.shape, jnp.float32)
+
+        def ahead_of(number):
+            group, head = pairs[number]
+            at = pl.ds(group * cols, cols)
+            q = only_head(q_ref[seq, :, at], head)
+            g = only_head(g_ref[seq, :, at], head)
+            return q, g, dot_t(key_block, q), dot_t(value_block, g)
+
+        ahead = ahead_of(0)
+        for number, (group, head) in enumerate(pairs):
+            part = pl.ds(number * rows, rows)
+            at = pl.ds(group * cols, cols)
+            q, g, scores, back = ahead
+            if number + 1 < len(pairs):
+                ahead = ahead_of(number + 1)
+            probs = jnp.exp(scores - log_ref[seq, :1, part])
+            if masked:
+                probs = jnp.where(causal(scores.shape), probs, 0.0)
+            grads = (probs * (back - inner_ref[seq, :1, part])).astype(jnp.bfloat16)
+            dv = dv + dot_n(probs.astype(jnp.bfloat16), g)
+            dk = dk + dot_n(grads, q)
+            dq_ref[seq, :, at] = dq_ref[seq, :, at] + dot_c(grads, only_head(key_block, head))
+        return dk, dv
+
+    def block_into(block, out_ref, step, masked):
+        def body(seq, carried):
+            dk, dv = one(block, seq, masked)
+            out_ref[step, seq] = jnp.concatenate([dk, dv], axis=1).astype(out_ref.dtype)
+            return carried
+
+        lax.fori_loop(0, seqs, body, 0)
+
+    def pass_on(step):
+        core_copy(step).wait_recv()
+        mine_ref[step] = mine_ref[step] + core_in[step].astype(jnp.float32)
+
+        @pl.when(has_above)
+        def _():
+            down_copy(step + 1).wait_recv()
+            mine_ref[step] = mine_ref[step] + down_in[step].astype(jnp.float32)
+
+        down_out[step] = mine_ref[step].astype(down_out.dtype)
+        down_copy(step).start()
+
+    def step_body(number, carried):
+        step = chips - 1 - number
+
+        @pl.when(chip >= step)
+        def _():
+            target = (chip - step) * 2
+            block_into(target + 1 - core, core_out, step, False)
+            core_copy(step).start()
+            block_into(target + core, mine_ref, step, False)
+
+        @pl.when(jnp.logical_and(has_above, chip >= step + 1))
+        def _():
+            pass_on(step + 1)
+
+        @pl.when(jnp.logical_and(jnp.logical_not(has_above), chip >= step))
+        def _():
+            pass_on(step)
+
+        return carried
+
+    lax.fori_loop(0, chips - 1, step_body, 0)
+
+    @pl.when(core == 1)
+    def _():
+        block_into(chip * 2, core_out, 0, False)
+        core_copy(0).start()
+
+    block_into(chip * 2 + core, mine_ref, 0, True)
+
+    @pl.when(jnp.logical_and(has_above, chip >= 1))
+    def _():
+        pass_on(1)
+
+    @pl.when(core == 0)
+    def _():
+        core_copy(0).wait_recv()
+        mine_ref[0] = mine_ref[0] + core_in[0].astype(jnp.float32)
+
+    @pl.when(has_above)
+    def _():
+        down_copy(1).wait_recv()
+        mine_ref[0] = mine_ref[0] + down_in[0].astype(jnp.float32)
+
+    own_ref[...] = mine_ref[0]
+    dq_ref[...] = dq_ref[...] * scale
+
+    @pl.when(core == 1)
+    def _():
+        core_copy(0).wait_send()
+
+    def sent_body(step, carried):
+        @pl.when(chip >= step)
+        def _():
+            core_copy(step).wait_send()
+            down_copy(step).wait_send()
+
+        return carried
+
+    lax.fori_loop(1, chips, sent_body, 0)
+
+
+def attn_bwd(scale, q, g, o, logs, held, number):
+    seqs, rows, query_cols = q.shape
+    chips = lax.axis_size("wide") // 2
+    heads = query_cols // HD
+    whole = pl.BlockSpec(memory_space=pltpu.VMEM)
+    block = (chips,) + held.shape[1:]
+    return pl.pallas_call(
+        functools.partial(attn_bwd_kernel, scale),
+        in_specs=[whole] * 5,
+        out_specs=[whole] * 2,
+        out_shape=[
+            jax.ShapeDtypeStruct(q.shape, jnp.float32),
+            jax.ShapeDtypeStruct(held.shape[1:], jnp.float32),
+        ],
+        scratch_shapes=[
+            pltpu.VMEM((seqs, 8, heads * rows), jnp.float32),
+            pltpu.VMEM(block, jnp.float32),
+        ]
+        + [pltpu.VMEM(block, jnp.bfloat16)] * 4
+        + [pltpu.SemaphoreType.DMA((chips,))] * 4,
+        compiler_params=pltpu.CompilerParams(
+            collective_id=number, has_side_effects=True, vmem_limit_bytes=VMEM_BYTES
+        ),
+        name="attention_backward",
+    )(q, g, o, logs, held)
+
+
+def expert_kernel(x_ref, u_ref, share_ref, gate_ref, up_ref, down_ref, out_ref, copy_ref, pick_ref, hid_ref, sig_ref):
+    x = x_ref[...]
+    u = u_ref[...]
+    experts, width = gate_ref.shape[0], gate_ref.shape[2]
+    out = jnp.zeros(out_ref.shape, jnp.float32)
+    copy = jnp.zeros(copy_ref.shape, jnp.float32)
+    share_columns = jnp.transpose(share_ref[0])
+    lane = lax.broadcasted_iota(jnp.int32, (x.shape[0], 128), 1)
+    picks = jnp.zeros((x.shape[0], 128), jnp.float32)
+    for e in range(experts):
+        gate = dot_n(x, gate_ref[e])
+        up = dot_n(x, up_ref[e])
+        back = dot_t(u, down_ref[e])
+        share = share_columns[:, e : e + 1]
+        sig = 1.0 / (1.0 + jnp.exp(-gate))
+        act = gate * sig
+        hidden = act * up
+        picks = jnp.where(lane == e, jnp.sum(hidden * back, axis=1, keepdims=True), picks)
+        hidden_low = (hidden * share).astype(jnp.bfloat16)
+        back = back * share
+        gate_signal = (back * up * (sig * (1.0 + gate * (1.0 - sig)))).astype(jnp.bfloat16)
+        up_signal = (back * act).astype(jnp.bfloat16)
+        hid_ref[:, e * width : (e + 1) * width] = hidden_low
+        sig_ref[:, e * width : (e + 1) * width] = gate_signal
+        sig_ref[:, (experts + e) * width : (experts + e + 1) * width] = up_signal
+        out = out + dot_n(hidden_low, down_ref[e])
+        copy = copy + dot_t(gate_signal, gate_ref[e]) + dot_t(up_signal, up_ref[e])
+    out_ref[...] = out.astype(out_ref.dtype)
+    copy_ref[...] = copy.astype(copy_ref.dtype)
+    pick_ref[0] = jnp.transpose(picks)[: pick_ref.shape[1]]
+
+
+def experts_both(x, u, shares, gate, up, down):
+    tokens, model = x.shape
+    tile = shares.shape[2]
+    experts, _, width = gate.shape
+    def rows(cols): return pl.BlockSpec((tile, cols), lambda t: (t, 0))
+    def fixed(a): return pl.BlockSpec(a.shape, lambda t: (0,) * a.ndim, pipeline_mode=pl.Buffered(1))
+    small = pl.BlockSpec((1,) + shares.shape[1:], lambda t: (t, 0, 0))
+    return pl.pallas_call(
+        expert_kernel,
+        grid=(tokens // tile,),
+        in_specs=[rows(model), rows(model), small, fixed(gate), fixed(up), fixed(down)],
+        out_specs=[rows(model), rows(model), small, rows(experts * width), rows(2 * experts * width)],
+        out_shape=[
+            jax.ShapeDtypeStruct((tokens, model), jnp.bfloat16),
+            jax.ShapeDtypeStruct((tokens, model), jnp.bfloat16),
+            jax.ShapeDtypeStruct(shares.shape, jnp.float32),
+            jax.ShapeDtypeStruct((tokens, experts * width), jnp.bfloat16),
+            jax.ShapeDtypeStruct((tokens, 2 * experts * width), jnp.bfloat16),
+        ],
+        compiler_params=pltpu.CompilerParams(vmem_limit_bytes=VMEM_BYTES),
+        name="experts_both",
+    )(x, u, shares, gate, up, down)
+
+
+def turned_kernel(left_ref, right_ref, *out_refs):
+    product = dot_c(left_ref[...], right_ref[...])
+    at = 0
+    for out_ref in out_refs:
+        for part in range(out_ref.shape[0]):
+            out_ref[part] = product[:, at : at + out_ref.shape[2]].astype(out_ref.dtype)
+            at += out_ref.shape[2]
+
+
+def turned_product(left, right, rows, kinds, parts):
+    cols = right.shape[1] // (kinds * parts)
+    return pl.pallas_call(
+        turned_kernel,
+        grid=(left.shape[1] // rows,),
+        in_specs=[
+            pl.BlockSpec((left.shape[0], rows), lambda i: (0, i)),
+            pl.BlockSpec(right.shape, lambda i: (0, 0), pipeline_mode=pl.Buffered(1)),
+        ],
+        out_specs=[pl.BlockSpec((parts, rows, cols), lambda i: (0, i, 0))] * kinds,
+        out_shape=[jax.ShapeDtypeStruct((parts, left.shape[1], cols), jnp.bfloat16)] * kinds,
+        compiler_params=pltpu.CompilerParams(vmem_limit_bytes=VMEM_BYTES),
+        name="turned_product",
+    )(left, right)
 
 
 def angles_of(positions, factor):
@@ -837,7 +1014,6 @@
     group_size = heads // kv_heads
     score_scale = HD ** (-0.5)
     factor = rope_scale[0]
-    place = wide_place.astype(jnp.int32).reshape(1)
     token_count = local_rows * sequences
 
     token_float = tokens.swapaxes(0, 1).astype(jnp.float32)
@@ -862,20 +1038,12 @@
     cosine, sine = angles_of(wide_place * block_rows + lax.iota(jnp.int32, block_rows), factor)
     head_cosine, head_sine = cosine[None, :, None, :], sine[None, :, None, :]
 
-    def by_group(flat):
-        return flat.reshape(sequences, block_rows, group_size, kv_cols).swapaxes(1, 2)
-
-    def flat_of(groups):
-        return groups.swapaxes(1, 2).reshape(sequences, block_rows, query_cols)
-
     query_rot = rotate(
         joint_proj[..., :query_cols].reshape(sequences, block_rows, heads, HD),
         head_cosine,
         head_sine,
     ).astype(jnp.bfloat16)
-    query_group = by_group(
-        (query_rot * jnp.bfloat16(score_scale)).reshape(sequences, block_rows, query_cols)
-    )
+    query_low = (query_rot * jnp.bfloat16(score_scale)).reshape(sequences, block_rows, query_cols)
     key_rot = rotate(
         joint_proj[..., query_cols : query_cols + kv_cols].reshape(
             sequences, block_rows, kv_heads, HD
@@ -885,13 +1053,9 @@
     )
     key_local = key_rot.astype(jnp.bfloat16).reshape(sequences, block_rows, kv_cols)
     value_local = joint_proj[..., query_cols + kv_cols :].astype(jnp.bfloat16)
-    (pair_all,) = gather_wide([jnp.stack([key_local, value_local])], (2,), False, 1)
-    key_all, value_all = pair_all[0], pair_all[1]
-
-    attn_result, attended, log_total = attn_fwd(
-        place, query_group, key_all, value_all.swapaxes(1, 2)
-    )
-    out_low = flat_of(attended)
+    pair_all, attn_result, out_low, log_total = attn_fwd(
+        query_low, jnp.concatenate([key_local, value_local], axis=-1), 1
+    )
     attn_branch = scatter_narrow(
         jnp.einsum("stc,cd->std", out_low, out_weight, preferred_element_type=jnp.float32).astype(
             jnp.bfloat16
@@ -928,19 +1092,19 @@
         return rows.reshape((wide_count, rows.shape[0] // wide_count) + rows.shape[1:])
 
     copy_sum, picks = scatter_wide([by_block(part_copy), part_picks], True, 4)
-    (moe_part,) = scatter_wide([by_block(part_out)], True, 5)
+    moe_part = lax.psum_scatter(part_out, "wide", scatter_dimension=0, tiled=True).astype(
+        jnp.float32
+    )
     layer_out = (residual + moe_part.reshape(residual.shape)).astype(jnp.bfloat16)
 
-    joint_signal = turned_product(moe_all, signals, block_rows // 2)
-    down_update = turned_product(hidden_shared, upstream_all, block_rows // 2)
     width = w_gate.shape[2]
-    split = joint_signal.reshape(model_width, local_experts, 2, width)
     expert_grads = tuple(
         lax.psum_scatter(update, "narrow", scatter_dimension=1, tiled=True).astype(jnp.float32)
         for update in (
-            split[:, :, 0].swapaxes(0, 1),
-            split[:, :, 1].swapaxes(0, 1),
-            down_update.reshape(local_experts, width, model_width),
+            *turned_product(moe_all, signals, block_rows // 2, 2, local_experts),
+            turned_product(hidden_shared, upstream_all, block_rows // 2, 1, 1)[0].reshape(
+                local_experts, width, model_width
+            ),
         )
     )
 
@@ -957,34 +1121,23 @@
     attended_grads = jnp.einsum(
         "std,cd->stc", branch_all, out_weight, preferred_element_type=jnp.float32
     ).astype(jnp.bfloat16)
-    query_grads, key_part, value_part = attn_bwd(
-        score_scale,
-        place,
-        query_group,
-        by_group(attended_grads),
-        attn_result,
-        log_total,
-        key_all,
-        value_all,
+    query_grads, pair_own = attn_bwd(
+        score_scale, query_low, attended_grads, attn_result, log_total, pair_all, 7
     )
     out_update = jnp.einsum("stc,std->cd", out_low, branch_all, preferred_element_type=jnp.float32)
-    pair_parts = jnp.stack([key_part, value_part]).reshape(
-        2, sequences, wide_count, block_rows, kv_cols
-    )
-    (pair_own,) = scatter_wide([pair_parts.transpose(2, 0, 1, 3, 4)], False, 7)
-    query_low = rotate(
-        flat_of(query_grads).reshape(sequences, block_rows, heads, HD), head_cosine, -head_sine
+    query_turned = rotate(
+        query_grads.reshape(sequences, block_rows, heads, HD), head_cosine, -head_sine
     ).astype(jnp.bfloat16)
     key_low = rotate(
-        pair_own[0].reshape(sequences, block_rows, kv_heads, HD),
+        pair_own[..., :kv_cols].reshape(sequences, block_rows, kv_heads, HD),
         head_cosine,
         -head_sine,
     ).astype(jnp.bfloat16)
     joint_grads = jnp.concatenate(
         [
-            query_low.reshape(sequences, block_rows, query_cols),
+            query_turned.reshape(sequences, block_rows, query_cols),
             key_low.reshape(sequences, block_rows, kv_cols),
-            pair_own[1].astype(jnp.bfloat16),
+            pair_own[..., kv_cols:].astype(jnp.bfloat16),
         ],
         axis=-1,
     )

time: 628 us -> 509 us (0.81)
  Pallas kernels: 496 us -> 410 us
  local copies, waits for them, and re-layouts: 65.9 us -> 32.3 us
    pallas_call x4 -> x2, Pallas kernels: 190 us -> 62.4 us  [scatter_wide(): pl.pallas_call(functools.partial(line_scatter_kernel, rising, count), out...]
    pallas_call x2, Pallas kernels: 24.5 us -> 106 us  [the longest x1 79.5 us: attn_bwd(): pl.pallas_call(functools.partial(attn_bwd_kernel, scale), in_specs=[whole...]
    pallas_call x2 -> x1, Pallas kernels: 116 us -> 75.6 us  [gather_wide(): pl.pallas_call(functools.partial(line_gather_kernel, axes, falling), out_...]
    reshape x2 -> x0, local copies, waits for them, and re-layouts: 9.86 us -> none  [the longest x1 7.82 us: on_device(): split = joint_signal.reshape(model_width, local_experts, 2, width)]
    slice x3, local copies, waits for them, and re-layouts: 13.7 us -> 5.7 us  [the longest x2 3.91 us: on_device(): pair_own[..., :kv_cols].reshape(sequences, block_rows, kv_heads, HD)]
    transpose x3 -> x0, local copies, waits for them, and re-layouts: 7.84 us -> none  [the longest x1 4.07 us: on_device(): value_all.swapaxes(1, 2)]
    pallas_call x2, Pallas kernels: 46 us -> 39.5 us  [scatter_narrow(): pl.pallas_call(square_scatter_kernel, out_shape=jax.ShapeDtypeStruct((seq...]
    unnamed x72 -> x68, local copies, waits for them, and re-layouts: 17.5 us -> 11.2 us
  transfers between devices with their start and end apart: 4 -> 5, of which waited for: 0 -> 0; matrix products, arithmetic and copies ran while one was open for 16% -> 12% of each run, Pallas kernels for 73% -> 72%
where the time goes in v3:
time: 509 us; the launch traced here: 500 us
  Pallas kernels  410 us (81%)
  local copies, waits for them, and re-layouts  32.3 us (6%)
  other arithmetic  22.6 us (4%)
  matrix products  17.9 us (4%)
  between operations  15.6 us (3%)
    pallas_call x1, Pallas kernels, attn_bwd(): pl.pallas_call(functools.partial(attn_bwd_kernel, scale), in_specs=[whole...  79.5 us
    pallas_call x1, Pallas kernels, gather_wide(): pl.pallas_call(functools.partial(line_gather_kernel, axes, falling), out_...  75.6 us
    pallas_call x2, Pallas kernels, scatter_wide(): pl.pallas_call(functools.partial(line_scatter_kernel, rising, count), out...  62.4 us
    pallas_call x2, Pallas kernels, gather_narrow(): pl.pallas_call(square_gather_kernel, out_shape=jax.ShapeDtypeStruct((bloc...  47.4 us
    pallas_call x2, Pallas kernels, scatter_narrow(): pl.pallas_call(square_scatter_kernel, out_shape=jax.ShapeDtypeStruct((seq...  39.5 us
    pallas_call x1, Pallas kernels, experts_both(): pl.pallas_call(expert_kernel, grid=(tokens // tile,), in_specs=[rows(mode...  34.3 us
    pallas_call x1, Pallas kernels, attn_fwd(): pl.pallas_call(attn_fwd_kernel, in_specs=[whole, whole], out_specs=[whole...  26.7 us
    pallas_call x2, Pallas kernels, turned_product(): pl.pallas_call(turned_kernel, grid=(left.shape[1] // rows,), in_specs=[pl...  23 us
  transfers between devices with their start and end apart: 5, of which 0 were waited for; matrix products, arithmetic and copies ran while one was open for 12% of the time, Pallas kernels for 72%

profile of v3, /device:TPU:0, one launch (start us, length us, event | category | flops | bytes accessed | tf_op | source)
XLA Modules:
  0.0 500.1 jit_solution(3342412321743894309)
XLA Ops:
  7.3 2.0 copy.104
  9.4 1.1 copy.99
  11.2 1.0 fusion.6.x_ref
  12.2 22.2 %square_gather.2 = bf16[2,512,1024]{2,1,0:T(8,128)(2,1)} custom-call(bf16[2,128,1024]{2,1,0:T(8,128)(2,1)} %fusion.6.x_ref), custom_call_target="tpu_custom_call" | custom-call | tf_op jit(solution)/shard_map/square_gather/pallas_call | solution.py:89
  34.4 2.9 fusion.14
  37.4 1.2 copy-done.8
  40.0 1.0 copy.102.q_ref
  41.5 0.9 pad_maximum_fusion.2.pair_ref
  42.4 26.7 %attention_forward.1 = (bf16[8,2,512,256]{3,2,1,0:T(8,128)(2,1)}, f32[2,512,256]{2,1,0:T(8,128)}, bf16[2,512,256]{2,1,0:T(8,128)(2,1)}, f32[2,8,2048]{2,1,0:T(8,128)}) custom-call(bf16[2,512,256]{2,1,0:T(8,128)(2,1)} %copy.102.q_ref, bf16[2,512,256]{2,1,0:T(8,128)(2,1)} %pad_maximum_fusion.2.pair_ref), custom_call_target="tpu_custom_call" | custom-call | tf_op jit(solution)/shard_map/attention_forward/pallas_call | solution.py:669
  69.1 3.1 convolution_convert_fusion.1.p_ref
  72.2 22.4 %square_scatter.2 = f32[2,128,1024]{2,1,0:T(8,128)} custom-call(bf16[2,512,1024]{2,1,0:T(8,128)(2,1)} %convolution_convert_fusion.1.p_ref), custom_call_target="tpu_custom_call" | custom-call | tf_op jit(solution)/shard_map/square_scatter/pallas_call | solution.py:160
  94.6 1.4 multiply_reduce_fusion.2
  96.6 0.6 fusion.24.refs_1_
  97.2 75.6 %line_gather.1 = (bf16[2048,1024]{1,0:T(8,128)(2,1)}, f32[8,16,256]{2,1,0:T(8,128)}) custom-call(bf16[256,1024]{1,0:T(8,128)(2,1)} %bitcast.145, f32[1,16,256]{2,1,0:T(8,128)} %fusion.24.refs_1_), custom_call_target="tpu_custom_call" | custom-call | tf_op jit(solution)/shard_map/line_gather/pallas_call | solution.py:296
  172.8 0.9 constant_dynamic-slice_fusion
  173.7 0.6 pad.8.share_ref
  174.3 34.3 %experts_both.1 = (bf16[2048,1024]{1,0:T(8,128)(2,1)}, bf16[2048,1024]{1,0:T(8,128)(2,1)}, f32[8,8,256]{2,1,0:T(8,128)}, bf16[2048,1024]{1,0:T(8,128)(2,1)}, bf16[2048,2048]{1,0:T(8,128)(2,1)}) custom-call(bf16[2048,1024]{1,0:T(8,128)(2,1)} %get-tuple-element.30.x_ref.left_ref, bf16[2048,1024]{1,0:T(8,128)(2,1)} %all-gather.2.cloned.1.call-done.u_ref.right_ref, ...), custom_call_target="tpu_custom_call" | custom-call | tf_op jit(solution)/shard_map/experts_both/pallas_call | solution.py:919
  208.6 14.3 %turned_product.2 = (bf16[2,1024,512]{2,1,0:T(8,128)(2,1)}, bf16[2,1024,512]{2,1,0:T(8,128)(2,1)}) custom-call(bf16[2048,1024]{1,0:T(8,128)(2,1)} %get-tuple-element.30.x_ref.left_ref, bf16[2048,2048]{1,0:T(8,128)(2,1)} %get-tuple-element.42.right_ref), custom_call_target="tpu_custom_call" | custom-call | tf_op jit(solution)/shard_map/turned_product/pallas_call | solution.py:947
  223.0 0.7 reduce-scatter.9.cloned.1.call-update
  223.7 8.7 %turned_product.3 = bf16[1,1024,1024]{2,1,0:T(8,128)(2,1)} custom-call(bf16[2048,1024]{1,0:T(8,128)(2,1)} %get-tuple-element.45.left_ref, bf16[2048,1024]{1,0:T(8,128)(2,1)} %all-gather.2.cloned.1.call-done.u_ref.right_ref), custom_call_target="tpu_custom_call" | custom-call | tf_op jit(solution)/shard_map/turned_product/pallas_call | solution.py:947
  232.5 0.5 reduce-scatter.5.cloned.1.call-update
  233.0 0.9 slice_dynamic-update-slice_fusion.refs_1_
  233.9 0.6 copy-done.12
  234.5 41.5 %line_scatter.2 = (f32[256,1024]{1,0:T(8,128)}, f32[16,256]{1,0:T(8,128)}) custom-call(bf16[8,256,1024]{2,1,0:T(8,128)(2,1)} %bitcast.147, f32[8,16,256]{2,1,0:T(8,128)} %copy-done.12), custom_call_target="tpu_custom_call" | custom-call | tf_op jit(solution)/shard_map/line_scatter/pallas_call | solution.py:444
  276.1 0.7 fusion.18
  276.8 1.9 convolution_add_fusion
  278.7 0.3 multiply_reduce_fusion
  279.1 0.7 copy-done.5
  279.8 1.1 fusion.16.x_ref
  280.9 25.3 %square_gather.3 = bf16[2,512,1024]{2,1,0:T(8,128)(2,1)} custom-call(bf16[2,128,1024]{2,1,0:T(8,128)(2,1)} %fusion.16.x_ref), custom_call_target="tpu_custom_call" | custom-call | tf_op jit(solution)/shard_map/square_gather/pallas_call | solution.py:89
  306.2 3.2 convolution_convert_fusion.2.g_ref
  309.4 79.5 %attention_backward.1 = (f32[2,512,256]{2,1,0:T(8,128)}, f32[2,512,256]{2,1,0:T(8,128)}) custom-call(bf16[2,512,256]{2,1,0:T(8,128)(2,1)} %copy.102.q_ref, bf16[2,512,256]{2,1,0:T(8,128)(2,1)} %convolution_convert_fusion.2.g_ref, f32[2,512,256]{2,1,0:T(8,128)} %get-tuple-element.37.o_ref, f32[2,8,2048]{2,1,0:T(8,128)} %get-tuple-element.38.log_ref, ...), custom_call_target="tpu_custom_call" | custom-call | tf_op jit(solution)/shard_map/attention_backward/pallas_call | solution.py:859
  388.9 1.8 slice.118
  390.6 1.9 slice.75
  392.5 2.0 copy.107
  394.6 1.1 subtract_convert_fusion.2
  395.7 0.8 copy.109
  396.6 2.6 copy.106
  399.1 1.4 subtract_convert_fusion
  400.5 0.8 pad_maximum_fusion.3
  401.4 2.0 copy.108
  403.4 4.1 convolution_convert_fusion.p_ref
  407.6 17.1 %square_scatter.3 = f32[2,128,1024]{2,1,0:T(8,128)} custom-call(bf16[2,512,1024]{2,1,0:T(8,128)(2,1)} %convolution_convert_fusion.p_ref), custom_call_target="tpu_custom_call" | custom-call | tf_op jit(solution)/shard_map/square_scatter/pallas_call | solution.py:160
  424.7 1.6 fusion.12
  426.6 0.7 select_maximum_fusion.x_ref
  427.3 22.0 %small_sum.1 = f32[24,1024]{1,0:T(8,128)} custom-call(f32[24,1024]{1,0:T(8,128)} %select_maximum_fusion.x_ref), custom_call_target="tpu_custom_call" | custom-call | tf_op jit(solution)/shard_map/small_sum/pallas_call | solution.py:480
  449.4 0.8 fusion
  450.2 0.8 copy-done.6
  451.2 1.3 bitcast_convert_fusion
  452.5 1.3 pad_maximum_fusion.refs_0_
  453.8 20.8 %line_scatter.3 = f32[128,768]{1,0:T(8,128)} custom-call(bf16[8,128,768]{2,1,0:T(8,128)(2,1)} %pad_maximum_fusion.refs_0_), custom_call_target="tpu_custom_call" | custom-call | tf_op jit(solution)/shard_map/line_scatter/pallas_call | solution.py:444
  474.6 1.6 slice_bitcast_fusion
  476.4 0.8 copy.119
  477.1 1.0 copy.115
  478.1 0.7 copy.116
  478.8 0.6 fusion.34
  479.4 0.6 slice_bitcast_fusion.1
  480.0 1.5 fusion.33
  481.6 2.1 convert_element_type.93
  483.7 2.1 convert_element_type.94
  485.8 2.1 convert_element_type.95
  488.0 2.0 fusion.11
  490.0 1.3 copy.117
  491.3 1.8 copy.118
  (100 shorter events, 3.3 us)
Async XLA Ops:
  7.2 89.1 %copy-start = (bf16[1024,16]{0,1:T(8,128)(2,1)S(1)}, bf16[1024,16]{0,1:T(8,128)(2,1)}, u32[]{:S(2)}) copy-start(bf16[1024,16]{0,1:T(8,128)(2,1)} %param.21) | copy-start | bytes 98308
  7.2 3.3 copy-start.19
  7.2 3.5 copy-start.13
  7.2 167.1 %all-gather.2.cloned.1.call-start = ((), (), s32[]{:S(2)}) async-start(), calls=%async_computation.4 | async-start | bytes 4718592 | tf_op jit(solution)/shard_map/all_gather | solution.py:1022
  9.3 1.7 copy-start.2
  9.3 1.9 copy-start.26
  9.3 472.2 %reduce-scatter.7.cloned.1.call-start = ((), (), s32[]{:S(2)}) async-start(), calls=%async_computation.6 | async-start | bytes 2621440 | tf_op jit(solution)/shard_map/reduce_scatter | solution.py:1102
  10.5 23.8 %copy-start.20 = (bf16[1024,128]{0,1:T(8,128)(2,1)}, bf16[1024,128]{0,1:T(8,128)(2,1)S(1)}, u32[]{:S(2)}) copy-start(bf16[1024,128]{0,1:T(8,128)(2,1)S(1)} %copy.99) | copy-start | bytes 786436
  10.7 23.7 %copy-start.21 = (bf16[1024,128]{0,1:T(8,128)(2,1)}, bf16[1024,128]{0,1:T(8,128)(2,1)S(1)}, u32[]{:S(2)}) copy-start(bf16[1024,128]{0,1:T(8,128)(2,1)S(1)} %copy.98) | copy-start | bytes 786436
  11.0 23.4 %copy-start.15 = (bf16[1024,2,2,64]{0,3,2,1:T(8,128)(2,1)}, bf16[1024,2,2,64]{0,3,2,1:T(8,128)(2,1)S(1)}, u32[]{:S(2)}) copy-start(bf16[1024,2,2,64]{0,3,2,1:T(8,128)(2,1)S(1)} %copy.97) | copy-start | bytes 1572868
  37.3 1.3 copy-start.8
  39.7 354.9 %copy-start.10 = (f32[512,32]{0,1:T(8,128)}, f32[512,32]{0,1:T(8,128)S(1)}, u32[]{:S(2)}) copy-start(f32[512,32]{0,1:T(8,128)S(1)} %get-tuple-element.118) | copy-start | bytes 196612
  39.7 1.5 slice-start
  39.9 1.5 copy-start.14
  41.5 30.7 %copy-start.9 = (bf16[2,2,64,1024]{3,2,1,0:T(8,128)(2,1)}, bf16[2,2,64,1024]{3,2,1,0:T(8,128)(2,1)S(1)}, u32[]{:S(2)}) copy-start(bf16[2,2,64,1024]{3,2,1,0:T(8,128)(2,1)S(1)} %copy.103) | copy-start | bytes 1572868
  72.2 22.4 %copy-start.29 = (s32[128,2,8]{0,2,1:T(8,128)S(1)}, s32[128,2,8]{0,2,1:T(8,128)}, u32[]{:S(2)}) copy-start(s32[128,2,8]{0,2,1:T(8,128)} %param.25) | copy-start | bytes 24580
  94.6 1.5 copy-start.25
  96.3 0.9 copy-start.3
  222.9 260.8 %reduce-scatter.9.cloned.1.call-start = ((), (), s32[]{:S(2)}) async-start(), calls=%async_computation.7 | async-start | bytes 2621440 | tf_op jit(solution)/shard_map/reduce_scatter | solution.py:1102
  223.7 262.2 %reduce-scatter.11.cloned.1.call-start = ((), (), s32[]{:S(2)}) async-start(), calls=%async_computation.8 | async-start | bytes 2621440 | tf_op jit(solution)/shard_map/reduce_scatter | solution.py:1102
  232.4 255.6 %reduce-scatter.5.cloned.1.call-start = ((), (), s32[]{:S(2)}) async-start(), calls=%async_computation.5 | async-start | bytes 4718592 | tf_op jit(solution)/shard_map/reduce_scatter | solution.py:1095
  233.9 0.7 copy-start.12
  278.7 1.0 copy-start.5
  279.8 26.4 %copy-start.27 = (f32[2,128]{1,0:T(2,128)}, f32[2,128]{1,0:T(2,128)S(1)}, u32[]{:S(2)}) copy-start(f32[2,128]{1,0:T(2,128)S(1)} %broadcast_multiply_fusion.1) | copy-start | bytes 3076
  396.6 2.6 copy-start.11
  407.5 18.8 %copy-start.4 = (bf16[2,128,1024]{2,1,0:T(8,128)(2,1)S(1)}, bf16[2,128,1024]{2,1,0:T(8,128)(2,1)}, u32[]{:S(2)}) copy-start(bf16[2,128,1024]{2,1,0:T(8,128)(2,1)} %copy-done.3) | copy-start | bytes 1572868
  407.5 18.8 %copy-start.24 = (f32[16,256]{1,0:T(8,128)S(1)}, f32[16,256]{1,0:T(8,128)}, u32[]{:S(2)}) copy-start(f32[16,256]{1,0:T(8,128)} %get-tuple-element.35) | copy-start | bytes 49156
  407.6 41.8 %copy-start.7 = (bf16[2,512,1024]{2,1,0:T(8,128)(2,1)S(1)}, bf16[2,512,1024]{2,1,0:T(8,128)(2,1)}, u32[]{:S(2)}) copy-start(bf16[2,512,1024]{2,1,0:T(8,128)(2,1)} %square_gather.3) | copy-start | bytes 6291460
  407.6 41.8 %copy-start.17 = (bf16[2,512,256]{2,1,0:T(8,128)(2,1)S(1)}, bf16[2,512,256]{2,1,0:T(8,128)(2,1)}, u32[]{:S(2)}) copy-start(bf16[2,512,256]{2,1,0:T(8,128)(2,1)} %get-tuple-element.29) | copy-start | bytes 1572868
  449.4 1.6 copy-start.6
  449.4 1.7 copy-start.16
  449.4 1.7 copy-start.22
  449.4 1.8 copy-start.23
  453.8 25.0 %copy-start.18 = (f32[24,1024]{1,0:T(8,128)S(1)}, f32[24,1024]{1,0:T(8,128)}, u32[]{:S(2)}) copy-start(f32[24,1024]{1,0:T(8,128)} %small_sum.1) | copy-start | bytes 294916
  481.6 6.4 %copy-start.28 = (f32[2,128]{1,0:T(2,128)S(1)}, f32[2,128]{1,0:T(2,128)}, u32[]{:S(2)}) copy-start(f32[2,128]{1,0:T(2,128)} %copy-done.27) | copy-start | bytes 3076
  488.0 5.1 %copy-start.1 = (bf16[1024,16]{0,1:T(8,128)(2,1)S(1)}, bf16[1024,16]{0,1:T(8,128)(2,1)}, u32[]{:S(2)}) copy-start(bf16[1024,16]{0,1:T(8,128)(2,1)} %param.21) | copy-start | bytes 98308
Sparse Core Ops, SparseCore 0:
  10.2 55.2 all-gather.1
  223.1 32.4 reduce-scatter.6
  258.8 40.9 reduce-scatter.8
  302.6 35.0 reduce-scatter.10
  339.9 68.4 reduce-scatter.4
